TPU v7x, 32 devices: a whole 2x2x4 slice. The times are simulated.
32 devices in a mesh: az: 8 (over z, x), ch: 4 (over y, core).
Axes of the slice: x: 2, y: 2, z: 4, core: 2. Of those that a mesh axis runs over, the one named last changes fastest.
Arguments:
- features: bfloat16 [256, 32, 256], P(None, 'az'), may hold values from -6 to 6
- conv1_weight: bfloat16 [256, 3, 3, 256], P('ch'), may hold values from -0.125 to 0.125
- conv1_bias: float32 [256], P('ch'), may hold values from -3 to 3
- conv2_weight: bfloat16 [256, 3, 3, 256], P('ch'), may hold values from -0.125 to 0.125
- conv2_bias: float32 [256], P('ch'), may hold values from -3 to 3
- request_cell: int32 [32768], P('az'), may hold values from 0 to 1023, as said below
- corner_slot: int32 [4, 4096], P(None, 'az'), may hold values from 0 to 4095, as said below
- corner_frac: float32 [2, 4096], P(None, 'az'), may hold values from 0 to 1
- expand_weight: bfloat16 [256, 512], P('ch'), may hold values from -0.375 to 0.375
- expand_bias: float32 [512], P('ch'), may hold values from -3 to 3
Outputs:
- occupancy: bfloat16 [512, 4096], P('ch', 'az')
Inputs may be any that keep to these rules, and one draw needn't show every extreme that they name: `request_cell`: cell index a * 256 + r within the sector that the slot's block names; entries of slots that no corner_slot entry names are never read. `corner_slot`: within one tile the 2048 entries name distinct slots; at most 512 slots of one sector block are named, exactly 512 for some sector of every tile.
All inputs are finite; a program needn't handle non-finite values.
Results may differ from a plain program's by a relative error of at most 0.014.
Values may be sent and summed in bfloat16 or wider, within the bound.
No kernel may reach another device: no remote copies, remote signals or barrier semaphores. Data moves between devices by JAX's collectives and lax.ppermute only.
A program may use at most 64 MiB of HBM per device.

v0:
```python
import jax
import jax.numpy as jnp
from jax import lax
from jax.sharding import PartitionSpec as P


def padded_2(array, sides, width):
    for axis, dim in sides:
        size, length = (lax.axis_size(axis), array.shape[dim])
        up = [(i, (i + 1) % size) for i in range(size)]
        down = [(j, i) for i, j in up]
        last = lax.slice_in_dim(array, length - width, length, axis=dim)
        first = lax.slice_in_dim(array, 0, width, axis=dim)
        before = lax.ppermute(last, axis, up)
        after = lax.ppermute(first, axis, down)
        array = jnp.concatenate([before, array, after], axis=dim)
    return array


def convolve(padded, weight, columns, ranges):
    inputs = padded.shape[0]
    ranged = jnp.pad(padded, ((0, 0), (0, 0), (1, 1)))
    running = jnp.zeros((weight.shape[0], columns * ranges), jnp.float32)
    for tap_az in range(3):
        for tap_rg in range(3):
            window = ranged[:, tap_az : tap_az + columns, tap_rg : tap_rg + ranges].reshape(
                inputs, columns * ranges
            )
            running = running + jnp.dot(
                weight[:, tap_az, tap_rg, :], window, preferred_element_type=jnp.float32
            )
    return running


def local(
    features,
    conv1_weight,
    conv1_bias,
    conv2_weight,
    conv2_bias,
    request_cell,
    corner_slot,
    corner_frac,
    expand_weight,
    expand_bias,
):
    columns = features.shape[1]
    ranges = features.shape[2]
    outputs = conv1_weight.shape[0]
    widened = padded_2(features, (("az", 1),), 1)
    hidden_one = jax.nn.relu(
        convolve(widened, conv1_weight, columns, ranges) + conv1_bias[:, None]
    ).astype(jnp.bfloat16)
    hidden_one = padded_2(hidden_one.reshape(outputs, columns, ranges), (("az", 1),), 1)
    second_sum = convolve(
        lax.all_gather(hidden_one, "ch", axis=0, tiled=True), conv2_weight, columns, ranges
    )
    hidden_two = jax.nn.relu(second_sum + conv2_bias[:, None]).astype(jnp.bfloat16)
    asked_cells = lax.all_to_all(request_cell, "az", split_axis=0, concat_axis=0, tiled=True)
    picked_cells = jnp.take(hidden_two, asked_cells, axis=1)
    arrived = lax.all_to_all(picked_cells, "az", split_axis=1, concat_axis=1, tiled=True)
    frac_range = corner_frac[0][None, :]
    frac_azim = corner_frac[1][None, :]
    weights = [
        (1.0 - frac_range) * (1.0 - frac_azim),
        frac_range * (1.0 - frac_azim),
        (1.0 - frac_range) * frac_azim,
        frac_range * frac_azim,
    ]
    resampled = jnp.zeros((outputs, corner_slot.shape[1]), jnp.float32)
    for k in range(4):
        resampled = resampled + weights[k] * jnp.take(arrived, corner_slot[k], axis=1).astype(
            jnp.float32
        )
    resampled = resampled.astype(jnp.bfloat16)
    share_rows = expand_weight.shape[1] // lax.axis_size("ch")
    partial_term = lax.dot_general(
        expand_weight, resampled, (((0,), (0,)), ((), ())), preferred_element_type=jnp.float32
    )
    summed = lax.psum(partial_term.astype(jnp.bfloat16), "ch").astype(jnp.float32)
    own_rows = lax.dynamic_slice_in_dim(summed, lax.axis_index("ch") * share_rows, share_rows, 0)
    return (own_rows + expand_bias[:, None]).astype(jnp.bfloat16)


def solution(mesh):
    return jax.shard_map(
        local,
        mesh=mesh,
        in_specs=(
            P(None, "az", None),
            P("ch", None, None, None),
            P("ch"),
            P("ch", None, None, None),
            P("ch"),
            P("az"),
            P(None, "az"),
            P(None, "az"),
            P("ch", None),
            P("ch"),
        ),
        out_specs=P("ch", "az"),
        check_vma=False,
    )
```

profile of v0, /device:TPU:0, one launch (start us, length us, event | category | flops | bytes accessed | tf_op | source)
XLA Modules:
  0.0 134.2 jit_solution(17773252524848126637)
XLA Ops:
  6.5 1.7 %fusion.78 = (bf16[256,1,256]{2,1,0:T(2,128)(2,1)S(1)}, bf16[256,1,256]{2,1,0:T(2,128)(2,1)S(1)}) fusion(bf16[256,4,256]{2,1,0:T(4,128)(2,1)} %param.12), kind=kLoop, calls=%fused_computation.134 | loop fusion | bytes 524288 | tf_op jit(solution)/shard_map/slice | solution.py:12
  8.3 3.0 %collective-permute-start = (bf16[256,1,256]{2,1,0:T(2,128)(2,1)S(1)}, bf16[256,1,256]{2,1,0:T(2,128)(2,1)S(1)}, u32[]{:S(2)}, u32[]{:S(2)}) collective-permute-start(bf16[256,1,256]{2,1,0:T(2,128)(2,1)S(1)} %get-tuple-element.23), channel_id=1, source_target_pairs={{0,4},{4,8},{8,12},{12,16},{16,20},{20,24},{24,28},{28,0},{1,5},{5... | collective-permute-start | bytes 393224 | tf_op jit(solution)/shard_map/ppermute | solution.py:14
  11.3 3.1 %collective-permute-start.1 = (bf16[256,1,256]{2,1,0:T(2,128)(2,1)S(1)}, bf16[256,1,256]{2,1,0:T(2,128)(2,1)S(1)}, u32[]{:S(2)}, u32[]{:S(2)}) collective-permute-start(bf16[256,1,256]{2,1,0:T(2,128)(2,1)S(1)} %get-tuple-element.24), channel_id=1, source_target_pairs={{4,0},{8,4},{12,8},{16,12},{20,16},{24,20},{28,24},{0,28},{5,1},{9... | collective-permute-start | bytes 393224 | tf_op jit(solution)/shard_map/ppermute | solution.py:15
  14.4 3.3 %all-to-all-start = ((s32[8,512,1]{1,2,0:T(1,128)}), s32[8,512,1]{1,2,0:T(1,128)S(1)}, u32[]{:S(2)}, u32[]{:S(2)}) async-start(s32[8,512,1]{1,2,0:T(1,128)} %bitcast.218), calls=%async_computation | async-start | bytes 32768 | tf_op jit(solution)/shard_map/all_to_all | solution.py:59
  17.7 1.1 copy.37
  19.2 5.7 %all-to-all-done = s32[8,512,1]{1,2,0:T(1,128)S(1)} async-done(((s32[8,512,1]{1,2,0:T(1,128)}), s32[8,512,1]{1,2,0:T(1,128)S(1)}, u32[]{:S(2)}, u32[]{:S(2)}) %all-to-all-start) | async-done | bytes 16416 | tf_op jit(solution)/shard_map/all_to_all | solution.py:59
  24.9 2.4 %fusion.5 = bf16[256,6,258]{2,1,0:T(8,128)(2,1)S(1)} fusion(bf16[256,1,256]{2,1,0:T(2,128)(2,1)S(1)} %collective-permute-done.1, bf16[256,4,256]{2,1,0:T(4,128)(2,1)S(1)} %copy-done.1, bf16[256,1,256]{2,1,0:T(2,128)(2,1)S(1)} %collective-permute-done), kind=kLoop, calls=%fused_computation.12 | loop fusion | flops 4755456 | bytes 1579008 | tf_op jit(solution)/shard_map/concatenate | solution.py:16
  27.3 1.8 %fusion.77 = (bf16[256,4,256]{2,1,0:T(4,128)(2,1)S(1)}, bf16[256,4,256]{2,1,0:T(4,128)(2,1)S(1)}, bf16[256,4,256]{2,1,0:T(4,128)(2,1)S(1)}, bf16[256,4,256]{2,1,...) fusion(bf16[256,6,258]{2,1,0:T(8,128)(2,1)S(1)} %fusion.5), kind=kLoop, calls=%fused_computation.133 | loop fusion | bytes 6291456 | tf_op jit(solution)/shard_map/slice | solution.py:26
  29.2 0.2 fusion.56
  29.4 1.2 pad_maximum_fusion
  31.3 0.2 convolution_add_fusion.2
  31.5 0.2 convolution_add_fusion.1
  31.7 0.2 fusion.13
  32.0 0.2 fusion.11
  32.2 0.2 fusion.10
  32.4 0.2 fusion.9
  32.6 0.2 fusion.17
  32.9 0.3 collective-permute-start.2
  33.2 4.4 %collective-permute-start.3 = (bf16[64,1,256]{2,0,1:T(8,128)(2,1)S(1)}, bf16[64,1,256]{2,0,1:T(8,128)(2,1)S(1)}, u32[]{:S(2)}, u32[]{:S(2)}) collective-permute-start(bf16[64,1,256]{2,0,1:T(8,128)(2,1)S(1)} %get-tuple-element.26), channel_id=1, source_target_pairs={{4,0},{8,4},{12,8},{16,12},{20,16},{24,20},{28,24},{0,28},{5,1},{9... | collective-permute-start | bytes 98312 | tf_op jit(solution)/shard_map/ppermute | solution.py:15
  37.7 1.9 %collective-permute-done.2 = bf16[64,1,256]{2,0,1:T(8,128)(2,1)S(1)} collective-permute-done((bf16[64,1,256]{2,0,1:T(8,128)(2,1)S(1)}, bf16[64,1,256]{2,0,1:T(8,128)(2,1)S(1)}, u32[]{:S(2)}, u32[]{:S(2)}) %collective-permute-start.2) | collective-permute-done | bytes 32800 | tf_op jit(solution)/shard_map/ppermute | solution.py:14
  39.6 8.6 %all_gather.3 = bf16[256,6,256]{2,0,1:T(8,128)(2,1)S(1)} all-gather(bf16[64,6,256]{2,0,1:T(8,128)(2,1)S(1)} %pad_maximum_fusion.2), channel_id=1, replica_groups=mesh['az'=8,'ch'=4] {'ch'}, dimensions={0}, use_global_device_ids=true | all-gather | bytes 983040 | tf_op jit(solution)/shard_map/all_gather | solution.py:56
  48.2 0.3 copy.23
  48.5 0.6 pad_slice_fusion
  49.2 0.3 copy-done.2
  49.5 0.3 fusion.45
  49.7 0.3 convolution_add_fusion.10
  50.0 0.3 convolution_add_fusion.9
  50.3 0.3 convolution_add_fusion.8
  50.6 0.3 convolution_add_fusion.7
  50.9 0.3 convolution_add_fusion.6
  51.2 0.3 convolution_add_fusion.5
  51.5 0.3 convolution_add_fusion.4
  51.8 0.3 fusion.19
  52.2 12.1 %gather_fusion = bf16[4096,64]{1,0:T(8,128)(2,1)S(1)} fusion(bf16[64,1024]{0,1:T(8,128)(2,1)S(1)} %copy.27, s32[4096]{0:T(1024)S(1)} %broadcast_clamp_fusion), kind=kCustom, calls=%fused_computation.4 | custom fusion | bytes 1064960 | tf_op jit(solution)/shard_map/jit(_take)/gather | solution.py:60
  64.4 0.3 copy.28
  64.7 0.9 broadcast_select_fusion
  65.6 6.0 %all-to-all-start.1 = ((bf16[64,8,512]{2,0,1:T(8,128)(2,1)}), bf16[64,8,512]{2,0,1:T(8,128)(2,1)S(1)}, u32[]{:S(2)}, u32[]{:S(2)}) async-start(bf16[64,8,512]{2,0,1:T(8,128)(2,1)} %broadcast_select_fusion), calls=%async_computation.1 | async-start | bytes 1048576 | tf_op jit(solution)/shard_map/all_to_all | solution.py:61
  71.6 0.2 all-reduce.4.cloned.1.call-start
  71.9 14.7 %all-to-all-done.1 = bf16[64,8,512]{2,0,1:T(8,128)(2,1)S(1)} async-done(((bf16[64,8,512]{2,0,1:T(8,128)(2,1)}), bf16[64,8,512]{2,0,1:T(8,128)(2,1)S(1)}, u32[]{:S(2)}, u32[]{:S(2)}) %all-to-all-start.1) | async-done | bytes 524320 | tf_op jit(solution)/shard_map/all_to_all | solution.py:61
  86.6 0.5 copy.29
  87.1 1.3 gather_fusion.1
  88.4 1.3 gather_fusion.2
  89.8 1.3 gather_fusion.3
  91.1 1.3 gather_fusion.4
  92.5 1.7 %fusion.6 = bf16[512,512]{0,1:T(8,128)(2,1)} fusion(bf16[64,512]{1,0:T(8,128)(2,1)S(1)} %copy-done, bf16[512,64]{1,0:T(8,128)(2,1)S(1)} %gather_fusion.4, bf16[512,64]{1,0:T(8,128)(2,1)S(1)} %gather_fusion.3, bf16[512,64]{1,0:T(8,128)(2,1)S(1)} %gather_fusion.2, bf16[512,64]{1,0:T(8,128)(2,1)S(1)} %gather_fusion.1, f32[512]{0:T(512)S(1)} %bitcast.220, ...), kind=kOutput, calls=%fused_computation.14 | convolution fusion | flops 34340864 | bytes 862208 | tf_op jit(solution)/shard_map/dot_general | solution.py:77
  94.2 31.5 %all-reduce.4.cloned.1.call-done = bf16[512,512]{0,1:T(8,128)(2,1)} async-done(((bf16[512,512]{0,1:T(8,128)(2,1)}), bf16[512,512]{0,1:T(8,128)(2,1)}) %all-reduce.4.cloned.1.call-update) | async-done | bytes 524304 | tf_op jit(solution)/shard_map/psum | solution.py:80
  125.7 0.9 add_convert_fusion
  126.6 0.8 copy.30
  (49 shorter events, 1.3 us)
Async XLA Ops:
  6.5 86.0 %copy-start = (bf16[64,512]{1,0:T(8,128)(2,1)S(1)}, bf16[64,512]{1,0:T(8,128)(2,1)}, u32[]{:S(2)}) copy-start(bf16[64,512]{1,0:T(8,128)(2,1)} %param.20) | copy-start | bytes 196612
  6.5 18.3 %copy-start.1 = (bf16[256,4,256]{2,1,0:T(4,128)(2,1)S(1)}, bf16[256,4,256]{2,1,0:T(4,128)(2,1)}, u32[]{:S(2)}) copy-start(bf16[256,4,256]{2,1,0:T(4,128)(2,1)} %param.12) | copy-start | bytes 1572868
  6.5 12.3 %copy-start.4 = (s32[4,512]{1,0:T(4,128)S(1)}, s32[4,512]{1,0:T(4,128)}, u32[]{:S(2)}) copy-start(s32[4,512]{1,0:T(4,128)} %param.18) | copy-start | bytes 24580
  6.5 12.4 %copy-start.3 = (bf16[64,3,3,256]{3,0,2,1:T(8,128)(2,1)S(1)}, bf16[64,3,3,256]{3,0,2,1:T(8,128)(2,1)}, u32[]{:S(2)}) copy-start(bf16[64,3,3,256]{3,0,2,1:T(8,128)(2,1)} %param.13) | copy-start | bytes 884740
  8.3 16.6 %collective-permute-start = (bf16[256,1,256]{2,1,0:T(2,128)(2,1)S(1)}, bf16[256,1,256]{2,1,0:T(2,128)(2,1)S(1)}, u32[]{:S(2)}, u32[]{:S(2)}) collective-permute-start(bf16[256,1,256]{2,1,0:T(2,128)(2,1)S(1)} %get-tuple-element.23), channel_id=1, source_target_pairs={{0,4},{4,8},{8,12},{12,16},{16,20},{20,24},{24,28},{28,0},{1,5},{5... | collective-permute-start | bytes 393224 | tf_op jit(solution)/shard_map/ppermute | solution.py:14
  11.3 13.6 %collective-permute-start.1 = (bf16[256,1,256]{2,1,0:T(2,128)(2,1)S(1)}, bf16[256,1,256]{2,1,0:T(2,128)(2,1)S(1)}, u32[]{:S(2)}, u32[]{:S(2)}) collective-permute-start(bf16[256,1,256]{2,1,0:T(2,128)(2,1)S(1)} %get-tuple-element.24), channel_id=1, source_target_pairs={{4,0},{8,4},{12,8},{16,12},{20,16},{24,20},{28,24},{0,28},{5,1},{9... | collective-permute-start | bytes 393224 | tf_op jit(solution)/shard_map/ppermute | solution.py:15
  14.4 10.5 %all-to-all-start = ((s32[8,512,1]{1,2,0:T(1,128)}), s32[8,512,1]{1,2,0:T(1,128)S(1)}, u32[]{:S(2)}, u32[]{:S(2)}) async-start(s32[8,512,1]{1,2,0:T(1,128)} %bitcast.218), calls=%async_computation | async-start | bytes 32768 | tf_op jit(solution)/shard_map/all_to_all | solution.py:59
  32.0 0.7 copy-start.6
  32.9 6.7 %collective-permute-start.2 = (bf16[64,1,256]{2,0,1:T(8,128)(2,1)S(1)}, bf16[64,1,256]{2,0,1:T(8,128)(2,1)S(1)}, u32[]{:S(2)}, u32[]{:S(2)}) collective-permute-start(bf16[64,1,256]{2,0,1:T(8,128)(2,1)S(1)} %get-tuple-element.25), channel_id=1, source_target_pairs={{0,4},{4,8},{8,12},{12,16},{16,20},{20,24},{24,28},{28,0},{1,5},{5... | collective-permute-start | bytes 98312 | tf_op jit(solution)/shard_map/ppermute | solution.py:14
  33.2 6.3 %collective-permute-start.3 = (bf16[64,1,256]{2,0,1:T(8,128)(2,1)S(1)}, bf16[64,1,256]{2,0,1:T(8,128)(2,1)S(1)}, u32[]{:S(2)}, u32[]{:S(2)}) collective-permute-start(bf16[64,1,256]{2,0,1:T(8,128)(2,1)S(1)} %get-tuple-element.26), channel_id=1, source_target_pairs={{4,0},{8,4},{12,8},{16,12},{20,16},{24,20},{28,24},{0,28},{5,1},{9... | collective-permute-start | bytes 98312 | tf_op jit(solution)/shard_map/ppermute | solution.py:15
  48.5 1.0 copy-start.2
  50.9 0.9 copy-start.7
  64.4 7.5 %copy-start.5 = (f32[2,512]{1,0:T(2,128)S(1)}, f32[2,512]{1,0:T(2,128)}, u32[]{:S(2)}) copy-start(f32[2,512]{1,0:T(2,128)} %param.19) | copy-start | bytes 12292
  65.6 21.0 %all-to-all-start.1 = ((bf16[64,8,512]{2,0,1:T(8,128)(2,1)}), bf16[64,8,512]{2,0,1:T(8,128)(2,1)S(1)}, u32[]{:S(2)}, u32[]{:S(2)}) async-start(bf16[64,8,512]{2,0,1:T(8,128)(2,1)} %broadcast_select_fusion), calls=%async_computation.1 | async-start | bytes 1048576 | tf_op jit(solution)/shard_map/all_to_all | solution.py:61
  71.6 54.1 %all-reduce.4.cloned.1.call-start = ((), (), s32[]{:S(2)}) async-start(), calls=%async_computation.2 | async-start | bytes 1048576 | tf_op jit(solution)/shard_map/psum | solution.py:80
  89.8 35.9 %copy-start.8 = (f32[128]{0:T(128)S(1)}, f32[128]{0:T(128)}, u32[]{:S(2)}) copy-start(f32[128]{0:T(128)} %param.21) | copy-start | bytes 1540
Sparse Core Ops, SparseCore 0:
  94.3 31.2 all-reduce.3
where the time goes:
time: 135 us; the launch traced here: 134 us
  waiting for transfers between devices  53.7 us (40%)
  local copies, waits for them, and re-layouts  26 us (19%)
  starting transfers between devices  20.4 us (15%)
  between operations  13.9 us (10%)
  blocking collectives  8.63 us (6%)
  matrix products  6.15 us (5%)
  other arithmetic  5.47 us (4%)
    psum x1, waiting for transfers between devices, local(): lax.psum(partial_term.astype(jnp.bfloat16), 'ch').astype(jnp.float32)  31.5 us
    all_to_all x1, waiting for transfers between devices, local(): lax.all_to_all(picked_cells, 'az', split_axis=1, concat_axis=1, tiled=True)  14.7 us
    gather x2, local copies, waits for them, and re-layouts, local(): picked_cells = jnp.take(hidden_two, asked_cells, axis=1)  12.5 us
    all_gather x1, blocking collectives, local(): lax.all_gather(hidden_one, 'ch', axis=0, tiled=True)  8.63 us
    ppermute x2, starting transfers between devices, padded_2(): after = lax.ppermute(first, axis, down)  7.54 us
    all_to_all x1, starting transfers between devices, local(): lax.all_to_all(picked_cells, 'az', split_axis=1, concat_axis=1, tiled=True)  6 us
    all_to_all x1, waiting for transfers between devices, local(): lax.all_to_all(request_cell, 'az', split_axis=0, concat_axis=0, tiled=True)  5.66 us
    gather x4, local copies, waits for them, and re-layouts, local(): jnp.take(arrived, corner_slot[k], axis=1).astype(jnp.float32)  5.36 us
  transfers between devices with their start and end apart: 7, of which 4 were waited for; matrix products, arithmetic and copies ran while one was open for 1% of the time, Pallas kernels for 0%

commit v1 on v0

v1 whole, which is shorter than its diff:
```python
import functools

import jax
import jax.numpy as jnp
from jax import lax
from jax.experimental import pallas as pl
from jax.experimental.pallas import tpu as pltpu
from jax.sharding import PartitionSpec as P

BF16 = jnp.bfloat16
F32 = jnp.float32
VMEM_LIMIT = 48 * 1024 * 1024
TILES = 8


def call(kernel, outs, *args, scratch=(), flops=0, space=None):
    vmem = pl.BlockSpec(memory_space=pltpu.VMEM)
    specs = [
        pl.BlockSpec(memory_space=pltpu.SMEM) if a.ndim == 1 else vmem for a in args
    ]
    touched = sum(a.size * a.dtype.itemsize for a in args)
    touched += sum(o.size * o.dtype.itemsize for o in outs)
    return pl.pallas_call(
        kernel,
        out_shape=tuple(outs),
        in_specs=specs,
        out_specs=tuple(vmem for _ in outs),
        scratch_shapes=list(scratch),
        compiler_params=pltpu.CompilerParams(vmem_limit_bytes=VMEM_LIMIT),
        cost_estimate=pl.CostEstimate(flops=flops, bytes_accessed=touched, transcendentals=0),
    )(*args)


def shape(dims, dtype):
    return jax.ShapeDtypeStruct(dims, dtype)


def range_sum(z, rows):
    length = z.shape[1]
    lane = lax.broadcasted_iota(jnp.int32, (rows, length), 1)
    before = jnp.where(lane == 0, 0.0, pltpu.roll(z[:rows], 1, 1))
    after = jnp.where(lane == length - 1, 0.0, pltpu.roll(z[2 * rows :], length - 1, 1))
    return z[rows : 2 * rows] + before + after


def stack_weights(dest, pieces, places, inputs):
    rows = dest.shape[0] // 3
    share = pieces[0].shape[2]
    for piece, place in zip(pieces, places):
        for i in range(3):
            for j in range(3):
                dest[pl.ds(j * rows + place, share), i * inputs : (i + 1) * inputs] = piece[i, j]


def prepare_kernel(place, w1a, w1b, w2a, w2b, near, plane):
    core = place[0]
    share = w1a.shape[2]
    places = [pl.multiple_of((core ^ f) * share, share) for f in range(2)]
    stack_weights(near, (w1a, w1b), places, w1a.shape[3])
    stack_weights(plane, (w2a, w2b), places, w2a.shape[3])


def conv_kernel(place, own, halo, near, w2s, w1c, w1d, bias, bias_core, out, xs, far, hs, bs):
    inputs, length = own.shape[0], xs.shape[1]
    core, ch = place[0], place[1]
    columns = own.shape[1] // length
    extra = halo.shape[1] // length
    share = w1c.shape[2]
    total = bs.shape[1]
    for a in range(columns):
        at = pl.multiple_of((a + extra * (1 - core)) * inputs, inputs)
        xs[pl.ds(at, inputs), :] = own[:, a * length : (a + 1) * length]
    for a in range(extra):
        at = pl.multiple_of((a + columns * core) * inputs, inputs)
        xs[pl.ds(at, inputs), :] = halo[:, a * length : (a + 1) * length]
    stack_weights(
        far, (w1c, w1d), [pl.multiple_of((core ^ f) * share, share) for f in range(2)], inputs
    )
    lane = lax.broadcasted_iota(jnp.int32, (share, 2 * share), 1)
    sub = lax.broadcasted_iota(jnp.int32, (share, 2 * share), 0)
    rows = (bias[0:1, :], bias_core[0:1, :], bias[1:2, :], bias_core[1:2, :])
    for f, row in enumerate(rows):
        at = pl.multiple_of((ch ^ f) * share, share)
        for n in range(2):
            column = jnp.sum(jnp.where(lane == sub + n * share, row, 0.0), axis=1, keepdims=True)
            bs[n, pl.ds(at, share), :] = column
    wide = 2 * share
    near_at = pl.multiple_of((ch - core) * share, wide)
    far_at = pl.multiple_of(total - wide - near_at, wide)
    bias2 = bs[1, pl.ds(near_at, wide), :]
    hidden_columns = hs.shape[0] // total
    for weights, at in ((near, near_at), (far, far_at)):
        bias1 = bs[0, pl.ds(at, wide), :]
        for h in range(hidden_columns):
            z = jnp.dot(
                weights[...], xs[h * inputs : (h + 3) * inputs, :], preferred_element_type=F32
            )
            value = jnp.maximum(range_sum(z, wide) + bias1, 0.0)
            hs[pl.ds(pl.multiple_of(h * total + at, wide), wide), :] = value.astype(BF16)
    for g in range(hidden_columns - 2):
        z = jnp.dot(w2s[...], hs[g * total : (g + 3) * total, :], preferred_element_type=F32)
        value = jnp.maximum(range_sum(z, wide) + bias2, 0.0)
        out[:, g * length : (g + 1) * length] = value.astype(BF16)


def table_kernel(asks, slot, frac, table, *, sectors, columns):
    blocks, length = asks.shape
    width = blocks * length // sectors
    lhs = jnp.concatenate(
        [lax.rem(asks[...], length).astype(F32), lax.div(asks[...], length).astype(F32)], axis=0
    ).astype(BF16)
    cells = slot.shape[1]
    high = lax.broadcasted_iota(jnp.int32, (blocks, cells), 0)
    low = lax.broadcasted_iota(jnp.int32, (length, cells), 0)
    for k in range(4):
        q = slot[k : k + 1, :]
        hot = jnp.where(low == lax.rem(q, length), 1.0, 0.0).astype(BF16)
        z = jnp.dot(lhs, hot, preferred_element_type=F32)
        mask = high == lax.div(q, length)
        at = jnp.sum(jnp.where(mask, z[:blocks], 0.0), axis=0, keepdims=True)
        column = jnp.sum(jnp.where(mask, z[blocks:], 0.0), axis=0, keepdims=True)
        sector = lax.div(q, width).astype(F32)
        table[k : k + 1, :] = (sector * columns + column) * length + at
    u, v = frac[0:1, :], frac[1:2, :]
    weights = ((1.0 - u) * (1.0 - v), u * (1.0 - v), (1.0 - u) * v, u * v)
    for k in range(4):
        table[4 + k : 5 + k, :] = weights[k]


def sampling_kernel(place, own, partner, sampling):
    az, core = place[0], place[1]
    blocks, held, both = sampling.shape
    cells = both // 2
    z, x = lax.div(az, 2), lax.rem(az, 2)
    rows = 64
    places, weights = [], []
    for table in (own, partner):
        for k in range(4):
            at = table[k : k + 1, :].astype(jnp.int32)
            sector, cell = lax.div(at, 2 * held), lax.rem(at, 2 * held)
            block = lax.rem(z - lax.div(sector, 2) + blocks, blocks)
            used = (lax.rem(sector, 2) == x) & (lax.div(cell, held) == core)
            places.append(jnp.where(used, block * held + lax.rem(cell, held), -1))
            weights.append(table[4 + k : 5 + k, :])

    def step(n, carry):
        m, r = lax.div(n, held // rows), lax.rem(n, held // rows)
        row = lax.broadcasted_iota(jnp.int32, (rows, cells), 0) + n * rows
        at = pl.ds(pl.multiple_of(r * rows, rows), rows)
        for t in range(2):
            value = jnp.where(places[4 * t] == row, weights[4 * t], 0.0)
            for k in range(4 * t + 1, 4 * t + 4):
                value = value + jnp.where(places[k] == row, weights[k], 0.0)
            sampling[m, at, t * cells : (t + 1) * cells] = value.astype(BF16)
        return carry

    lax.fori_loop(0, blocks * held // rows, step, 0)


def resample_kernel(sampling, *refs):
    held, own, partner = refs[:-2], refs[-2], refs[-1]
    cells = own.shape[1]
    total = jnp.zeros((own.shape[0], 2 * cells), F32)
    for m, block in enumerate(held):
        total = total + jnp.dot(block[...], sampling[m], preferred_element_type=F32)
    own[...] = total[:, :cells].astype(BF16)
    partner[...] = total[:, cells:].astype(BF16)


def expand_kernel(near, far, bias, *refs):
    pieces, out = refs[:-1], refs[-1]
    half = len(pieces) // 2
    z = bias[...]
    for w, group in ((near, pieces[:half]), (far, pieces[half:])):
        for piece in group:
            z = z + lax.dot_general(
                w[...], piece[...], (((0,), (0,)), ((), ())), preferred_element_type=F32
            )
    out[...] = z.astype(BF16)


def sampled_by_request(mine, other, core, request_cell, corner_slot, corner_frac, n_az):
    share = mine.shape[0] // 2
    halves = jnp.where(core == 0, jnp.stack([mine, other]), jnp.stack([other, mine]))
    hidden = lax.dynamic_slice_in_dim(halves, core * share, share, 1)
    hidden = hidden.transpose(1, 0, 2).reshape(share, -1)
    asked = lax.all_to_all(request_cell, "az", split_axis=0, concat_axis=0, tiled=True)
    picked = jnp.take(hidden, asked, axis=1)
    arrived = lax.all_to_all(picked, "az", split_axis=1, concat_axis=1, tiled=True)
    u, v = corner_frac[0][None, :], corner_frac[1][None, :]
    weights = ((1.0 - u) * (1.0 - v), u * (1.0 - v), (1.0 - u) * v, u * v)
    sampled = jnp.zeros((share, corner_slot.shape[1]), F32)
    for k in range(4):
        sampled = sampled + weights[k] * jnp.take(arrived, corner_slot[k], axis=1).astype(F32)
    sampled = sampled.astype(BF16)
    zeros = jnp.zeros_like(sampled)
    placed = jnp.where(core == 0, jnp.stack([sampled, zeros]), jnp.stack([zeros, sampled]))
    return placed.reshape(2 * share, -1)


def local(
    features,
    conv1_weight,
    conv1_bias,
    conv2_weight,
    conv2_bias,
    request_cell,
    corner_slot,
    corner_frac,
    expand_weight,
    expand_bias,
):
    n_az, n_ch = lax.axis_size("az"), lax.axis_size("ch")
    az, ch = lax.axis_index("az"), lax.axis_index("ch")
    core = lax.rem(ch, 2)
    inputs, columns, length = features.shape
    share = conv1_weight.shape[0]
    total = share * n_ch
    cells = corner_slot.shape[1]
    slots = request_cell.shape[0]
    direct = n_az == TILES
    half = columns // 2

    def swap(x, mask):
        return lax.ppermute(x, "ch", [(i, i ^ mask) for i in range(n_ch)])

    def joint(x, target):
        pairs = []
        for a in range(n_az):
            for c in range(n_ch):
                pairs.append((a * n_ch + c, target(a, c % 2) * n_ch + c))
        return lax.ppermute(x, ("az", "ch"), pairs)

    w1 = conv1_weight.transpose(1, 2, 0, 3)
    w2 = conv2_weight.transpose(1, 2, 0, 3)
    w1_y = swap(w1, 2)
    own = lax.optimization_barrier(features.reshape(inputs, columns * length))
    edge = jnp.where(core == 0, own[:, half * length :], own[:, : half * length])
    halo = joint(edge, lambda a, k: (a + 1 - 2 * k) % n_az)
    edge, w1_again, w2_again, conv1_bias, conv2_bias = lax.optimization_barrier(
        (edge, w1, w2, conv1_bias, conv2_bias)
    )

    bias = jnp.concatenate([conv1_bias, conv2_bias]).reshape(1, 2 * share)
    w1_y, bias_y = lax.optimization_barrier((w1_y, swap(bias, 2)))
    bias = jnp.concatenate([bias, bias_y])
    bias, halo = lax.optimization_barrier((bias, halo))
    bias_core = swap(bias, 1)

    w1_far = swap(w1_y, 1)
    w1_core = swap(w1_again, 1)
    w2_core = swap(w2_again, 1)
    w1_near, w2_plane = call(
        prepare_kernel,
        [shape((3 * 2 * share, 3 * inputs), BF16), shape((3 * 2 * share, 3 * total), BF16)],
        core.reshape(1),
        w1,
        w1_core,
        w2,
        w2_core,
    )

    (mine,) = call(
        conv_kernel,
        [shape((2 * share, half * length), BF16)],
        jnp.stack([core, ch]),
        own,
        halo,
        w1_near,
        w2_plane,
        w1_y,
        w1_far,
        bias,
        bias_core,
        scratch=[
            pltpu.VMEM(((columns + half) * inputs, length), BF16),
            pltpu.VMEM((3 * 2 * share, 3 * inputs), BF16),
            pltpu.VMEM((columns * total, length), BF16),
            pltpu.VMEM((2, total, 1), F32),
        ],
        flops=2 * 9 * inputs * total * columns * length,
    )
    outs = expand_weight.shape[1] // n_ch
    expand_weight, mine = lax.optimization_barrier((expand_weight, mine))
    core_rows = swap(expand_weight, 1)
    plane_rows = jnp.where(
        core == 0,
        jnp.stack([expand_weight, core_rows]),
        jnp.stack([core_rows, expand_weight]),
    ).reshape(2 * share, -1)
    weight = lax.dynamic_slice_in_dim(plane_rows, ch * outs, outs, 1)
    weight_y = swap(lax.dynamic_slice_in_dim(plane_rows, (ch ^ 2) * outs, outs, 1), 2)

    if direct:
        turns = TILES // 2
        (table,) = call(
            functools.partial(table_kernel, sectors=n_az, columns=columns),
            [shape((8, cells), F32)],
            request_cell.reshape(-1, length),
            corner_slot,
            corner_frac,
        )
        held = [mine]
        for m in range(1, turns):
            held.append(joint(mine, lambda a, k, m=m: (a + 2 * m) % n_az))
        (sampling,) = call(
            sampling_kernel,
            [shape((turns, half * length, 2 * cells), BF16)],
            jnp.stack([az, core]),
            table,
            joint(table, lambda a, k: a ^ 1),
        )
        held[0], weight, weight_y = lax.optimization_barrier((held[0], weight, weight_y))
        near, partner = call(
            resample_kernel,
            [shape((2 * share, cells), BF16)] * 2,
            sampling,
            *held,
            flops=4 * share * slots * cells,
        )
        nears = [near, joint(partner, lambda a, k: a ^ 1)]
        across = [(a * n_ch + c, (a ^ 1) * n_ch + (c ^ 2)) for a in range(n_az) for c in range(n_ch)]
        fars = [swap(near, 2), lax.ppermute(partner, ("az", "ch"), across)]
    else:
        near = sampled_by_request(
            mine, swap(mine, 1), core, request_cell, corner_slot, corner_frac, n_az
        )
        nears, fars = [near], [swap(near, 2)]
    pieces = nears + [swap(x, 1) for x in nears] + fars + [swap(x, 1) for x in fars]
    (out,) = call(
        expand_kernel,
        [shape((outs, cells), BF16)],
        weight,
        weight_y,
        expand_bias.reshape(outs, 1),
        *pieces,
        flops=4 * outs * total * cells,
    )
    return out


def solution(mesh):
    return jax.shard_map(
        local,
        mesh=mesh,
        in_specs=(
            P(None, "az", None),
            P("ch", None, None, None),
            P("ch"),
            P("ch", None, None, None),
            P("ch"),
            P("az"),
            P(None, "az"),
            P(None, "az"),
            P("ch", None),
            P("ch"),
        ),
        out_specs=P("ch", "az"),
        check_vma=False,
    )
```

time: 135 us -> 46.4 us (0.34)
  the two profiles are of different devices: /device:TPU:0 before, /device:TPU:11 now
where the time goes in v1:
time: 46.4 us; the launch traced here: 46.2 us
  starting transfers between devices  20.3 us (44%)
  waiting for transfers between devices  12.4 us (27%)
  Pallas kernels  9.12 us (20%)
  local copies, waits for them, and re-layouts  3.21 us (7%)
  other arithmetic  0.95 us (2%)
    ppermute x13, starting transfers between devices, swap(): return lax.ppermute(x, 'ch', [(i, i ^ mask) for i in range(n_ch)])  13.1 us
    pallas_call x6, Pallas kernels, call(): pl.pallas_call(kernel, out_shape=tuple(outs), in_specs=specs, out_specs=t...  9.12 us
    ppermute x6, waiting for transfers between devices, joint(): return lax.ppermute(x, ('az', 'ch'), pairs)  6.94 us
    ppermute x6, starting transfers between devices, joint(): return lax.ppermute(x, ('az', 'ch'), pairs)  6.15 us
    ppermute x13, waiting for transfers between devices, swap(): return lax.ppermute(x, 'ch', [(i, i ^ mask) for i in range(n_ch)])  5.42 us
    unnamed x15, local copies, waits for them, and re-layouts  3.07 us
    ppermute x1, starting transfers between devices, local(): fars = [swap(near, 2), lax.ppermute(partner, ('az', 'ch'), across)]  1.06 us
  transfers between devices with their start and end apart: 20, of which 7 were waited for; matrix products, arithmetic and copies ran while one was open for 5% of the time, Pallas kernels for 10%

profile of v1, /device:TPU:11, one launch (start us, length us, event | category | flops | bytes accessed | tf_op | source)
XLA Modules:
  0.0 46.2 jit_solution(3364084524791218521)
XLA Ops:
  0.0 1.3 %collective-permute-start = (bf16[3,3,64,256]{3,2,1,0:T(8,128)(2,1)}, bf16[3,3,64,256]{3,2,1,0:T(8,128)(2,1)S(1)}, u32[]{:S(2)}, u32[]{:S(2)}) collective-permute-start(bf16[3,3,64,256]{3,2,1,0:T(8,128)(2,1)} %bitcast.15), channel_id=1, source_target_pairs={{0,2},{1,3},{2,0},{3,1},{4,6},{5,7},{6,4},{7,5},{8,10},{9,11},{10,... | collective-permute-start | bytes 884744 | tf_op jit(solution)/shard_map/ppermute | solution.py:225
  1.3 1.1 %copy.12 = bf16[32,8,4,256]{3,1,2,0:T(8,128)(2,1)S(1)} copy(bf16[32,8,4,256]{3,2,1,0:T(4,128)(2,1)} %bitcast.20) | data formatting | bytes 1048576
  2.5 0.3 collective-permute-start.2
  2.8 0.7 %maximum_bitcast_fusion = f32[1,128]{1,0:T(1,128)S(1)} fusion(f32[64]{0:T(128)} %param.14, f32[64]{0:T(128)} %param.12), kind=kLoop, calls=%fused_computation.4 | loop fusion | flops 128 | bytes 1024 | tf_op jit(solution)/shard_map/reshape | solution.py:244
  3.6 0.2 collective-permute-start.1
  3.8 2.5 %collective-permute-start.3 = (bf16[3,3,64,256]{3,2,1,0:T(8,128)(2,1)}, bf16[3,3,64,256]{3,2,1,0:T(8,128)(2,1)S(1)}, u32[]{:S(2)}, u32[]{:S(2)}) collective-permute-start(bf16[3,3,64,256]{3,2,1,0:T(8,128)(2,1)} %bitcast.16), channel_id=1, source_target_pairs={{0,1},{1,0},{2,3},{3,2},{4,5},{5,4},{6,7},{7,6},{8,9},{9,8},{10,11... | collective-permute-start | bytes 884744 | tf_op jit(solution)/shard_map/ppermute | solution.py:225
  6.3 0.0 collective-permute-start.4
  6.3 1.9 %collective-permute-done.1 = f32[1,128]{1,0:T(1,128)S(1)} collective-permute-done((f32[1,128]{1,0:T(1,128)S(1)}, f32[1,128]{1,0:T(1,128)S(1)}, u32[]{:S(2)}, u32[]{:S(2)}) %collective-permute-start.1) | collective-permute-done | bytes 544 | tf_op jit(solution)/shard_map/ppermute | solution.py:225
  8.2 0.0 collective-permute-done.w1c
  8.2 1.6 %collective-permute-start.5 = (bf16[3,3,64,256]{3,2,1,0:T(8,128)(2,1)S(1)}, bf16[3,3,64,256]{3,2,1,0:T(8,128)(2,1)S(1)}, u32[]{:S(2)}, u32[]{:S(2)}) collective-permute-start(bf16[3,3,64,256]{3,2,1,0:T(8,128)(2,1)S(1)} %collective-permute-done.w1c), channel_id=1, source_target_pairs={{0,1},{1,0},{2,3},{3,2},{4,5},{5,4},{6,7},{7,6},{8,9},{9,8},{10,11... | collective-permute-start | bytes 884744 | tf_op jit(solution)/shard_map/ppermute | solution.py:225
  9.8 0.0 collective-permute-done.2.halo
  9.8 2.4 %collective-permute-start.6 = (f32[2,128]{1,0:T(2,128)S(1)}, f32[2,128]{1,0:T(2,128)S(1)}, u32[]{:S(2)}, u32[]{:S(2)}) collective-permute-start(f32[2,128]{1,0:T(2,128)S(1)} %pad_maximum_fusion.bias), channel_id=1, source_target_pairs={{0,1},{1,0},{2,3},{3,2},{4,5},{5,4},{6,7},{7,6},{8,9},{9,8},{10,11... | collective-permute-start | bytes 3080 | tf_op jit(solution)/shard_map/ppermute | solution.py:225
  12.2 0.1 pad_add_fusion.place
  12.3 0.0 collective-permute-done.3.w1b
  12.3 0.0 collective-permute-done.4.w2b
  12.3 1.0 %copy-done = bf16[64,3,3,256]{3,0,2,1:T(8,128)(2,1)S(1)} copy-done((bf16[64,3,3,256]{3,0,2,1:T(8,128)(2,1)S(1)}, bf16[64,3,3,256]{3,0,2,1:T(8,128)(2,1)}, u32[]{:S(2)}) %copy-start) | copy-done | bytes 294936
  13.2 1.0 %copy-done.1 = bf16[64,3,3,256]{3,0,2,1:T(8,128)(2,1)S(1)} copy-done((bf16[64,3,3,256]{3,0,2,1:T(8,128)(2,1)S(1)}, bf16[64,3,3,256]{3,0,2,1:T(8,128)(2,1)}, u32[]{:S(2)}) %copy-start.1) | copy-done | bytes 294936
  14.2 0.1 shard_map.100
  14.3 0.0 collective-permute-done.5.w1d
  14.3 2.7 %shard_map.101.refs_0_ = bf16[128,512]{1,0:T(8,128)(2,1)S(1)} custom-call(s32[2]{0:T(128)S(1)} %pad_add_fusion.place, bf16[256,1024]{1,0:T(8,128)(2,1)S(1)} %bitcast.14, bf16[256,512]{1,0:T(8,128)(2,1)S(1)} %collective-permute-done.2.halo, bf16[384,768]{1,0:T(8,128)(2,1)S(1)} %get-tuple-element.28.near, bf16[384,768]{1,0:T(8,128)(2,1)S(1)} %get-tuple-element.29.w2s, ...), custom_call_target="tpu_custom_call" | custom-call | flops 1207959552 | bytes 2689032 | tf_op jit(solution)/shard_map/pallas_call | solution.py:23
  17.0 0.1 collective-permute-start.7
  17.1 0.3 shard_map.102.own
  17.5 0.1 collective-permute-start.9
  17.5 1.3 %collective-permute-start.10 = (bf16[128,512]{1,0:T(8,128)(2,1)S(1)}, bf16[128,512]{1,0:T(8,128)(2,1)S(1)}, u32[]{:S(2)}, u32[]{:S(2)}) collective-permute-start(bf16[128,512]{1,0:T(8,128)(2,1)S(1)} %shard_map.101.refs_0_), channel_id=1, source_target_pairs={{0,8},{1,9},{2,10},{3,11},{4,12},{5,13},{6,14},{7,15},{8,16},{9,17... | collective-permute-start | bytes 393224 | tf_op jit(solution)/shard_map/ppermute | solution.py:232
  18.9 1.6 %collective-permute-start.11 = (bf16[128,512]{1,0:T(8,128)(2,1)S(1)}, bf16[128,512]{1,0:T(8,128)(2,1)S(1)}, u32[]{:S(2)}, u32[]{:S(2)}) collective-permute-start(bf16[128,512]{1,0:T(8,128)(2,1)S(1)} %shard_map.101.refs_0_), channel_id=1, source_target_pairs={{0,16},{1,17},{2,18},{3,19},{4,20},{5,21},{6,22},{7,23},{8,24},{9,... | collective-permute-start | bytes 393224 | tf_op jit(solution)/shard_map/ppermute | solution.py:232
  20.5 1.4 %collective-permute-start.12 = (bf16[128,512]{1,0:T(8,128)(2,1)S(1)}, bf16[128,512]{1,0:T(8,128)(2,1)S(1)}, u32[]{:S(2)}, u32[]{:S(2)}) collective-permute-start(bf16[128,512]{1,0:T(8,128)(2,1)S(1)} %shard_map.101.refs_0_), channel_id=1, source_target_pairs={{0,24},{1,25},{2,26},{3,27},{4,28},{5,29},{6,30},{7,31},{8,0},{9,1... | collective-permute-start | bytes 393224 | tf_op jit(solution)/shard_map/ppermute | solution.py:232
  21.9 0.0 collective-permute-done.7
  21.9 0.3 collective-permute-start.8
  22.2 0.1 pad_add_fusion.1.place
  22.3 4.2 %shard_map.103.sampling = bf16[4,512,1024]{2,1,0:T(8,128)(2,1)S(1)} custom-call(s32[2]{0:T(128)S(1)} %pad_add_fusion.1.place, f32[8,512]{1,0:T(8,128)S(1)} %shard_map.102.own, f32[8,512]{1,0:T(8,128)S(1)} %collective-permute-done.9.partner), custom_call_target="tpu_custom_call" | custom-call | bytes 4227080 | tf_op jit(solution)/shard_map/pallas_call | solution.py:23
  26.5 0.0 collective-permute-done.10.refs_1_
  26.5 3.2 %collective-permute-done.11.refs_2_ = bf16[128,512]{1,0:T(8,128)(2,1)S(1)} collective-permute-done((bf16[128,512]{1,0:T(8,128)(2,1)S(1)}, bf16[128,512]{1,0:T(8,128)(2,1)S(1)}, u32[]{:S(2)}, u32[]{:S(2)}) %collective-permute-start.11) | collective-permute-done | bytes 131104 | tf_op jit(solution)/shard_map/ppermute | solution.py:232
  29.7 3.1 %collective-permute-done.12.refs_3_ = bf16[128,512]{1,0:T(8,128)(2,1)S(1)} collective-permute-done((bf16[128,512]{1,0:T(8,128)(2,1)S(1)}, bf16[128,512]{1,0:T(8,128)(2,1)S(1)}, u32[]{:S(2)}, u32[]{:S(2)}) %collective-permute-start.12) | collective-permute-done | bytes 131104 | tf_op jit(solution)/shard_map/ppermute | solution.py:232
  32.8 0.7 %shard_map.104 = (bf16[128,512]{1,0:T(8,128)(2,1)S(1)}, bf16[128,512]{1,0:T(8,128)(2,1)S(1)}) custom-call(bf16[4,512,1024]{2,1,0:T(8,128)(2,1)S(1)} %shard_map.103.sampling, bf16[128,512]{1,0:T(8,128)(2,1)S(1)} %shard_map.101.refs_0_, bf16[128,512]{1,0:T(8,128)(2,1)S(1)} %collective-permute-done.10.refs_1_, ...), custom_call_target="tpu_custom_call" | custom-call | flops 536870912 | bytes 4980736 | tf_op jit(solution)/shard_map/pallas_call | solution.py:23
  33.5 1.4 %collective-permute-start.13 = (bf16[128,512]{1,0:T(8,128)(2,1)S(1)}, bf16[128,512]{1,0:T(8,128)(2,1)S(1)}, u32[]{:S(2)}, u32[]{:S(2)}) collective-permute-start(bf16[128,512]{1,0:T(8,128)(2,1)S(1)} %get-tuple-element.38), channel_id=1, source_target_pairs={{0,4},{1,5},{2,6},{3,7},{4,0},{5,1},{6,2},{7,3},{8,12},{9,13},{10,... | collective-permute-start | bytes 393224 | tf_op jit(solution)/shard_map/ppermute | solution.py:232
  35.0 0.2 collective-permute-start.16
  35.2 1.1 %collective-permute-start.17 = (bf16[128,512]{1,0:T(8,128)(2,1)S(1)}, bf16[128,512]{1,0:T(8,128)(2,1)S(1)}, u32[]{:S(2)}, u32[]{:S(2)}) collective-permute-start(bf16[128,512]{1,0:T(8,128)(2,1)S(1)} %get-tuple-element.38), channel_id=1, source_target_pairs={{0,6},{1,7},{2,4},{3,5},{4,2},{5,3},{6,0},{7,1},{8,14},{9,15},{10,... | collective-permute-start | bytes 393224 | tf_op jit(solution)/shard_map/ppermute | solution.py:323
  36.3 1.3 %collective-permute-start.14 = (bf16[128,512]{1,0:T(8,128)(2,1)S(1)}, bf16[128,512]{1,0:T(8,128)(2,1)S(1)}, u32[]{:S(2)}, u32[]{:S(2)}) collective-permute-start(bf16[128,512]{1,0:T(8,128)(2,1)S(1)} %get-tuple-element.37.refs_0_), channel_id=1, source_target_pairs={{0,1},{1,0},{2,3},{3,2},{4,5},{5,4},{6,7},{7,6},{8,9},{9,8},{10,11... | collective-permute-start | bytes 393224 | tf_op jit(solution)/shard_map/ppermute | solution.py:225
  37.6 0.6 %collective-permute-done.13.refs_1_ = bf16[128,512]{1,0:T(8,128)(2,1)S(1)} collective-permute-done((bf16[128,512]{1,0:T(8,128)(2,1)S(1)}, bf16[128,512]{1,0:T(8,128)(2,1)S(1)}, u32[]{:S(2)}, u32[]{:S(2)}) %collective-permute-start.13) | collective-permute-done | bytes 131104 | tf_op jit(solution)/shard_map/ppermute | solution.py:232
  38.2 1.5 %collective-permute-start.15 = (bf16[128,512]{1,0:T(8,128)(2,1)S(1)}, bf16[128,512]{1,0:T(8,128)(2,1)S(1)}, u32[]{:S(2)}, u32[]{:S(2)}) collective-permute-start(bf16[128,512]{1,0:T(8,128)(2,1)S(1)} %collective-permute-done.13.refs_1_), channel_id=1, source_target_pairs={{0,1},{1,0},{2,3},{3,2},{4,5},{5,4},{6,7},{7,6},{8,9},{9,8},{10,11... | collective-permute-start | bytes 393224 | tf_op jit(solution)/shard_map/ppermute | solution.py:225
  39.7 2.3 %collective-permute-done.16.refs_4_ = bf16[128,512]{1,0:T(8,128)(2,1)S(1)} collective-permute-done((bf16[128,512]{1,0:T(8,128)(2,1)S(1)}, bf16[128,512]{1,0:T(8,128)(2,1)S(1)}, u32[]{:S(2)}, u32[]{:S(2)}) %collective-permute-start.16) | collective-permute-done | bytes 131104 | tf_op jit(solution)/shard_map/ppermute | solution.py:225
  42.1 1.6 %collective-permute-start.18 = (bf16[128,512]{1,0:T(8,128)(2,1)S(1)}, bf16[128,512]{1,0:T(8,128)(2,1)S(1)}, u32[]{:S(2)}, u32[]{:S(2)}) collective-permute-start(bf16[128,512]{1,0:T(8,128)(2,1)S(1)} %collective-permute-done.16.refs_4_), channel_id=1, source_target_pairs={{0,1},{1,0},{2,3},{3,2},{4,5},{5,4},{6,7},{7,6},{8,9},{9,8},{10,11... | collective-permute-start | bytes 393224 | tf_op jit(solution)/shard_map/ppermute | solution.py:225
  43.7 0.0 collective-permute-done.17.refs_5_
  43.7 0.0 collective-permute-start.19
  43.7 0.1 copy.11.bias
  43.8 0.8 %collective-permute-done.18.refs_6_ = bf16[128,512]{1,0:T(8,128)(2,1)S(1)} collective-permute-done((bf16[128,512]{1,0:T(8,128)(2,1)S(1)}, bf16[128,512]{1,0:T(8,128)(2,1)S(1)}, u32[]{:S(2)}, u32[]{:S(2)}) %collective-permute-start.18) | collective-permute-done | bytes 131104 | tf_op jit(solution)/shard_map/ppermute | solution.py:225
  44.7 0.4 collective-permute-done.19.refs_7_
  45.0 1.1 %shard_map.105 = bf16[128,512]{1,0:T(8,128)(2,1)} custom-call(bf16[128,128]{1,0:T(8,128)(2,1)S(1)} %get-tuple-element.34.near, bf16[128,128]{1,0:T(8,128)(2,1)S(1)} %collective-permute-done.8.far, f32[128,1]{1,0:T(8,128)S(1)} %copy.11.bias, bf16[128,512]{1,0:T(8,128)(2,1)S(1)} %get-tuple-element.37.refs_0_, ...), custom_call_target="tpu_custom_call" | custom-call | flops 67108864 | bytes 1245696 | tf_op jit(solution)/shard_map/pallas_call | solution.py:23
  (22 shorter events, 0.1 us)
Async XLA Ops:
  0.0 17.0 %copy-start.4 = (bf16[64,512]{1,0:T(8,128)(2,1)S(1)}, bf16[64,512]{1,0:T(8,128)(2,1)}, u32[]{:S(2)}) copy-start(bf16[64,512]{1,0:T(8,128)(2,1)} %param.18) | copy-start | bytes 196612
  0.0 17.1 %copy-start.5 = (s32[4096]{0:T(1024)S(1)}, s32[4096]{0:T(1024)}, u32[]{:S(2)}) copy-start(s32[4096]{0:T(1024)} %param.15) | copy-start | bytes 49156
  0.0 17.1 %copy-start.2 = (s32[4,512]{1,0:T(4,128)S(1)}, s32[4,512]{1,0:T(4,128)}, u32[]{:S(2)}) copy-start(s32[4,512]{1,0:T(4,128)} %slot.1) | copy-start | bytes 24580
  0.0 17.1 %copy-start.3 = (f32[2,512]{1,0:T(2,128)S(1)}, f32[2,512]{1,0:T(2,128)}, u32[]{:S(2)}) copy-start(f32[2,512]{1,0:T(2,128)} %frac.1) | copy-start | bytes 12292
  0.0 8.2 %collective-permute-start = (bf16[3,3,64,256]{3,2,1,0:T(8,128)(2,1)}, bf16[3,3,64,256]{3,2,1,0:T(8,128)(2,1)S(1)}, u32[]{:S(2)}, u32[]{:S(2)}) collective-permute-start(bf16[3,3,64,256]{3,2,1,0:T(8,128)(2,1)} %bitcast.15), channel_id=1, source_target_pairs={{0,2},{1,3},{2,0},{3,1},{4,6},{5,7},{6,4},{7,5},{8,10},{9,11},{10,... | collective-permute-start | bytes 884744 | tf_op jit(solution)/shard_map/ppermute | solution.py:225
  2.5 7.3 %collective-permute-start.2 = (bf16[256,512]{1,0:T(8,128)(2,1)S(1)}, bf16[256,512]{1,0:T(8,128)(2,1)S(1)}, u32[]{:S(2)}, u32[]{:S(2)}) collective-permute-start(bf16[256,512]{1,0:T(8,128)(2,1)S(1)} %slice_select_fusion), channel_id=1, source_target_pairs={{0,4},{1,29},{2,6},{3,31},{4,8},{5,1},{6,10},{7,3},{8,12},{9,5},{1... | collective-permute-start | bytes 786440 | tf_op jit(solution)/shard_map/ppermute | solution.py:232
  3.6 4.6 %collective-permute-start.1 = (f32[1,128]{1,0:T(1,128)S(1)}, f32[1,128]{1,0:T(1,128)S(1)}, u32[]{:S(2)}, u32[]{:S(2)}) collective-permute-start(f32[1,128]{1,0:T(1,128)S(1)} %maximum_bitcast_fusion), channel_id=1, source_target_pairs={{0,2},{1,3},{2,0},{3,1},{4,6},{5,7},{6,4},{7,5},{8,10},{9,11},{10,... | collective-permute-start | bytes 1544 | tf_op jit(solution)/shard_map/ppermute | solution.py:225
  3.8 8.5 %collective-permute-start.3 = (bf16[3,3,64,256]{3,2,1,0:T(8,128)(2,1)}, bf16[3,3,64,256]{3,2,1,0:T(8,128)(2,1)S(1)}, u32[]{:S(2)}, u32[]{:S(2)}) collective-permute-start(bf16[3,3,64,256]{3,2,1,0:T(8,128)(2,1)} %bitcast.16), channel_id=1, source_target_pairs={{0,1},{1,0},{2,3},{3,2},{4,5},{5,4},{6,7},{7,6},{8,9},{9,8},{10,11... | collective-permute-start | bytes 884744 | tf_op jit(solution)/shard_map/ppermute | solution.py:225
  6.3 5.9 %collective-permute-start.4 = (bf16[3,3,64,256]{3,2,1,0:T(8,128)(2,1)}, bf16[3,3,64,256]{3,2,1,0:T(8,128)(2,1)S(1)}, u32[]{:S(2)}, u32[]{:S(2)}) collective-permute-start(bf16[3,3,64,256]{3,2,1,0:T(8,128)(2,1)} %bitcast.18), channel_id=1, source_target_pairs={{0,1},{1,0},{2,3},{3,2},{4,5},{5,4},{6,7},{7,6},{8,9},{9,8},{10,11... | collective-permute-start | bytes 884744 | tf_op jit(solution)/shard_map/ppermute | solution.py:225
  8.2 6.1 %collective-permute-start.5 = (bf16[3,3,64,256]{3,2,1,0:T(8,128)(2,1)S(1)}, bf16[3,3,64,256]{3,2,1,0:T(8,128)(2,1)S(1)}, u32[]{:S(2)}, u32[]{:S(2)}) collective-permute-start(bf16[3,3,64,256]{3,2,1,0:T(8,128)(2,1)S(1)} %collective-permute-done.w1c), channel_id=1, source_target_pairs={{0,1},{1,0},{2,3},{3,2},{4,5},{5,4},{6,7},{7,6},{8,9},{9,8},{10,11... | collective-permute-start | bytes 884744 | tf_op jit(solution)/shard_map/ppermute | solution.py:225
  9.8 4.5 %collective-permute-start.6 = (f32[2,128]{1,0:T(2,128)S(1)}, f32[2,128]{1,0:T(2,128)S(1)}, u32[]{:S(2)}, u32[]{:S(2)}) collective-permute-start(f32[2,128]{1,0:T(2,128)S(1)} %pad_maximum_fusion.bias), channel_id=1, source_target_pairs={{0,1},{1,0},{2,3},{3,2},{4,5},{5,4},{6,7},{7,6},{8,9},{9,8},{10,11... | collective-permute-start | bytes 3080 | tf_op jit(solution)/shard_map/ppermute | solution.py:225
  12.3 1.0 %copy-start = (bf16[64,3,3,256]{3,0,2,1:T(8,128)(2,1)S(1)}, bf16[64,3,3,256]{3,0,2,1:T(8,128)(2,1)}, u32[]{:S(2)}) copy-start(bf16[64,3,3,256]{3,0,2,1:T(8,128)(2,1)} %param.11) | copy-start | bytes 884740
  13.2 1.0 %copy-start.1 = (bf16[64,3,3,256]{3,0,2,1:T(8,128)(2,1)S(1)}, bf16[64,3,3,256]{3,0,2,1:T(8,128)(2,1)}, u32[]{:S(2)}) copy-start(bf16[64,3,3,256]{3,0,2,1:T(8,128)(2,1)} %param.13) | copy-start | bytes 884740
  17.0 4.9 %collective-permute-start.7 = (bf16[64,512]{1,0:T(8,128)(2,1)S(1)}, bf16[64,512]{1,0:T(8,128)(2,1)S(1)}, u32[]{:S(2)}, u32[]{:S(2)}) collective-permute-start(bf16[64,512]{1,0:T(8,128)(2,1)S(1)} %copy-done.4), channel_id=1, source_target_pairs={{0,1},{1,0},{2,3},{3,2},{4,5},{5,4},{6,7},{7,6},{8,9},{9,8},{10,11... | collective-permute-start | bytes 196616 | tf_op jit(solution)/shard_map/ppermute | solution.py:225
  17.5 4.9 %collective-permute-start.9 = (f32[8,512]{1,0:T(8,128)S(1)}, f32[8,512]{1,0:T(8,128)S(1)}, u32[]{:S(2)}, u32[]{:S(2)}) collective-permute-start(f32[8,512]{1,0:T(8,128)S(1)} %shard_map.102.own), channel_id=1, source_target_pairs={{0,4},{1,5},{2,6},{3,7},{4,0},{5,1},{6,2},{7,3},{8,12},{9,13},{10,... | collective-permute-start | bytes 49160 | tf_op jit(solution)/shard_map/ppermute | solution.py:232
  17.5 9.0 %collective-permute-start.10 = (bf16[128,512]{1,0:T(8,128)(2,1)S(1)}, bf16[128,512]{1,0:T(8,128)(2,1)S(1)}, u32[]{:S(2)}, u32[]{:S(2)}) collective-permute-start(bf16[128,512]{1,0:T(8,128)(2,1)S(1)} %shard_map.101.refs_0_), channel_id=1, source_target_pairs={{0,8},{1,9},{2,10},{3,11},{4,12},{5,13},{6,14},{7,15},{8,16},{9,17... | collective-permute-start | bytes 393224 | tf_op jit(solution)/shard_map/ppermute | solution.py:232
  18.9 10.8 %collective-permute-start.11 = (bf16[128,512]{1,0:T(8,128)(2,1)S(1)}, bf16[128,512]{1,0:T(8,128)(2,1)S(1)}, u32[]{:S(2)}, u32[]{:S(2)}) collective-permute-start(bf16[128,512]{1,0:T(8,128)(2,1)S(1)} %shard_map.101.refs_0_), channel_id=1, source_target_pairs={{0,16},{1,17},{2,18},{3,19},{4,20},{5,21},{6,22},{7,23},{8,24},{9,... | collective-permute-start | bytes 393224 | tf_op jit(solution)/shard_map/ppermute | solution.py:232
  20.5 12.3 %collective-permute-start.12 = (bf16[128,512]{1,0:T(8,128)(2,1)S(1)}, bf16[128,512]{1,0:T(8,128)(2,1)S(1)}, u32[]{:S(2)}, u32[]{:S(2)}) collective-permute-start(bf16[128,512]{1,0:T(8,128)(2,1)S(1)} %shard_map.101.refs_0_), channel_id=1, source_target_pairs={{0,24},{1,25},{2,26},{3,27},{4,28},{5,29},{6,30},{7,31},{8,0},{9,1... | collective-permute-start | bytes 393224 | tf_op jit(solution)/shard_map/ppermute | solution.py:232
  21.9 4.6 %collective-permute-start.8 = (bf16[128,128]{1,0:T(8,128)(2,1)S(1)}, bf16[128,128]{1,0:T(8,128)(2,1)S(1)}, u32[]{:S(2)}, u32[]{:S(2)}) collective-permute-start(bf16[128,128]{1,0:T(8,128)(2,1)S(1)} %get-tuple-element.39), channel_id=1, source_target_pairs={{0,2},{1,3},{2,0},{3,1},{4,6},{5,7},{6,4},{7,5},{8,10},{9,11},{10,... | collective-permute-start | bytes 98312 | tf_op jit(solution)/shard_map/ppermute | solution.py:225
  22.3 21.4 %copy-start.6 = (f32[128]{0:T(128)S(1)}, f32[128]{0:T(128)}, u32[]{:S(2)}) copy-start(f32[128]{0:T(128)} %param.19) | copy-start | bytes 1540
  33.5 4.7 %collective-permute-start.13 = (bf16[128,512]{1,0:T(8,128)(2,1)S(1)}, bf16[128,512]{1,0:T(8,128)(2,1)S(1)}, u32[]{:S(2)}, u32[]{:S(2)}) collective-permute-start(bf16[128,512]{1,0:T(8,128)(2,1)S(1)} %get-tuple-element.38), channel_id=1, source_target_pairs={{0,4},{1,5},{2,6},{3,7},{4,0},{5,1},{6,2},{7,3},{8,12},{9,13},{10,... | collective-permute-start | bytes 393224 | tf_op jit(solution)/shard_map/ppermute | solution.py:232
  35.0 7.1 %collective-permute-start.16 = (bf16[128,512]{1,0:T(8,128)(2,1)S(1)}, bf16[128,512]{1,0:T(8,128)(2,1)S(1)}, u32[]{:S(2)}, u32[]{:S(2)}) collective-permute-start(bf16[128,512]{1,0:T(8,128)(2,1)S(1)} %get-tuple-element.37.refs_0_), channel_id=1, source_target_pairs={{0,2},{1,3},{2,0},{3,1},{4,6},{5,7},{6,4},{7,5},{8,10},{9,11},{10,... | collective-permute-start | bytes 393224 | tf_op jit(solution)/shard_map/ppermute | solution.py:225
  35.2 8.5 %collective-permute-start.17 = (bf16[128,512]{1,0:T(8,128)(2,1)S(1)}, bf16[128,512]{1,0:T(8,128)(2,1)S(1)}, u32[]{:S(2)}, u32[]{:S(2)}) collective-permute-start(bf16[128,512]{1,0:T(8,128)(2,1)S(1)} %get-tuple-element.38), channel_id=1, source_target_pairs={{0,6},{1,7},{2,4},{3,5},{4,2},{5,3},{6,0},{7,1},{8,14},{9,15},{10,... | collective-permute-start | bytes 393224 | tf_op jit(solution)/shard_map/ppermute | solution.py:323
  36.3 7.6 %collective-permute-start.14 = (bf16[128,512]{1,0:T(8,128)(2,1)S(1)}, bf16[128,512]{1,0:T(8,128)(2,1)S(1)}, u32[]{:S(2)}, u32[]{:S(2)}) collective-permute-start(bf16[128,512]{1,0:T(8,128)(2,1)S(1)} %get-tuple-element.37.refs_0_), channel_id=1, source_target_pairs={{0,1},{1,0},{2,3},{3,2},{4,5},{5,4},{6,7},{7,6},{8,9},{9,8},{10,11... | collective-permute-start | bytes 393224 | tf_op jit(solution)/shard_map/ppermute | solution.py:225
  38.2 5.6 %collective-permute-start.15 = (bf16[128,512]{1,0:T(8,128)(2,1)S(1)}, bf16[128,512]{1,0:T(8,128)(2,1)S(1)}, u32[]{:S(2)}, u32[]{:S(2)}) collective-permute-start(bf16[128,512]{1,0:T(8,128)(2,1)S(1)} %collective-permute-done.13.refs_1_), channel_id=1, source_target_pairs={{0,1},{1,0},{2,3},{3,2},{4,5},{5,4},{6,7},{7,6},{8,9},{9,8},{10,11... | collective-permute-start | bytes 393224 | tf_op jit(solution)/shard_map/ppermute | solution.py:225
  42.1 2.6 %collective-permute-start.18 = (bf16[128,512]{1,0:T(8,128)(2,1)S(1)}, bf16[128,512]{1,0:T(8,128)(2,1)S(1)}, u32[]{:S(2)}, u32[]{:S(2)}) collective-permute-start(bf16[128,512]{1,0:T(8,128)(2,1)S(1)} %collective-permute-done.16.refs_4_), channel_id=1, source_target_pairs={{0,1},{1,0},{2,3},{3,2},{4,5},{5,4},{6,7},{7,6},{8,9},{9,8},{10,11... | collective-permute-start | bytes 393224 | tf_op jit(solution)/shard_map/ppermute | solution.py:225
  43.7 1.3 %collective-permute-start.19 = (bf16[128,512]{1,0:T(8,128)(2,1)S(1)}, bf16[128,512]{1,0:T(8,128)(2,1)S(1)}, u32[]{:S(2)}, u32[]{:S(2)}) collective-permute-start(bf16[128,512]{1,0:T(8,128)(2,1)S(1)} %collective-permute-done.17.refs_5_), channel_id=1, source_target_pairs={{0,1},{1,0},{2,3},{3,2},{4,5},{5,4},{6,7},{7,6},{8,9},{9,8},{10,11... | collective-permute-start | bytes 393224 | tf_op jit(solution)/shard_map/ppermute | solution.py:225

commit v2 on v1

--- a/solution.py
+++ b/solution.py
@@ -9,24 +9,27 @@
 
 BF16 = jnp.bfloat16
 F32 = jnp.float32
-VMEM_LIMIT = 48 * 1024 * 1024
+VMEM_LIMIT = 20 * 1024 * 1024
 TILES = 8
 
 
-def call(kernel, outs, *args, scratch=(), flops=0, space=None):
+def call(kernel, outs, *args, scratch=(), flops=0, left=(), limit=VMEM_LIMIT, touched=None):
     vmem = pl.BlockSpec(memory_space=pltpu.VMEM)
     specs = [
         pl.BlockSpec(memory_space=pltpu.SMEM) if a.ndim == 1 else vmem for a in args
     ]
-    touched = sum(a.size * a.dtype.itemsize for a in args)
-    touched += sum(o.size * o.dtype.itemsize for o in outs)
+    for n in left:
+        specs[n] = pl.BlockSpec(memory_space=pl.ANY)
+    if touched is None:
+        touched = sum(a.size * a.dtype.itemsize for a in args)
+        touched += sum(o.size * o.dtype.itemsize for o in outs)
     return pl.pallas_call(
         kernel,
         out_shape=tuple(outs),
         in_specs=specs,
         out_specs=tuple(vmem for _ in outs),
         scratch_shapes=list(scratch),
-        compiler_params=pltpu.CompilerParams(vmem_limit_bytes=VMEM_LIMIT),
+        compiler_params=pltpu.CompilerParams(vmem_limit_bytes=limit),
         cost_estimate=pl.CostEstimate(flops=flops, bytes_accessed=touched, transcendentals=0),
     )(*args)
 
@@ -52,6 +55,18 @@
                 dest[pl.ds(j * rows + place, share), i * inputs : (i + 1) * inputs] = piece[i, j]
 
 
+def edge_kernel(own, edge):
+    width = edge.shape[1]
+    at = pl.multiple_of((1 - lax.rem(lax.axis_index("ch"), 2)) * width, width)
+    edge[...] = own[:, pl.ds(at, width)]
+
+
+def rows_kernel(wide, rows):
+    channels, length = wide.shape[0], rows.shape[1]
+    for a in range(rows.shape[0] // channels):
+        rows[a * channels : (a + 1) * channels, :] = wide[:, a * length : (a + 1) * length]
+
+
 def prepare_kernel(place, w1a, w1b, w2a, w2b, near, plane):
     core = place[0]
     share = w1a.shape[2]
@@ -64,7 +79,7 @@
     inputs, length = own.shape[0], xs.shape[1]
     core, ch = place[0], place[1]
     columns = own.shape[1] // length
-    extra = halo.shape[1] // length
+    extra = halo.shape[0] // inputs
     share = w1c.shape[2]
     total = bs.shape[1]
     for a in range(columns):
@@ -72,7 +87,7 @@
         xs[pl.ds(at, inputs), :] = own[:, a * length : (a + 1) * length]
     for a in range(extra):
         at = pl.multiple_of((a + columns * core) * inputs, inputs)
-        xs[pl.ds(at, inputs), :] = halo[:, a * length : (a + 1) * length]
+        xs[pl.ds(at, inputs), :] = halo[a * inputs : (a + 1) * inputs, :]
     stack_weights(
         far, (w1c, w1d), [pl.multiple_of((core ^ f) * share, share) for f in range(2)], inputs
     )
@@ -127,56 +142,77 @@
         table[4 + k : 5 + k, :] = weights[k]
 
 
-def sampling_kernel(place, own, partner, sampling):
-    az, core = place[0], place[1]
-    blocks, held, both = sampling.shape
-    cells = both // 2
+def sampling_kernel(table, sampling):
+    az, core = lax.axis_index("az"), lax.rem(lax.axis_index("ch"), 2)
+    blocks, held, cells = sampling.shape
     z, x = lax.div(az, 2), lax.rem(az, 2)
     rows = 64
     places, weights = [], []
-    for table in (own, partner):
-        for k in range(4):
-            at = table[k : k + 1, :].astype(jnp.int32)
-            sector, cell = lax.div(at, 2 * held), lax.rem(at, 2 * held)
-            block = lax.rem(z - lax.div(sector, 2) + blocks, blocks)
-            used = (lax.rem(sector, 2) == x) & (lax.div(cell, held) == core)
-            places.append(jnp.where(used, block * held + lax.rem(cell, held), -1))
-            weights.append(table[4 + k : 5 + k, :])
+    for k in range(4):
+        at = table[k : k + 1, :].astype(jnp.int32)
+        sector, cell = lax.div(at, 2 * held), lax.rem(at, 2 * held)
+        block = lax.rem(z - lax.div(sector, 2) + blocks, blocks)
+        used = (lax.rem(sector, 2) == x) & (lax.div(cell, held) == core)
+        places.append(jnp.where(used, block * held + lax.rem(cell, held), -1))
+        weights.append(table[4 + k : 5 + k, :])
 
     def step(n, carry):
         m, r = lax.div(n, held // rows), lax.rem(n, held // rows)
         row = lax.broadcasted_iota(jnp.int32, (rows, cells), 0) + n * rows
-        at = pl.ds(pl.multiple_of(r * rows, rows), rows)
-        for t in range(2):
-            value = jnp.where(places[4 * t] == row, weights[4 * t], 0.0)
-            for k in range(4 * t + 1, 4 * t + 4):
-                value = value + jnp.where(places[k] == row, weights[k], 0.0)
-            sampling[m, at, t * cells : (t + 1) * cells] = value.astype(BF16)
+        value = jnp.where(places[0] == row, weights[0], 0.0)
+        for k in range(1, 4):
+            value = value + jnp.where(places[k] == row, weights[k], 0.0)
+        sampling[m, pl.ds(pl.multiple_of(r * rows, rows), rows), :] = value.astype(BF16)
         return carry
 
     lax.fori_loop(0, blocks * held // rows, step, 0)
 
 
-def resample_kernel(sampling, *refs):
-    held, own, partner = refs[:-2], refs[-2], refs[-1]
-    cells = own.shape[1]
-    total = jnp.zeros((own.shape[0], 2 * cells), F32)
-    for m, block in enumerate(held):
-        total = total + jnp.dot(block[...], sampling[m], preferred_element_type=F32)
-    own[...] = total[:, :cells].astype(BF16)
-    partner[...] = total[:, cells:].astype(BF16)
-
-
-def expand_kernel(near, far, bias, *refs):
-    pieces, out = refs[:-1], refs[-1]
-    half = len(pieces) // 2
-    z = bias[...]
-    for w, group in ((near, pieces[:half]), (far, pieces[half:])):
-        for piece in group:
-            z = z + lax.dot_general(
-                w[...], piece[...], (((0,), (0,)), ((), ())), preferred_element_type=F32
-            )
-    out[...] = z.astype(BF16)
+def resample_kernel(own, partner, *refs):
+    held, kept, sent = refs[:-2], refs[-2], refs[-1]
+    first = lax.rem(lax.axis_index("ch"), 2) == 0
+    samples = []
+    for sampling in (own, partner):
+        total = jnp.zeros(kept.shape, F32)
+        for m, block in enumerate(held):
+            total = total + jnp.dot(block[...], sampling[m], preferred_element_type=F32)
+        samples.append(total)
+    kept[...] = jnp.where(first, samples[0], samples[1]).astype(BF16)
+    sent[...] = jnp.where(first, samples[1], samples[0]).astype(BF16)
+
+
+def pass_kernel(a, out):
+    out[...] = a[...]
+
+
+def add_kernel(a, b, out):
+    out[...] = (a[...].astype(F32) + b[...].astype(F32)).astype(BF16)
+
+
+def choose_kernel(a, b, out):
+    out[...] = jnp.where(lax.rem(lax.axis_index("ch"), 2) == 0, a[...], b[...])
+
+
+def expand_kernel(wa, wb, wc, wd, bias, *refs):
+    pieces, out = [ref[...].astype(F32) for ref in refs[:-1]], refs[-1]
+    first = lax.rem(lax.axis_index("ch"), 2) == 0
+    near, far = [
+        jnp.where(
+            first,
+            jnp.concatenate([a[...], b[...]], axis=0),
+            jnp.concatenate([b[...], a[...]], axis=0),
+        )
+        for a, b in ((wa, wb), (wc, wd))
+    ]
+    sums = [pieces[0] + pieces[1], pieces[2] + pieces[3]]
+    sums = [value.astype(BF16) for value in sums]
+    z = lax.dot_general(
+        jnp.concatenate([near, far], axis=0),
+        jnp.concatenate(sums, axis=0),
+        (((0,), (0,)), ((), ())),
+        preferred_element_type=F32,
+    )
+    out[...] = (z + bias[...]).astype(BF16)
 
 
 def sampled_by_request(mine, other, core, request_cell, corner_slot, corner_frac, n_az):
@@ -235,16 +271,26 @@
     w2 = conv2_weight.transpose(1, 2, 0, 3)
     w1_y = swap(w1, 2)
     own = lax.optimization_barrier(features.reshape(inputs, columns * length))
-    edge = jnp.where(core == 0, own[:, half * length :], own[:, : half * length])
+    (edge,) = call(edge_kernel, [shape((inputs, half * length), BF16)], own, flops=4 * 10**9)
     halo = joint(edge, lambda a, k: (a + 1 - 2 * k) % n_az)
     edge, w1_again, w2_again, conv1_bias, conv2_bias = lax.optimization_barrier(
         (edge, w1, w2, conv1_bias, conv2_bias)
     )
 
     bias = jnp.concatenate([conv1_bias, conv2_bias]).reshape(1, 2 * share)
-    w1_y, bias_y = lax.optimization_barrier((w1_y, swap(bias, 2)))
+    bias_y = swap(bias, 2)
+    if direct:
+        (table,) = call(
+            functools.partial(table_kernel, sectors=n_az, columns=columns),
+            [shape((8, cells), F32)],
+            request_cell.reshape(-1, length),
+            corner_slot,
+            corner_frac,
+            touched=0,
+        )
+        w1_y, table = lax.optimization_barrier((w1_y, table))
+    w1_y, bias_y = lax.optimization_barrier((w1_y, bias_y))
     bias = jnp.concatenate([bias, bias_y])
-    bias, halo = lax.optimization_barrier((bias, halo))
     bias_core = swap(bias, 1)
 
     w1_far = swap(w1_y, 1)
@@ -260,6 +306,7 @@
         w2_core,
     )
 
+    (halo,) = call(rows_kernel, [shape((half * inputs, length), BF16)], halo, flops=10**10)
     (mine,) = call(
         conv_kernel,
         [shape((2 * share, half * length), BF16)],
@@ -281,57 +328,65 @@
         flops=2 * 9 * inputs * total * columns * length,
     )
     outs = expand_weight.shape[1] // n_ch
-    expand_weight, mine = lax.optimization_barrier((expand_weight, mine))
-    core_rows = swap(expand_weight, 1)
-    plane_rows = jnp.where(
-        core == 0,
-        jnp.stack([expand_weight, core_rows]),
-        jnp.stack([core_rows, expand_weight]),
-    ).reshape(2 * share, -1)
-    weight = lax.dynamic_slice_in_dim(plane_rows, ch * outs, outs, 1)
-    weight_y = swap(lax.dynamic_slice_in_dim(plane_rows, (ch ^ 2) * outs, outs, 1), 2)
+
+    def expansion_slices(expand_weight):
+        slices = []
+        for f in range(n_ch):
+            part = lax.dynamic_slice_in_dim(expand_weight, (ch ^ f) * outs, outs, 1)
+            slices.append(swap(part, f) if f else part)
+            if f == 1:
+                expand_weight, slices[1] = lax.optimization_barrier((expand_weight, slices[1]))
+        return slices
 
     if direct:
         turns = TILES // 2
-        (table,) = call(
-            functools.partial(table_kernel, sectors=n_az, columns=columns),
-            [shape((8, cells), F32)],
-            request_cell.reshape(-1, length),
-            corner_slot,
-            corner_frac,
-        )
+        mine, table = lax.optimization_barrier((mine, table))
+        partner_table = joint(table, lambda a, k: a ^ 1)
         held = [mine]
         for m in range(1, turns):
             held.append(joint(mine, lambda a, k, m=m: (a + 2 * m) % n_az))
-        (sampling,) = call(
-            sampling_kernel,
-            [shape((turns, half * length, 2 * cells), BF16)],
-            jnp.stack([az, core]),
-            table,
-            joint(table, lambda a, k: a ^ 1),
-        )
-        held[0], weight, weight_y = lax.optimization_barrier((held[0], weight, weight_y))
-        near, partner = call(
+        samplings = []
+        for entries in (table, partner_table):
+            (sampling,) = call(
+                sampling_kernel,
+                [shape((turns, half * length, cells), BF16)],
+                entries,
+                touched=0,
+            )
+            samplings.append(sampling)
+        expand_weight, mine = lax.optimization_barrier((expand_weight, mine))
+        slices = expansion_slices(expand_weight)
+        held[0], slices = lax.optimization_barrier((held[0], slices))
+        kept, sent = call(
             resample_kernel,
             [shape((2 * share, cells), BF16)] * 2,
-            sampling,
+            *samplings,
             *held,
             flops=4 * share * slots * cells,
         )
-        nears = [near, joint(partner, lambda a, k: a ^ 1)]
-        across = [(a * n_ch + c, (a ^ 1) * n_ch + (c ^ 2)) for a in range(n_az) for c in range(n_ch)]
-        fars = [swap(near, 2), lax.ppermute(partner, ("az", "ch"), across)]
+        tile = shape((2 * share, cells), BF16)
+        (kept,) = call(add_kernel, [tile], kept, swap(sent, 1))
+        other_plane, same_plane = [], []
+        for a in range(n_az):
+            for c in range(n_ch):
+                other_plane.append((a * n_ch + c, (a ^ (c % 2)) * n_ch + (c ^ 2)))
+                if c % 2:
+                    same_plane.append((a * n_ch + c, (a ^ 1) * n_ch + c))
+        far = lax.ppermute(kept, ("az", "ch"), other_plane)
+        (far,) = call(pass_kernel, [tile], far, flops=6 * 10**9)
+        near = lax.ppermute(kept, ("az", "ch"), same_plane)
+        (near,) = call(choose_kernel, [tile], kept, near)
     else:
         near = sampled_by_request(
             mine, swap(mine, 1), core, request_cell, corner_slot, corner_frac, n_az
         )
-        nears, fars = [near], [swap(near, 2)]
-    pieces = nears + [swap(x, 1) for x in nears] + fars + [swap(x, 1) for x in fars]
+        far = swap(near, 2)
+        slices = expansion_slices(expand_weight)
+    pieces = [near, swap(near, 1), far, swap(far, 1)]
     (out,) = call(
         expand_kernel,
         [shape((outs, cells), BF16)],
-        weight,
-        weight_y,
+        *slices,
         expand_bias.reshape(outs, 1),
         *pieces,
         flops=4 * outs * total * cells,

time: 46.4 us -> 43.1 us (0.929)
  the two profiles are of different devices: /device:TPU:11 before, /device:TPU:0 now
where the time goes in v2:
time: 43.1 us; the launch traced here: 42.2 us
  starting transfers between devices  24.5 us (57%)
  Pallas kernels  8.61 us (20%)
  waiting for transfers between devices  7.39 us (17%)
  local copies, waits for them, and re-layouts  1.33 us (3%)
    ppermute x12, starting transfers between devices, swap(): return lax.ppermute(x, 'ch', [(i, i ^ mask) for i in range(n_ch)])  15.3 us
    pallas_call x12, Pallas kernels, call(): pl.pallas_call(kernel, out_shape=tuple(outs), in_specs=specs, out_specs=t...  8.61 us
    ppermute x5, starting transfers between devices, joint(): return lax.ppermute(x, ('az', 'ch'), pairs)  7.84 us
    ppermute x12, waiting for transfers between devices, swap(): return lax.ppermute(x, 'ch', [(i, i ^ mask) for i in range(n_ch)])  4.49 us
    ppermute x5, waiting for transfers between devices, joint(): return lax.ppermute(x, ('az', 'ch'), pairs)  2.89 us
    unnamed x19, local copies, waits for them, and re-layouts  1.19 us
  transfers between devices with their start and end apart: 19, of which 7 were waited for; matrix products, arithmetic and copies ran while one was open for 3% of the time, Pallas kernels for 10%

profile of v2, /device:TPU:0, one launch (start us, length us, event | category | flops | bytes accessed | tf_op | source)
XLA Modules:
  0.0 42.2 jit_solution(11955271818424591216)
XLA Ops:
  0.0 3.0 %collective-permute-start.3 = (bf16[3,3,64,256]{3,2,1,0:T(8,128)(2,1)}, bf16[3,3,64,256]{3,2,1,0:T(8,128)(2,1)S(1)}, u32[]{:S(2)}, u32[]{:S(2)}) collective-permute-start(bf16[3,3,64,256]{3,2,1,0:T(8,128)(2,1)} %bitcast.11), channel_id=1, source_target_pairs={{0,2},{1,3},{2,0},{3,1},{4,6},{5,7},{6,4},{7,5},{8,10},{9,11},{10,... | collective-permute-start | bytes 884744 | tf_op jit(solution)/shard_map/ppermute | solution.py:261
  3.0 1.1 %copy.12 = bf16[32,8,4,256]{3,1,2,0:T(8,128)(2,1)S(1)} copy(bf16[32,8,4,256]{3,2,1,0:T(4,128)(2,1)} %bitcast.16) | data formatting | bytes 1048576
  4.1 0.0 copy-start
  4.1 0.0 copy-start.1
  4.1 0.0 copy-start.7
  4.1 0.0 copy-start.8
  4.2 0.0 copy-start.5
  4.2 0.0 copy-start.2
  4.2 0.0 copy-start.3
  4.2 1.5 %collective-permute-start = (bf16[256,512]{1,0:T(8,128)(2,1)S(1)}, bf16[256,512]{1,0:T(8,128)(2,1)S(1)}, u32[]{:S(2)}, u32[]{:S(2)}) collective-permute-start(bf16[256,512]{1,0:T(8,128)(2,1)S(1)} %shard_map.100), channel_id=1, source_target_pairs={{0,4},{1,29},{2,6},{3,31},{4,8},{5,1},{6,10},{7,3},{8,12},{9,5},{1... | collective-permute-start | bytes 786440 | tf_op jit(solution)/shard_map/ppermute | solution.py:268
  5.8 2.3 %collective-permute-start.1 = (bf16[3,3,64,256]{3,2,1,0:T(8,128)(2,1)S(1)}, bf16[3,3,64,256]{3,2,1,0:T(8,128)(2,1)S(1)}, u32[]{:S(2)}, u32[]{:S(2)}) collective-permute-start(bf16[3,3,64,256]{3,2,1,0:T(8,128)(2,1)S(1)} %bitcast.12), channel_id=1, source_target_pairs={{0,1},{1,0},{2,3},{3,2},{4,5},{5,4},{6,7},{7,6},{8,9},{9,8},{10,11... | collective-permute-start | bytes 884744 | tf_op jit(solution)/shard_map/ppermute | solution.py:261
  8.1 0.1 collective-permute-start.2
  8.2 0.1 maximum_bitcast_fusion
  8.2 0.5 %collective-permute-start.4 = (f32[1,128]{1,0:T(1,128)S(1)}, f32[1,128]{1,0:T(1,128)S(1)}, u32[]{:S(2)}, u32[]{:S(2)}) collective-permute-start(f32[1,128]{1,0:T(1,128)S(1)} %maximum_bitcast_fusion), channel_id=1, source_target_pairs={{0,2},{1,3},{2,0},{3,1},{4,6},{5,7},{6,4},{7,5},{8,10},{9,11},{10,... | collective-permute-start | bytes 1544 | tf_op jit(solution)/shard_map/ppermute | solution.py:261
  8.8 0.1 pad_add_fusion.place
  8.9 0.3 shard_map.103.table
  9.2 1.0 %collective-permute-done.3.w1c = bf16[3,3,64,256]{3,2,1,0:T(8,128)(2,1)S(1)} collective-permute-done((bf16[3,3,64,256]{3,2,1,0:T(8,128)(2,1)}, bf16[3,3,64,256]{3,2,1,0:T(8,128)(2,1)S(1)}, u32[]{:S(2)}, u32[]{:S(2)}) %collective-permute-start.3) | collective-permute-done | bytes 294944 | tf_op jit(solution)/shard_map/ppermute | solution.py:261
  10.2 1.6 %collective-permute-done.4 = f32[1,128]{1,0:T(1,128)S(1)} collective-permute-done((f32[1,128]{1,0:T(1,128)S(1)}, f32[1,128]{1,0:T(1,128)S(1)}, u32[]{:S(2)}, u32[]{:S(2)}) %collective-permute-start.4) | collective-permute-done | bytes 544 | tf_op jit(solution)/shard_map/ppermute | solution.py:261
  11.8 0.0 collective-permute-start.6
  11.8 0.5 %collective-permute-start.5 = (bf16[3,3,64,256]{3,2,1,0:T(8,128)(2,1)S(1)}, bf16[3,3,64,256]{3,2,1,0:T(8,128)(2,1)S(1)}, u32[]{:S(2)}, u32[]{:S(2)}) collective-permute-start(bf16[3,3,64,256]{3,2,1,0:T(8,128)(2,1)S(1)} %collective-permute-done.3.w1c), channel_id=1, source_target_pairs={{0,1},{1,0},{2,3},{3,2},{4,5},{5,4},{6,7},{7,6},{8,9},{9,8},{10,11... | collective-permute-start | bytes 884744 | tf_op jit(solution)/shard_map/ppermute | solution.py:261
  12.3 1.0 %collective-permute-done.wide = bf16[256,512]{1,0:T(8,128)(2,1)S(1)} collective-permute-done((bf16[256,512]{1,0:T(8,128)(2,1)S(1)}, bf16[256,512]{1,0:T(8,128)(2,1)S(1)}, u32[]{:S(2)}, u32[]{:S(2)}) %collective-permute-start) | collective-permute-done | bytes 262176 | tf_op jit(solution)/shard_map/ppermute | solution.py:268
  13.4 0.0 collective-permute-done.1.w1b
  13.4 0.1 shard_map.102
  13.5 0.0 collective-permute-done.6.bias_core
  13.5 0.0 collective-permute-done.5.w1d
  13.5 2.7 %shard_map.104.refs_0_ = bf16[128,512]{1,0:T(8,128)(2,1)S(1)} custom-call(s32[2]{0:T(128)S(1)} %pad_add_fusion.place, bf16[256,1024]{1,0:T(8,128)(2,1)S(1)} %bitcast.10, bf16[512,256]{1,0:T(8,128)(2,1)S(1)} %shard_map.101.halo, bf16[384,768]{1,0:T(8,128)(2,1)S(1)} %get-tuple-element.29.near, bf16[384,768]{1,0:T(8,128)(2,1)S(1)} %get-tuple-element.30.w2s, ...), custom_call_target="tpu_custom_call" | custom-call | flops 1207959552 | bytes 2689032 | tf_op jit(solution)/shard_map/pallas_call | solution.py:26
  16.3 0.4 %collective-permute-start.7 = (bf16[64,128]{1,0:T(8,128)(2,1)S(1)}, bf16[64,128]{1,0:T(8,128)(2,1)S(1)}, u32[]{:S(2)}, u32[]{:S(2)}) collective-permute-start(bf16[64,128]{1,0:T(8,128)(2,1)S(1)} %get-tuple-element.51), channel_id=1, source_target_pairs={{0,1},{1,0},{2,3},{3,2},{4,5},{5,4},{6,7},{7,6},{8,9},{9,8},{10,11... | collective-permute-start | bytes 49160 | tf_op jit(solution)/shard_map/ppermute | solution.py:261
  16.7 0.3 collective-permute-start.11
  17.0 2.7 %collective-permute-start.12 = (bf16[128,512]{1,0:T(8,128)(2,1)S(1)}, bf16[128,512]{1,0:T(8,128)(2,1)S(1)}, u32[]{:S(2)}, u32[]{:S(2)}) collective-permute-start(bf16[128,512]{1,0:T(8,128)(2,1)S(1)} %shard_map.104.refs_0_), channel_id=1, source_target_pairs={{0,16},{1,17},{2,18},{3,19},{4,20},{5,21},{6,22},{7,23},{8,24},{9,... | collective-permute-start | bytes 393224 | tf_op jit(solution)/shard_map/ppermute | solution.py:268
  19.7 1.3 %collective-permute-start.13 = (bf16[128,512]{1,0:T(8,128)(2,1)S(1)}, bf16[128,512]{1,0:T(8,128)(2,1)S(1)}, u32[]{:S(2)}, u32[]{:S(2)}) collective-permute-start(bf16[128,512]{1,0:T(8,128)(2,1)S(1)} %shard_map.104.refs_0_), channel_id=1, source_target_pairs={{0,24},{1,25},{2,26},{3,27},{4,28},{5,29},{6,30},{7,31},{8,0},{9,1... | collective-permute-start | bytes 393224 | tf_op jit(solution)/shard_map/ppermute | solution.py:268
  20.9 2.1 %collective-permute-start.10 = (f32[8,512]{1,0:T(8,128)S(1)}, f32[8,512]{1,0:T(8,128)S(1)}, u32[]{:S(2)}, u32[]{:S(2)}) collective-permute-start(f32[8,512]{1,0:T(8,128)S(1)} %shard_map.103.table), channel_id=1, source_target_pairs={{0,4},{1,5},{2,6},{3,7},{4,0},{5,1},{6,2},{7,3},{8,12},{9,13},{10,... | collective-permute-start | bytes 49160 | tf_op jit(solution)/shard_map/ppermute | solution.py:268
  23.0 0.0 collective-permute-done.7.wb
  23.0 1.0 %collective-permute-start.8 = (bf16[64,128]{1,0:T(8,128)(2,1)S(1)}, bf16[64,128]{1,0:T(8,128)(2,1)S(1)}, u32[]{:S(2)}, u32[]{:S(2)}) collective-permute-start(bf16[64,128]{1,0:T(8,128)(2,1)S(1)} %get-tuple-element.50), channel_id=1, source_target_pairs={{0,2},{1,3},{2,0},{3,1},{4,6},{5,7},{6,4},{7,5},{8,10},{9,11},{10,... | collective-permute-start | bytes 49160 | tf_op jit(solution)/shard_map/ppermute | solution.py:261
  24.0 0.7 %collective-permute-done.10.table = f32[8,512]{1,0:T(8,128)S(1)} collective-permute-done((f32[8,512]{1,0:T(8,128)S(1)}, f32[8,512]{1,0:T(8,128)S(1)}, u32[]{:S(2)}, u32[]{:S(2)}) %collective-permute-start.10) | collective-permute-done | bytes 16416 | tf_op jit(solution)/shard_map/ppermute | solution.py:268
  24.7 1.9 %shard_map.105.own = bf16[4,512,512]{2,1,0:T(8,128)(2,1)S(1)} custom-call(f32[8,512]{1,0:T(8,128)S(1)} %shard_map.103.table), custom_call_target="tpu_custom_call" | custom-call | tf_op jit(solution)/shard_map/pallas_call | solution.py:26
  26.6 1.9 %shard_map.106.partner = bf16[4,512,512]{2,1,0:T(8,128)(2,1)S(1)} custom-call(f32[8,512]{1,0:T(8,128)S(1)} %collective-permute-done.10.table), custom_call_target="tpu_custom_call" | custom-call | tf_op jit(solution)/shard_map/pallas_call | solution.py:26
  28.6 1.2 %collective-permute-done.12.refs_2_ = bf16[128,512]{1,0:T(8,128)(2,1)S(1)} collective-permute-done((bf16[128,512]{1,0:T(8,128)(2,1)S(1)}, bf16[128,512]{1,0:T(8,128)(2,1)S(1)}, u32[]{:S(2)}, u32[]{:S(2)}) %collective-permute-start.12) | collective-permute-done | bytes 131104 | tf_op jit(solution)/shard_map/ppermute | solution.py:268
  29.7 0.7 %shard_map.107 = (bf16[128,512]{1,0:T(8,128)(2,1)S(1)}, bf16[128,512]{1,0:T(8,128)(2,1)S(1)}) custom-call(bf16[4,512,512]{2,1,0:T(8,128)(2,1)S(1)} %shard_map.105.own, bf16[4,512,512]{2,1,0:T(8,128)(2,1)S(1)} %shard_map.106.partner, bf16[128,512]{1,0:T(8,128)(2,1)S(1)} %shard_map.104.refs_0_, bf16[128,512]{1,0:T(8,128)(2,1)S(1)} %collective-permute-done.11.refs_1_, ...), custom_call_target="tpu_custom_call" | custom-call | flops 536870912 | bytes 4980736 | tf_op jit(solution)/shard_map/pallas_call | solution.py:26
  30.5 0.5 %collective-permute-start.14 = (bf16[128,512]{1,0:T(8,128)(2,1)S(1)}, bf16[128,512]{1,0:T(8,128)(2,1)S(1)}, u32[]{:S(2)}, u32[]{:S(2)}) collective-permute-start(bf16[128,512]{1,0:T(8,128)(2,1)S(1)} %get-tuple-element.48), channel_id=1, source_target_pairs={{0,1},{1,0},{2,3},{3,2},{4,5},{5,4},{6,7},{7,6},{8,9},{9,8},{10,11... | collective-permute-start | bytes 393224 | tf_op jit(solution)/shard_map/ppermute | solution.py:261
  31.0 1.0 %collective-permute-done.14.b = bf16[128,512]{1,0:T(8,128)(2,1)S(1)} collective-permute-done((bf16[128,512]{1,0:T(8,128)(2,1)S(1)}, bf16[128,512]{1,0:T(8,128)(2,1)S(1)}, u32[]{:S(2)}, u32[]{:S(2)}) %collective-permute-start.14) | collective-permute-done | bytes 131104 | tf_op jit(solution)/shard_map/ppermute | solution.py:261
  32.0 0.7 %collective-permute-start.15 = (bf16[128,512]{1,0:T(8,128)(2,1)S(1)}, bf16[128,512]{1,0:T(8,128)(2,1)S(1)}, u32[]{:S(2)}, u32[]{:S(2)}) collective-permute-start(bf16[128,512]{1,0:T(8,128)(2,1)S(1)} %shard_map.108.a), channel_id=1, source_target_pairs={{1,5},{3,7},{5,1},{7,3},{9,13},{11,15},{13,9},{15,11},{17,21},{19,... | collective-permute-start | bytes 393224 | tf_op jit(solution)/shard_map/ppermute | solution.py:377
  32.7 0.6 %collective-permute-start.17 = (bf16[128,512]{1,0:T(8,128)(2,1)S(1)}, bf16[128,512]{1,0:T(8,128)(2,1)S(1)}, u32[]{:S(2)}, u32[]{:S(2)}) collective-permute-start(bf16[128,512]{1,0:T(8,128)(2,1)S(1)} %shard_map.108.a), channel_id=1, source_target_pairs={{0,2},{1,7},{2,0},{3,5},{4,6},{5,3},{6,4},{7,1},{8,10},{9,15},{10,... | collective-permute-start | bytes 393224 | tf_op jit(solution)/shard_map/ppermute | solution.py:375
  33.3 0.0 copy-start.6
  33.3 4.9 %collective-permute-start.16 = (bf16[128,512]{1,0:T(8,128)(2,1)S(1)}, bf16[128,512]{1,0:T(8,128)(2,1)S(1)}, u32[]{:S(2)}, u32[]{:S(2)}) collective-permute-start(bf16[128,512]{1,0:T(8,128)(2,1)S(1)} %shard_map.109.refs_0_), channel_id=1, source_target_pairs={{0,1},{1,0},{2,3},{3,2},{4,5},{5,4},{6,7},{7,6},{8,9},{9,8},{10,11... | collective-permute-start | bytes 393224 | tf_op jit(solution)/shard_map/ppermute | solution.py:261
  38.2 2.2 %collective-permute-start.18 = (bf16[128,512]{1,0:T(8,128)(2,1)S(1)}, bf16[128,512]{1,0:T(8,128)(2,1)S(1)}, u32[]{:S(2)}, u32[]{:S(2)}) collective-permute-start(bf16[128,512]{1,0:T(8,128)(2,1)S(1)} %shard_map.110.refs_2_), channel_id=1, source_target_pairs={{0,1},{1,0},{2,3},{3,2},{4,5},{5,4},{6,7},{7,6},{8,9},{9,8},{10,11... | collective-permute-start | bytes 393224 | tf_op jit(solution)/shard_map/ppermute | solution.py:261
  40.4 0.1 copy.11.bias
  40.5 0.9 %collective-permute-done.18.refs_3_ = bf16[128,512]{1,0:T(8,128)(2,1)S(1)} collective-permute-done((bf16[128,512]{1,0:T(8,128)(2,1)S(1)}, bf16[128,512]{1,0:T(8,128)(2,1)S(1)}, u32[]{:S(2)}, u32[]{:S(2)}) %collective-permute-start.18) | collective-permute-done | bytes 131104 | tf_op jit(solution)/shard_map/ppermute | solution.py:261
  41.3 0.9 %shard_map.111 = bf16[128,512]{1,0:T(8,128)(2,1)} custom-call(bf16[64,128]{1,0:T(8,128)(2,1)S(1)} %get-tuple-element.41.wa, bf16[64,128]{1,0:T(8,128)(2,1)S(1)} %collective-permute-done.7.wb, bf16[64,128]{1,0:T(8,128)(2,1)S(1)} %collective-permute-done.8.wc, bf16[64,128]{1,0:T(8,128)(2,1)S(1)} %collective-permute-done.9.wd, f32[128,1]{1,0:T(8,128)S(1)} %copy.11.bias, ...), custom_call_target="tpu_custom_call" | custom-call | flops 67108864 | bytes 721408 | tf_op jit(solution)/shard_map/pallas_call | solution.py:26
  (28 shorter events, 0.2 us)
Async XLA Ops:
  0.0 10.2 %collective-permute-start.3 = (bf16[3,3,64,256]{3,2,1,0:T(8,128)(2,1)}, bf16[3,3,64,256]{3,2,1,0:T(8,128)(2,1)S(1)}, u32[]{:S(2)}, u32[]{:S(2)}) collective-permute-start(bf16[3,3,64,256]{3,2,1,0:T(8,128)(2,1)} %bitcast.11), channel_id=1, source_target_pairs={{0,2},{1,3},{2,0},{3,1},{4,6},{5,7},{6,4},{7,5},{8,10},{9,11},{10,... | collective-permute-start | bytes 884744 | tf_op jit(solution)/shard_map/ppermute | solution.py:261
  4.1 1.7 %copy-start = (bf16[64,3,3,256]{3,0,2,1:T(8,128)(2,1)S(1)}, bf16[64,3,3,256]{3,0,2,1:T(8,128)(2,1)}, u32[]{:S(2)}) copy-start(bf16[64,3,3,256]{3,0,2,1:T(8,128)(2,1)} %param.11) | copy-start | bytes 884740
  4.1 4.0 %copy-start.1 = (bf16[64,3,3,256]{3,0,2,1:T(8,128)(2,1)S(1)}, bf16[64,3,3,256]{3,0,2,1:T(8,128)(2,1)}, u32[]{:S(2)}) copy-start(bf16[64,3,3,256]{3,0,2,1:T(8,128)(2,1)} %param.13) | copy-start | bytes 884740
  4.1 4.0 %copy-start.7 = (f32[64]{0:T(128)S(1)}, f32[64]{0:T(128)}, u32[]{:S(2)}) copy-start(f32[64]{0:T(128)} %param.14) | copy-start | bytes 772
  4.1 4.0 %copy-start.8 = (f32[64]{0:T(128)S(1)}, f32[64]{0:T(128)}, u32[]{:S(2)}) copy-start(f32[64]{0:T(128)} %param.12) | copy-start | bytes 772
  4.2 4.7 %copy-start.5 = (s32[4096]{0:T(1024)S(1)}, s32[4096]{0:T(1024)}, u32[]{:S(2)}) copy-start(s32[4096]{0:T(1024)} %param.15) | copy-start | bytes 49156
  4.2 4.7 %copy-start.2 = (s32[4,512]{1,0:T(4,128)S(1)}, s32[4,512]{1,0:T(4,128)}, u32[]{:S(2)}) copy-start(s32[4,512]{1,0:T(4,128)} %slot.1) | copy-start | bytes 24580
  4.2 4.7 %copy-start.3 = (f32[2,512]{1,0:T(2,128)S(1)}, f32[2,512]{1,0:T(2,128)}, u32[]{:S(2)}) copy-start(f32[2,512]{1,0:T(2,128)} %frac.1) | copy-start | bytes 12292
  4.2 9.1 %collective-permute-start = (bf16[256,512]{1,0:T(8,128)(2,1)S(1)}, bf16[256,512]{1,0:T(8,128)(2,1)S(1)}, u32[]{:S(2)}, u32[]{:S(2)}) collective-permute-start(bf16[256,512]{1,0:T(8,128)(2,1)S(1)} %shard_map.100), channel_id=1, source_target_pairs={{0,4},{1,29},{2,6},{3,31},{4,8},{5,1},{6,10},{7,3},{8,12},{9,5},{1... | collective-permute-start | bytes 786440 | tf_op jit(solution)/shard_map/ppermute | solution.py:268
  5.8 7.6 %collective-permute-start.1 = (bf16[3,3,64,256]{3,2,1,0:T(8,128)(2,1)S(1)}, bf16[3,3,64,256]{3,2,1,0:T(8,128)(2,1)S(1)}, u32[]{:S(2)}, u32[]{:S(2)}) collective-permute-start(bf16[3,3,64,256]{3,2,1,0:T(8,128)(2,1)S(1)} %bitcast.12), channel_id=1, source_target_pairs={{0,1},{1,0},{2,3},{3,2},{4,5},{5,4},{6,7},{7,6},{8,9},{9,8},{10,11... | collective-permute-start | bytes 884744 | tf_op jit(solution)/shard_map/ppermute | solution.py:261
  8.1 5.3 %collective-permute-start.2 = (bf16[3,3,64,256]{3,2,1,0:T(8,128)(2,1)S(1)}, bf16[3,3,64,256]{3,2,1,0:T(8,128)(2,1)S(1)}, u32[]{:S(2)}, u32[]{:S(2)}) collective-permute-start(bf16[3,3,64,256]{3,2,1,0:T(8,128)(2,1)S(1)} %bitcast.14), channel_id=1, source_target_pairs={{0,1},{1,0},{2,3},{3,2},{4,5},{5,4},{6,7},{7,6},{8,9},{9,8},{10,11... | collective-permute-start | bytes 884744 | tf_op jit(solution)/shard_map/ppermute | solution.py:261
  8.2 3.5 %collective-permute-start.4 = (f32[1,128]{1,0:T(1,128)S(1)}, f32[1,128]{1,0:T(1,128)S(1)}, u32[]{:S(2)}, u32[]{:S(2)}) collective-permute-start(f32[1,128]{1,0:T(1,128)S(1)} %maximum_bitcast_fusion), channel_id=1, source_target_pairs={{0,2},{1,3},{2,0},{3,1},{4,6},{5,7},{6,4},{7,5},{8,10},{9,11},{10,... | collective-permute-start | bytes 1544 | tf_op jit(solution)/shard_map/ppermute | solution.py:261
  11.8 1.7 %collective-permute-start.6 = (f32[2,128]{1,0:T(2,128)S(1)}, f32[2,128]{1,0:T(2,128)S(1)}, u32[]{:S(2)}, u32[]{:S(2)}) collective-permute-start(f32[2,128]{1,0:T(2,128)S(1)} %pad_maximum_fusion.bias), channel_id=1, source_target_pairs={{0,1},{1,0},{2,3},{3,2},{4,5},{5,4},{6,7},{7,6},{8,9},{9,8},{10,11... | collective-permute-start | bytes 3080 | tf_op jit(solution)/shard_map/ppermute | solution.py:261
  11.8 1.7 %collective-permute-start.5 = (bf16[3,3,64,256]{3,2,1,0:T(8,128)(2,1)S(1)}, bf16[3,3,64,256]{3,2,1,0:T(8,128)(2,1)S(1)}, u32[]{:S(2)}, u32[]{:S(2)}) collective-permute-start(bf16[3,3,64,256]{3,2,1,0:T(8,128)(2,1)S(1)} %collective-permute-done.3.w1c), channel_id=1, source_target_pairs={{0,1},{1,0},{2,3},{3,2},{4,5},{5,4},{6,7},{7,6},{8,9},{9,8},{10,11... | collective-permute-start | bytes 884744 | tf_op jit(solution)/shard_map/ppermute | solution.py:261
  13.5 2.7 %copy-start.4 = (bf16[64,512]{1,0:T(8,128)(2,1)S(1)}, bf16[64,512]{1,0:T(8,128)(2,1)}, u32[]{:S(2)}) copy-start(bf16[64,512]{1,0:T(8,128)(2,1)} %param.18) | copy-start | bytes 196612
  16.3 6.7 %collective-permute-start.7 = (bf16[64,128]{1,0:T(8,128)(2,1)S(1)}, bf16[64,128]{1,0:T(8,128)(2,1)S(1)}, u32[]{:S(2)}, u32[]{:S(2)}) collective-permute-start(bf16[64,128]{1,0:T(8,128)(2,1)S(1)} %get-tuple-element.51), channel_id=1, source_target_pairs={{0,1},{1,0},{2,3},{3,2},{4,5},{5,4},{6,7},{7,6},{8,9},{9,8},{10,11... | collective-permute-start | bytes 49160 | tf_op jit(solution)/shard_map/ppermute | solution.py:261
  16.7 11.9 %collective-permute-start.11 = (bf16[128,512]{1,0:T(8,128)(2,1)S(1)}, bf16[128,512]{1,0:T(8,128)(2,1)S(1)}, u32[]{:S(2)}, u32[]{:S(2)}) collective-permute-start(bf16[128,512]{1,0:T(8,128)(2,1)S(1)} %shard_map.104.refs_0_), channel_id=1, source_target_pairs={{0,8},{1,9},{2,10},{3,11},{4,12},{5,13},{6,14},{7,15},{8,16},{9,17... | collective-permute-start | bytes 393224 | tf_op jit(solution)/shard_map/ppermute | solution.py:268
  17.0 12.7 %collective-permute-start.12 = (bf16[128,512]{1,0:T(8,128)(2,1)S(1)}, bf16[128,512]{1,0:T(8,128)(2,1)S(1)}, u32[]{:S(2)}, u32[]{:S(2)}) collective-permute-start(bf16[128,512]{1,0:T(8,128)(2,1)S(1)} %shard_map.104.refs_0_), channel_id=1, source_target_pairs={{0,16},{1,17},{2,18},{3,19},{4,20},{5,21},{6,22},{7,23},{8,24},{9,... | collective-permute-start | bytes 393224 | tf_op jit(solution)/shard_map/ppermute | solution.py:268
  19.7 10.0 %collective-permute-start.13 = (bf16[128,512]{1,0:T(8,128)(2,1)S(1)}, bf16[128,512]{1,0:T(8,128)(2,1)S(1)}, u32[]{:S(2)}, u32[]{:S(2)}) collective-permute-start(bf16[128,512]{1,0:T(8,128)(2,1)S(1)} %shard_map.104.refs_0_), channel_id=1, source_target_pairs={{0,24},{1,25},{2,26},{3,27},{4,28},{5,29},{6,30},{7,31},{8,0},{9,1... | collective-permute-start | bytes 393224 | tf_op jit(solution)/shard_map/ppermute | solution.py:268
  20.9 3.8 %collective-permute-start.10 = (f32[8,512]{1,0:T(8,128)S(1)}, f32[8,512]{1,0:T(8,128)S(1)}, u32[]{:S(2)}, u32[]{:S(2)}) collective-permute-start(f32[8,512]{1,0:T(8,128)S(1)} %shard_map.103.table), channel_id=1, source_target_pairs={{0,4},{1,5},{2,6},{3,7},{4,0},{5,1},{6,2},{7,3},{8,12},{9,13},{10,... | collective-permute-start | bytes 49160 | tf_op jit(solution)/shard_map/ppermute | solution.py:268
  23.0 5.5 %collective-permute-start.8 = (bf16[64,128]{1,0:T(8,128)(2,1)S(1)}, bf16[64,128]{1,0:T(8,128)(2,1)S(1)}, u32[]{:S(2)}, u32[]{:S(2)}) collective-permute-start(bf16[64,128]{1,0:T(8,128)(2,1)S(1)} %get-tuple-element.50), channel_id=1, source_target_pairs={{0,2},{1,3},{2,0},{3,1},{4,6},{5,7},{6,4},{7,5},{8,10},{9,11},{10,... | collective-permute-start | bytes 49160 | tf_op jit(solution)/shard_map/ppermute | solution.py:261
  24.7 3.8 %collective-permute-start.9 = (bf16[64,128]{1,0:T(8,128)(2,1)S(1)}, bf16[64,128]{1,0:T(8,128)(2,1)S(1)}, u32[]{:S(2)}, u32[]{:S(2)}) collective-permute-start(bf16[64,128]{1,0:T(8,128)(2,1)S(1)} %get-tuple-element.49), channel_id=1, source_target_pairs={{0,3},{1,2},{2,1},{3,0},{4,7},{5,6},{6,5},{7,4},{8,11},{9,10},{10,... | collective-permute-start | bytes 49160 | tf_op jit(solution)/shard_map/ppermute | solution.py:261
  30.5 1.5 %collective-permute-start.14 = (bf16[128,512]{1,0:T(8,128)(2,1)S(1)}, bf16[128,512]{1,0:T(8,128)(2,1)S(1)}, u32[]{:S(2)}, u32[]{:S(2)}) collective-permute-start(bf16[128,512]{1,0:T(8,128)(2,1)S(1)} %get-tuple-element.48), channel_id=1, source_target_pairs={{0,1},{1,0},{2,3},{3,2},{4,5},{5,4},{6,7},{7,6},{8,9},{9,8},{10,11... | collective-permute-start | bytes 393224 | tf_op jit(solution)/shard_map/ppermute | solution.py:261
  32.0 1.3 %collective-permute-start.15 = (bf16[128,512]{1,0:T(8,128)(2,1)S(1)}, bf16[128,512]{1,0:T(8,128)(2,1)S(1)}, u32[]{:S(2)}, u32[]{:S(2)}) collective-permute-start(bf16[128,512]{1,0:T(8,128)(2,1)S(1)} %shard_map.108.a), channel_id=1, source_target_pairs={{1,5},{3,7},{5,1},{7,3},{9,13},{11,15},{13,9},{15,11},{17,21},{19,... | collective-permute-start | bytes 393224 | tf_op jit(solution)/shard_map/ppermute | solution.py:377
  32.7 5.5 %collective-permute-start.17 = (bf16[128,512]{1,0:T(8,128)(2,1)S(1)}, bf16[128,512]{1,0:T(8,128)(2,1)S(1)}, u32[]{:S(2)}, u32[]{:S(2)}) collective-permute-start(bf16[128,512]{1,0:T(8,128)(2,1)S(1)} %shard_map.108.a), channel_id=1, source_target_pairs={{0,2},{1,7},{2,0},{3,5},{4,6},{5,3},{6,4},{7,1},{8,10},{9,15},{10,... | collective-permute-start | bytes 393224 | tf_op jit(solution)/shard_map/ppermute | solution.py:375
  33.3 7.0 %copy-start.6 = (f32[128]{0:T(128)S(1)}, f32[128]{0:T(128)}, u32[]{:S(2)}) copy-start(f32[128]{0:T(128)} %param.19) | copy-start | bytes 1540
  33.3 7.2 %collective-permute-start.16 = (bf16[128,512]{1,0:T(8,128)(2,1)S(1)}, bf16[128,512]{1,0:T(8,128)(2,1)S(1)}, u32[]{:S(2)}, u32[]{:S(2)}) collective-permute-start(bf16[128,512]{1,0:T(8,128)(2,1)S(1)} %shard_map.109.refs_0_), channel_id=1, source_target_pairs={{0,1},{1,0},{2,3},{3,2},{4,5},{5,4},{6,7},{7,6},{8,9},{9,8},{10,11... | collective-permute-start | bytes 393224 | tf_op jit(solution)/shard_map/ppermute | solution.py:261
  38.2 3.1 %collective-permute-start.18 = (bf16[128,512]{1,0:T(8,128)(2,1)S(1)}, bf16[128,512]{1,0:T(8,128)(2,1)S(1)}, u32[]{:S(2)}, u32[]{:S(2)}) collective-permute-start(bf16[128,512]{1,0:T(8,128)(2,1)S(1)} %shard_map.110.refs_2_), channel_id=1, source_target_pairs={{0,1},{1,0},{2,3},{3,2},{4,5},{5,4},{6,7},{7,6},{8,9},{9,8},{10,11... | collective-permute-start | bytes 393224 | tf_op jit(solution)/shard_map/ppermute | solution.py:261

commit v3 on v2

--- a/solution.py
+++ b/solution.py
@@ -67,17 +67,25 @@
         rows[a * channels : (a + 1) * channels, :] = wide[:, a * length : (a + 1) * length]
 
 
-def prepare_kernel(place, w1a, w1b, w2a, w2b, near, plane):
-    core = place[0]
-    share = w1a.shape[2]
+def prepare_kernel(own, w1a, w1b, w2a, w2b, near, plane, inner, xs):
+    core = lax.rem(lax.axis_index("ch"), 2)
+    share, inputs, length = w1a.shape[2], w1a.shape[3], xs.shape[1]
     places = [pl.multiple_of((core ^ f) * share, share) for f in range(2)]
-    stack_weights(near, (w1a, w1b), places, w1a.shape[3])
+    stack_weights(near, (w1a, w1b), places, inputs)
     stack_weights(plane, (w2a, w2b), places, w2a.shape[3])
-
-
-def conv_kernel(place, own, halo, near, w2s, w1c, w1d, bias, bias_core, out, xs, far, hs, bs):
+    for a in range(own.shape[1] // length):
+        xs[a * inputs : (a + 1) * inputs, :] = own[:, a * length : (a + 1) * length]
+    for n in range(inner.shape[0]):
+        z = jnp.dot(near[...], xs[n * inputs : (n + 3) * inputs, :], preferred_element_type=F32)
+        inner[n] = range_sum(z, 2 * share)
+
+
+def conv_kernel(
+    own, halo, near, w2s, inner, w1c, w1d, bias, bias_core, out, xs, far, hs, bs
+):
     inputs, length = own.shape[0], xs.shape[1]
-    core, ch = place[0], place[1]
+    ch = lax.axis_index("ch")
+    core = lax.rem(ch, 2)
     columns = own.shape[1] // length
     extra = halo.shape[0] // inputs
     share = w1c.shape[2]
@@ -104,14 +112,22 @@
     far_at = pl.multiple_of(total - wide - near_at, wide)
     bias2 = bs[1, pl.ds(near_at, wide), :]
     hidden_columns = hs.shape[0] // total
-    for weights, at in ((near, near_at), (far, far_at)):
-        bias1 = bs[0, pl.ds(at, wide), :]
-        for h in range(hidden_columns):
-            z = jnp.dot(
-                weights[...], xs[h * inputs : (h + 3) * inputs, :], preferred_element_type=F32
-            )
-            value = jnp.maximum(range_sum(z, wide) + bias1, 0.0)
-            hs[pl.ds(pl.multiple_of(h * total + at, wide), wide), :] = value.astype(BF16)
+
+    def keep(h, at, value):
+        value = jnp.maximum(value + bs[0, pl.ds(at, wide), :], 0.0)
+        hs[pl.ds(pl.multiple_of(h * total + at, wide), wide), :] = value.astype(BF16)
+
+    inners = inner.shape[0]
+    for n in range(hidden_columns - inners):
+        h = n + inners * core
+        rows = pl.ds(pl.multiple_of(h * inputs, inputs), 3 * inputs)
+        z = jnp.dot(near[...], xs[rows, :], preferred_element_type=F32)
+        keep(h, near_at, range_sum(z, wide))
+    for n in range(inners):
+        keep(n + inners * (1 - core), near_at, inner[n])
+    for h in range(hidden_columns):
+        z = jnp.dot(far[...], xs[h * inputs : (h + 3) * inputs, :], preferred_element_type=F32)
+        keep(h, far_at, range_sum(z, wide))
     for g in range(hidden_columns - 2):
         z = jnp.dot(w2s[...], hs[g * total : (g + 3) * total, :], preferred_element_type=F32)
         value = jnp.maximum(range_sum(z, wide) + bias2, 0.0)
@@ -296,25 +312,29 @@
     w1_far = swap(w1_y, 1)
     w1_core = swap(w1_again, 1)
     w2_core = swap(w2_again, 1)
-    w1_near, w2_plane = call(
+    w1_near, w2_plane, inner = call(
         prepare_kernel,
-        [shape((3 * 2 * share, 3 * inputs), BF16), shape((3 * 2 * share, 3 * total), BF16)],
-        core.reshape(1),
+        [
+            shape((3 * 2 * share, 3 * inputs), BF16),
+            shape((3 * 2 * share, 3 * total), BF16),
+            shape((columns - 2, 2 * share, length), F32),
+        ],
+        own,
         w1,
         w1_core,
         w2,
         w2_core,
-    )
-
+        scratch=[pltpu.VMEM((columns * inputs, length), BF16)],
+    )
     (halo,) = call(rows_kernel, [shape((half * inputs, length), BF16)], halo, flops=10**10)
     (mine,) = call(
         conv_kernel,
         [shape((2 * share, half * length), BF16)],
-        jnp.stack([core, ch]),
         own,
         halo,
         w1_near,
         w2_plane,
+        inner,
         w1_y,
         w1_far,
         bias,
@@ -373,8 +393,8 @@
                 if c % 2:
                     same_plane.append((a * n_ch + c, (a ^ 1) * n_ch + c))
         far = lax.ppermute(kept, ("az", "ch"), other_plane)
-        (far,) = call(pass_kernel, [tile], far, flops=6 * 10**9)
         near = lax.ppermute(kept, ("az", "ch"), same_plane)
+        far, near = lax.optimization_barrier((far, near))
         (near,) = call(choose_kernel, [tile], kept, near)
     else:
         near = sampled_by_request(

time: 43.1 us -> 42 us (0.974); the launches traced: 42.2 us -> 41.9 us
  waiting for transfers between devices: 7.39 us -> 13.3 us
  starting transfers between devices: 24.5 us -> 18.6 us
    ppermute x12, starting transfers between devices: 15.3 us -> 8.86 us  [swap(): return lax.ppermute(x, 'ch', [(i, i ^ mask) for i in range(n_ch)])]
    ppermute x1, waiting for transfers between devices: 0.01 us -> 4.91 us  [local(): far = lax.ppermute(kept, ('az', 'ch'), other_plane)]
    ppermute x5, waiting for transfers between devices: 2.89 us -> 4.56 us  [joint(): return lax.ppermute(x, ('az', 'ch'), pairs)]
    ppermute x12, waiting for transfers between devices: 4.49 us -> 3.86 us  [swap(): return lax.ppermute(x, 'ch', [(i, i ^ mask) for i in range(n_ch)])]
    pallas_call x12 -> x11, Pallas kernels: 8.61 us -> 8.3 us  [call(): pl.pallas_call(kernel, out_shape=tuple(outs), in_specs=specs, out_specs=t...]
  transfers between devices with their start and end apart: 19 -> 19, of which waited for: 7 -> 9; matrix products, arithmetic and copies ran while one was open for 3% -> 3% of each run, Pallas kernels for 10% -> 11%
where the time goes in v3:
time: 42 us; the launch traced here: 41.9 us
  starting transfers between devices  18.6 us (44%)
  waiting for transfers between devices  13.3 us (32%)
  Pallas kernels  8.3 us (20%)
  local copies, waits for them, and re-layouts  1.33 us (3%)
    ppermute x12, starting transfers between devices, swap(): return lax.ppermute(x, 'ch', [(i, i ^ mask) for i in range(n_ch)])  8.86 us
    pallas_call x11, Pallas kernels, call(): pl.pallas_call(kernel, out_shape=tuple(outs), in_specs=specs, out_specs=t...  8.3 us
    ppermute x5, starting transfers between devices, joint(): return lax.ppermute(x, ('az', 'ch'), pairs)  8.2 us
    ppermute x1, waiting for transfers between devices, local(): far = lax.ppermute(kept, ('az', 'ch'), other_plane)  4.91 us
    ppermute x5, waiting for transfers between devices, joint(): return lax.ppermute(x, ('az', 'ch'), pairs)  4.56 us
    ppermute x12, waiting for transfers between devices, swap(): return lax.ppermute(x, 'ch', [(i, i ^ mask) for i in range(n_ch)])  3.86 us
    unnamed x19, local copies, waits for them, and re-layouts  1.19 us
    ppermute x1, starting transfers between devices, local(): far = lax.ppermute(kept, ('az', 'ch'), other_plane)  0.86 us
  transfers between devices with their start and end apart: 19, of which 9 were waited for; matrix products, arithmetic and copies ran while one was open for 3% of the time, Pallas kernels for 11%

profile of v3, /device:TPU:0, one launch (start us, length us, event | category | flops | bytes accessed | tf_op | source)
XLA Modules:
  0.0 41.9 jit_solution(6230474615634798869)
XLA Ops:
  0.0 3.0 %collective-permute-start.3 = (bf16[3,3,64,256]{3,2,1,0:T(8,128)(2,1)}, bf16[3,3,64,256]{3,2,1,0:T(8,128)(2,1)S(1)}, u32[]{:S(2)}, u32[]{:S(2)}) collective-permute-start(bf16[3,3,64,256]{3,2,1,0:T(8,128)(2,1)} %bitcast.10), channel_id=1, source_target_pairs={{0,2},{1,3},{2,0},{3,1},{4,6},{5,7},{6,4},{7,5},{8,10},{9,11},{10,... | collective-permute-start | bytes 884744 | tf_op jit(solution)/shard_map/ppermute | solution.py:277
  3.0 1.1 %copy.12 = bf16[32,8,4,256]{3,1,2,0:T(8,128)(2,1)S(1)} copy(bf16[32,8,4,256]{3,2,1,0:T(4,128)(2,1)} %bitcast.15) | data formatting | bytes 1048576
  4.1 0.0 copy-start.7
  4.1 0.0 copy-start.8
  4.1 0.0 copy-start
  4.1 0.0 copy-start.1
  4.2 0.0 copy-start.5
  4.2 0.0 copy-start.2
  4.2 0.0 copy-start.3
  4.2 1.5 %collective-permute-start = (bf16[256,512]{1,0:T(8,128)(2,1)S(1)}, bf16[256,512]{1,0:T(8,128)(2,1)S(1)}, u32[]{:S(2)}, u32[]{:S(2)}) collective-permute-start(bf16[256,512]{1,0:T(8,128)(2,1)S(1)} %shard_map.100), channel_id=1, source_target_pairs={{0,4},{1,29},{2,6},{3,31},{4,8},{5,1},{6,10},{7,3},{8,12},{9,5},{1... | collective-permute-start | bytes 786440 | tf_op jit(solution)/shard_map/ppermute | solution.py:284
  5.8 0.1 maximum_bitcast_fusion
  5.9 0.5 %collective-permute-start.4 = (f32[1,128]{1,0:T(1,128)S(1)}, f32[1,128]{1,0:T(1,128)S(1)}, u32[]{:S(2)}, u32[]{:S(2)}) collective-permute-start(f32[1,128]{1,0:T(1,128)S(1)} %maximum_bitcast_fusion), channel_id=1, source_target_pairs={{0,2},{1,3},{2,0},{3,1},{4,6},{5,7},{6,4},{7,5},{8,10},{9,11},{10,... | collective-permute-start | bytes 1544 | tf_op jit(solution)/shard_map/ppermute | solution.py:277
  6.4 2.0 %collective-permute-start.1 = (bf16[3,3,64,256]{3,2,1,0:T(8,128)(2,1)S(1)}, bf16[3,3,64,256]{3,2,1,0:T(8,128)(2,1)S(1)}, u32[]{:S(2)}, u32[]{:S(2)}) collective-permute-start(bf16[3,3,64,256]{3,2,1,0:T(8,128)(2,1)S(1)} %bitcast.11), channel_id=1, source_target_pairs={{0,1},{1,0},{2,3},{3,2},{4,5},{5,4},{6,7},{7,6},{8,9},{9,8},{10,11... | collective-permute-start | bytes 884744 | tf_op jit(solution)/shard_map/ppermute | solution.py:277
  8.4 0.1 collective-permute-start.2
  8.5 0.3 shard_map.103.table
  8.8 1.4 %collective-permute-done.3.w1c = bf16[3,3,64,256]{3,2,1,0:T(8,128)(2,1)S(1)} collective-permute-done((bf16[3,3,64,256]{3,2,1,0:T(8,128)(2,1)}, bf16[3,3,64,256]{3,2,1,0:T(8,128)(2,1)S(1)}, u32[]{:S(2)}, u32[]{:S(2)}) %collective-permute-start.3) | collective-permute-done | bytes 294944 | tf_op jit(solution)/shard_map/ppermute | solution.py:277
  10.2 0.1 collective-permute-done.4
  10.3 0.6 %collective-permute-start.6 = (f32[2,128]{1,0:T(2,128)S(1)}, f32[2,128]{1,0:T(2,128)S(1)}, u32[]{:S(2)}, u32[]{:S(2)}) collective-permute-start(f32[2,128]{1,0:T(2,128)S(1)} %pad_maximum_fusion.bias), channel_id=1, source_target_pairs={{0,1},{1,0},{2,3},{3,2},{4,5},{5,4},{6,7},{7,6},{8,9},{9,8},{10,11... | collective-permute-start | bytes 3080 | tf_op jit(solution)/shard_map/ppermute | solution.py:277
  10.9 0.1 collective-permute-start.5
  10.9 2.4 %collective-permute-done.wide = bf16[256,512]{1,0:T(8,128)(2,1)S(1)} collective-permute-done((bf16[256,512]{1,0:T(8,128)(2,1)S(1)}, bf16[256,512]{1,0:T(8,128)(2,1)S(1)}, u32[]{:S(2)}, u32[]{:S(2)}) %collective-permute-start) | collective-permute-done | bytes 262176 | tf_op jit(solution)/shard_map/ppermute | solution.py:284
  13.4 0.0 collective-permute-done.1.w1b
  13.4 0.6 %shard_map.102 = (bf16[384,768]{1,0:T(8,128)(2,1)S(1)}, bf16[384,768]{1,0:T(8,128)(2,1)S(1)}, f32[2,128,256]{2,1,0:T(8,128)S(1)}) custom-call(bf16[256,1024]{1,0:T(8,128)(2,1)S(1)} %bitcast.8, bf16[3,3,64,256]{3,2,1,0:T(8,128)(2,1)S(1)} %bitcast.12, bf16[3,3,64,256]{3,2,1,0:T(8,128)(2,1)S(1)} %collective-permute-done.1.w1b, ...), custom_call_target="tpu_custom_call" | custom-call | bytes 3145728 | tf_op jit(solution)/shard_map/pallas_call | solution.py:26
  14.0 0.0 copy-start.4
  14.1 1.9 %shard_map.104.refs_0_ = bf16[128,512]{1,0:T(8,128)(2,1)S(1)} custom-call(bf16[256,1024]{1,0:T(8,128)(2,1)S(1)} %bitcast.9, bf16[512,256]{1,0:T(8,128)(2,1)S(1)} %shard_map.101.halo, bf16[384,768]{1,0:T(8,128)(2,1)S(1)} %get-tuple-element.32.near, bf16[384,768]{1,0:T(8,128)(2,1)S(1)} %get-tuple-element.33.w2s, f32[2,128,256]{2,1,0:T(8,128)S(1)} %get-tuple-element.34.inner, ...), custom_call_target="tpu_custom_call" | custom-call | flops 1207959552 | bytes 2951168 | tf_op jit(solution)/shard_map/pallas_call | solution.py:26
  16.0 0.1 collective-permute-start.7
  16.0 0.2 collective-permute-start.11
  16.3 3.1 %collective-permute-start.12 = (bf16[128,512]{1,0:T(8,128)(2,1)S(1)}, bf16[128,512]{1,0:T(8,128)(2,1)S(1)}, u32[]{:S(2)}, u32[]{:S(2)}) collective-permute-start(bf16[128,512]{1,0:T(8,128)(2,1)S(1)} %shard_map.104.refs_0_), channel_id=1, source_target_pairs={{0,16},{1,17},{2,18},{3,19},{4,20},{5,21},{6,22},{7,23},{8,24},{9,... | collective-permute-start | bytes 393224 | tf_op jit(solution)/shard_map/ppermute | solution.py:284
  19.4 0.8 %collective-permute-start.13 = (bf16[128,512]{1,0:T(8,128)(2,1)S(1)}, bf16[128,512]{1,0:T(8,128)(2,1)S(1)}, u32[]{:S(2)}, u32[]{:S(2)}) collective-permute-start(bf16[128,512]{1,0:T(8,128)(2,1)S(1)} %shard_map.104.refs_0_), channel_id=1, source_target_pairs={{0,24},{1,25},{2,26},{3,27},{4,28},{5,29},{6,30},{7,31},{8,0},{9,1... | collective-permute-start | bytes 393224 | tf_op jit(solution)/shard_map/ppermute | solution.py:284
  20.2 2.5 %collective-permute-start.10 = (f32[8,512]{1,0:T(8,128)S(1)}, f32[8,512]{1,0:T(8,128)S(1)}, u32[]{:S(2)}, u32[]{:S(2)}) collective-permute-start(f32[8,512]{1,0:T(8,128)S(1)} %shard_map.103.table), channel_id=1, source_target_pairs={{0,4},{1,5},{2,6},{3,7},{4,0},{5,1},{6,2},{7,3},{8,12},{9,13},{10,... | collective-permute-start | bytes 49160 | tf_op jit(solution)/shard_map/ppermute | solution.py:284
  22.7 0.6 %collective-permute-start.8 = (bf16[64,128]{1,0:T(8,128)(2,1)S(1)}, bf16[64,128]{1,0:T(8,128)(2,1)S(1)}, u32[]{:S(2)}, u32[]{:S(2)}) collective-permute-start(bf16[64,128]{1,0:T(8,128)(2,1)S(1)} %get-tuple-element.56), channel_id=1, source_target_pairs={{0,2},{1,3},{2,0},{3,1},{4,6},{5,7},{6,4},{7,5},{8,10},{9,11},{10,... | collective-permute-start | bytes 49160 | tf_op jit(solution)/shard_map/ppermute | solution.py:277
  23.3 1.1 %collective-permute-done.10.table = f32[8,512]{1,0:T(8,128)S(1)} collective-permute-done((f32[8,512]{1,0:T(8,128)S(1)}, f32[8,512]{1,0:T(8,128)S(1)}, u32[]{:S(2)}, u32[]{:S(2)}) %collective-permute-start.10) | collective-permute-done | bytes 16416 | tf_op jit(solution)/shard_map/ppermute | solution.py:284
  24.4 0.0 collective-permute-start.9
  24.4 1.9 %shard_map.105.own = bf16[4,512,512]{2,1,0:T(8,128)(2,1)S(1)} custom-call(f32[8,512]{1,0:T(8,128)S(1)} %shard_map.103.table), custom_call_target="tpu_custom_call" | custom-call | tf_op jit(solution)/shard_map/pallas_call | solution.py:26
  26.3 1.9 %shard_map.106.partner = bf16[4,512,512]{2,1,0:T(8,128)(2,1)S(1)} custom-call(f32[8,512]{1,0:T(8,128)S(1)} %collective-permute-done.10.table), custom_call_target="tpu_custom_call" | custom-call | tf_op jit(solution)/shard_map/pallas_call | solution.py:26
  28.3 0.0 copy-start.6
  28.3 1.0 %collective-permute-done.12.refs_2_ = bf16[128,512]{1,0:T(8,128)(2,1)S(1)} collective-permute-done((bf16[128,512]{1,0:T(8,128)(2,1)S(1)}, bf16[128,512]{1,0:T(8,128)(2,1)S(1)}, u32[]{:S(2)}, u32[]{:S(2)}) %collective-permute-start.12) | collective-permute-done | bytes 131104 | tf_op jit(solution)/shard_map/ppermute | solution.py:284
  29.3 0.7 %shard_map.107 = (bf16[128,512]{1,0:T(8,128)(2,1)S(1)}, bf16[128,512]{1,0:T(8,128)(2,1)S(1)}) custom-call(bf16[4,512,512]{2,1,0:T(8,128)(2,1)S(1)} %shard_map.105.own, bf16[4,512,512]{2,1,0:T(8,128)(2,1)S(1)} %shard_map.106.partner, bf16[128,512]{1,0:T(8,128)(2,1)S(1)} %shard_map.104.refs_0_, bf16[128,512]{1,0:T(8,128)(2,1)S(1)} %collective-permute-done.11.refs_1_, ...), custom_call_target="tpu_custom_call" | custom-call | flops 536870912 | bytes 4980736 | tf_op jit(solution)/shard_map/pallas_call | solution.py:26
  30.0 0.1 collective-permute-start.14
  30.1 1.3 %collective-permute-done.14.b = bf16[128,512]{1,0:T(8,128)(2,1)S(1)} collective-permute-done((bf16[128,512]{1,0:T(8,128)(2,1)S(1)}, bf16[128,512]{1,0:T(8,128)(2,1)S(1)}, u32[]{:S(2)}, u32[]{:S(2)}) %collective-permute-start.14) | collective-permute-done | bytes 131104 | tf_op jit(solution)/shard_map/ppermute | solution.py:277
  31.5 0.9 %collective-permute-start.15 = (bf16[128,512]{1,0:T(8,128)(2,1)S(1)}, bf16[128,512]{1,0:T(8,128)(2,1)S(1)}, u32[]{:S(2)}, u32[]{:S(2)}) collective-permute-start(bf16[128,512]{1,0:T(8,128)(2,1)S(1)} %shard_map.108.a), channel_id=1, source_target_pairs={{0,2},{1,7},{2,0},{3,5},{4,6},{5,3},{6,4},{7,1},{8,10},{9,15},{10,... | collective-permute-start | bytes 393224 | tf_op jit(solution)/shard_map/ppermute | solution.py:395
  32.3 0.7 %collective-permute-start.16 = (bf16[128,512]{1,0:T(8,128)(2,1)S(1)}, bf16[128,512]{1,0:T(8,128)(2,1)S(1)}, u32[]{:S(2)}, u32[]{:S(2)}) collective-permute-start(bf16[128,512]{1,0:T(8,128)(2,1)S(1)} %shard_map.108.a), channel_id=1, source_target_pairs={{1,5},{3,7},{5,1},{7,3},{9,13},{11,15},{13,9},{15,11},{17,21},{19,... | collective-permute-start | bytes 393224 | tf_op jit(solution)/shard_map/ppermute | solution.py:396
  33.0 4.9 %collective-permute-done.15.refs_2_ = bf16[128,512]{1,0:T(8,128)(2,1)S(1)} collective-permute-done((bf16[128,512]{1,0:T(8,128)(2,1)S(1)}, bf16[128,512]{1,0:T(8,128)(2,1)S(1)}, u32[]{:S(2)}, u32[]{:S(2)}) %collective-permute-start.15) | collective-permute-done | bytes 131104 | tf_op jit(solution)/shard_map/ppermute | solution.py:395
  37.9 1.7 %collective-permute-start.17 = (bf16[128,512]{1,0:T(8,128)(2,1)S(1)}, bf16[128,512]{1,0:T(8,128)(2,1)S(1)}, u32[]{:S(2)}, u32[]{:S(2)}) collective-permute-start(bf16[128,512]{1,0:T(8,128)(2,1)S(1)} %shard_map.109.refs_0_), channel_id=1, source_target_pairs={{0,1},{1,0},{2,3},{3,2},{4,5},{5,4},{6,7},{7,6},{8,9},{9,8},{10,11... | collective-permute-start | bytes 393224 | tf_op jit(solution)/shard_map/ppermute | solution.py:277
  39.7 0.1 collective-permute-start.18
  39.7 0.1 copy.11.bias
  39.8 0.8 %collective-permute-done.17.refs_1_ = bf16[128,512]{1,0:T(8,128)(2,1)S(1)} collective-permute-done((bf16[128,512]{1,0:T(8,128)(2,1)S(1)}, bf16[128,512]{1,0:T(8,128)(2,1)S(1)}, u32[]{:S(2)}, u32[]{:S(2)}) %collective-permute-start.17) | collective-permute-done | bytes 131104 | tf_op jit(solution)/shard_map/ppermute | solution.py:277
  40.6 0.4 collective-permute-done.18.refs_3_
  41.0 0.9 %shard_map.110 = bf16[128,512]{1,0:T(8,128)(2,1)} custom-call(bf16[64,128]{1,0:T(8,128)(2,1)S(1)} %get-tuple-element.45.wa, bf16[64,128]{1,0:T(8,128)(2,1)S(1)} %collective-permute-done.7.wb, bf16[64,128]{1,0:T(8,128)(2,1)S(1)} %collective-permute-done.8.wc, bf16[64,128]{1,0:T(8,128)(2,1)S(1)} %collective-permute-done.9.wd, f32[128,1]{1,0:T(8,128)S(1)} %copy.11.bias, ...), custom_call_target="tpu_custom_call" | custom-call | flops 67108864 | bytes 721408 | tf_op jit(solution)/shard_map/pallas_call | solution.py:26
  (26 shorter events, 0.2 us)
Async XLA Ops:
  0.0 10.2 %collective-permute-start.3 = (bf16[3,3,64,256]{3,2,1,0:T(8,128)(2,1)}, bf16[3,3,64,256]{3,2,1,0:T(8,128)(2,1)S(1)}, u32[]{:S(2)}, u32[]{:S(2)}) collective-permute-start(bf16[3,3,64,256]{3,2,1,0:T(8,128)(2,1)} %bitcast.10), channel_id=1, source_target_pairs={{0,2},{1,3},{2,0},{3,1},{4,6},{5,7},{6,4},{7,5},{8,10},{9,11},{10,... | collective-permute-start | bytes 884744 | tf_op jit(solution)/shard_map/ppermute | solution.py:277
  4.1 1.7 %copy-start.7 = (f32[64]{0:T(128)S(1)}, f32[64]{0:T(128)}, u32[]{:S(2)}) copy-start(f32[64]{0:T(128)} %param.14) | copy-start | bytes 772
  4.1 1.7 %copy-start.8 = (f32[64]{0:T(128)S(1)}, f32[64]{0:T(128)}, u32[]{:S(2)}) copy-start(f32[64]{0:T(128)} %param.12) | copy-start | bytes 772
  4.1 2.2 %copy-start = (bf16[64,3,3,256]{3,0,2,1:T(8,128)(2,1)S(1)}, bf16[64,3,3,256]{3,0,2,1:T(8,128)(2,1)}, u32[]{:S(2)}) copy-start(bf16[64,3,3,256]{3,0,2,1:T(8,128)(2,1)} %param.11) | copy-start | bytes 884740
  4.1 4.3 %copy-start.1 = (bf16[64,3,3,256]{3,0,2,1:T(8,128)(2,1)S(1)}, bf16[64,3,3,256]{3,0,2,1:T(8,128)(2,1)}, u32[]{:S(2)}) copy-start(bf16[64,3,3,256]{3,0,2,1:T(8,128)(2,1)} %param.13) | copy-start | bytes 884740
  4.2 4.3 %copy-start.5 = (s32[4096]{0:T(1024)S(1)}, s32[4096]{0:T(1024)}, u32[]{:S(2)}) copy-start(s32[4096]{0:T(1024)} %param.15) | copy-start | bytes 49156
  4.2 4.3 %copy-start.2 = (s32[4,512]{1,0:T(4,128)S(1)}, s32[4,512]{1,0:T(4,128)}, u32[]{:S(2)}) copy-start(s32[4,512]{1,0:T(4,128)} %slot.1) | copy-start | bytes 24580
  4.2 4.3 %copy-start.3 = (f32[2,512]{1,0:T(2,128)S(1)}, f32[2,512]{1,0:T(2,128)}, u32[]{:S(2)}) copy-start(f32[2,512]{1,0:T(2,128)} %frac.1) | copy-start | bytes 12292
  4.2 9.1 %collective-permute-start = (bf16[256,512]{1,0:T(8,128)(2,1)S(1)}, bf16[256,512]{1,0:T(8,128)(2,1)S(1)}, u32[]{:S(2)}, u32[]{:S(2)}) collective-permute-start(bf16[256,512]{1,0:T(8,128)(2,1)S(1)} %shard_map.100), channel_id=1, source_target_pairs={{0,4},{1,29},{2,6},{3,31},{4,8},{5,1},{6,10},{7,3},{8,12},{9,5},{1... | collective-permute-start | bytes 786440 | tf_op jit(solution)/shard_map/ppermute | solution.py:284
  5.9 4.4 %collective-permute-start.4 = (f32[1,128]{1,0:T(1,128)S(1)}, f32[1,128]{1,0:T(1,128)S(1)}, u32[]{:S(2)}, u32[]{:S(2)}) collective-permute-start(f32[1,128]{1,0:T(1,128)S(1)} %maximum_bitcast_fusion), channel_id=1, source_target_pairs={{0,2},{1,3},{2,0},{3,1},{4,6},{5,7},{6,4},{7,5},{8,10},{9,11},{10,... | collective-permute-start | bytes 1544 | tf_op jit(solution)/shard_map/ppermute | solution.py:277
  6.4 7.0 %collective-permute-start.1 = (bf16[3,3,64,256]{3,2,1,0:T(8,128)(2,1)S(1)}, bf16[3,3,64,256]{3,2,1,0:T(8,128)(2,1)S(1)}, u32[]{:S(2)}, u32[]{:S(2)}) collective-permute-start(bf16[3,3,64,256]{3,2,1,0:T(8,128)(2,1)S(1)} %bitcast.11), channel_id=1, source_target_pairs={{0,1},{1,0},{2,3},{3,2},{4,5},{5,4},{6,7},{7,6},{8,9},{9,8},{10,11... | collective-permute-start | bytes 884744 | tf_op jit(solution)/shard_map/ppermute | solution.py:277
  8.4 5.0 %collective-permute-start.2 = (bf16[3,3,64,256]{3,2,1,0:T(8,128)(2,1)S(1)}, bf16[3,3,64,256]{3,2,1,0:T(8,128)(2,1)S(1)}, u32[]{:S(2)}, u32[]{:S(2)}) collective-permute-start(bf16[3,3,64,256]{3,2,1,0:T(8,128)(2,1)S(1)} %bitcast.13), channel_id=1, source_target_pairs={{0,1},{1,0},{2,3},{3,2},{4,5},{5,4},{6,7},{7,6},{8,9},{9,8},{10,11... | collective-permute-start | bytes 884744 | tf_op jit(solution)/shard_map/ppermute | solution.py:277
  10.3 3.8 %collective-permute-start.6 = (f32[2,128]{1,0:T(2,128)S(1)}, f32[2,128]{1,0:T(2,128)S(1)}, u32[]{:S(2)}, u32[]{:S(2)}) collective-permute-start(f32[2,128]{1,0:T(2,128)S(1)} %pad_maximum_fusion.bias), channel_id=1, source_target_pairs={{0,1},{1,0},{2,3},{3,2},{4,5},{5,4},{6,7},{7,6},{8,9},{9,8},{10,11... | collective-permute-start | bytes 3080 | tf_op jit(solution)/shard_map/ppermute | solution.py:277
  10.9 3.2 %collective-permute-start.5 = (bf16[3,3,64,256]{3,2,1,0:T(8,128)(2,1)S(1)}, bf16[3,3,64,256]{3,2,1,0:T(8,128)(2,1)S(1)}, u32[]{:S(2)}, u32[]{:S(2)}) collective-permute-start(bf16[3,3,64,256]{3,2,1,0:T(8,128)(2,1)S(1)} %collective-permute-done.3.w1c), channel_id=1, source_target_pairs={{0,1},{1,0},{2,3},{3,2},{4,5},{5,4},{6,7},{7,6},{8,9},{9,8},{10,11... | collective-permute-start | bytes 884744 | tf_op jit(solution)/shard_map/ppermute | solution.py:277
  14.0 1.9 %copy-start.4 = (bf16[64,512]{1,0:T(8,128)(2,1)S(1)}, bf16[64,512]{1,0:T(8,128)(2,1)}, u32[]{:S(2)}) copy-start(bf16[64,512]{1,0:T(8,128)(2,1)} %param.18) | copy-start | bytes 196612
  16.0 6.7 %collective-permute-start.7 = (bf16[64,128]{1,0:T(8,128)(2,1)S(1)}, bf16[64,128]{1,0:T(8,128)(2,1)S(1)}, u32[]{:S(2)}, u32[]{:S(2)}) collective-permute-start(bf16[64,128]{1,0:T(8,128)(2,1)S(1)} %get-tuple-element.57), channel_id=1, source_target_pairs={{0,1},{1,0},{2,3},{3,2},{4,5},{5,4},{6,7},{7,6},{8,9},{9,8},{10,11... | collective-permute-start | bytes 49160 | tf_op jit(solution)/shard_map/ppermute | solution.py:277
  16.0 12.2 %collective-permute-start.11 = (bf16[128,512]{1,0:T(8,128)(2,1)S(1)}, bf16[128,512]{1,0:T(8,128)(2,1)S(1)}, u32[]{:S(2)}, u32[]{:S(2)}) collective-permute-start(bf16[128,512]{1,0:T(8,128)(2,1)S(1)} %shard_map.104.refs_0_), channel_id=1, source_target_pairs={{0,8},{1,9},{2,10},{3,11},{4,12},{5,13},{6,14},{7,15},{8,16},{9,17... | collective-permute-start | bytes 393224 | tf_op jit(solution)/shard_map/ppermute | solution.py:284
  16.3 13.0 %collective-permute-start.12 = (bf16[128,512]{1,0:T(8,128)(2,1)S(1)}, bf16[128,512]{1,0:T(8,128)(2,1)S(1)}, u32[]{:S(2)}, u32[]{:S(2)}) collective-permute-start(bf16[128,512]{1,0:T(8,128)(2,1)S(1)} %shard_map.104.refs_0_), channel_id=1, source_target_pairs={{0,16},{1,17},{2,18},{3,19},{4,20},{5,21},{6,22},{7,23},{8,24},{9,... | collective-permute-start | bytes 393224 | tf_op jit(solution)/shard_map/ppermute | solution.py:284
  19.4 9.9 %collective-permute-start.13 = (bf16[128,512]{1,0:T(8,128)(2,1)S(1)}, bf16[128,512]{1,0:T(8,128)(2,1)S(1)}, u32[]{:S(2)}, u32[]{:S(2)}) collective-permute-start(bf16[128,512]{1,0:T(8,128)(2,1)S(1)} %shard_map.104.refs_0_), channel_id=1, source_target_pairs={{0,24},{1,25},{2,26},{3,27},{4,28},{5,29},{6,30},{7,31},{8,0},{9,1... | collective-permute-start | bytes 393224 | tf_op jit(solution)/shard_map/ppermute | solution.py:284
  20.2 4.2 %collective-permute-start.10 = (f32[8,512]{1,0:T(8,128)S(1)}, f32[8,512]{1,0:T(8,128)S(1)}, u32[]{:S(2)}, u32[]{:S(2)}) collective-permute-start(f32[8,512]{1,0:T(8,128)S(1)} %shard_map.103.table), channel_id=1, source_target_pairs={{0,4},{1,5},{2,6},{3,7},{4,0},{5,1},{6,2},{7,3},{8,12},{9,13},{10,... | collective-permute-start | bytes 49160 | tf_op jit(solution)/shard_map/ppermute | solution.py:284
  22.7 5.5 %collective-permute-start.8 = (bf16[64,128]{1,0:T(8,128)(2,1)S(1)}, bf16[64,128]{1,0:T(8,128)(2,1)S(1)}, u32[]{:S(2)}, u32[]{:S(2)}) collective-permute-start(bf16[64,128]{1,0:T(8,128)(2,1)S(1)} %get-tuple-element.56), channel_id=1, source_target_pairs={{0,2},{1,3},{2,0},{3,1},{4,6},{5,7},{6,4},{7,5},{8,10},{9,11},{10,... | collective-permute-start | bytes 49160 | tf_op jit(solution)/shard_map/ppermute | solution.py:277
  24.4 3.8 %collective-permute-start.9 = (bf16[64,128]{1,0:T(8,128)(2,1)S(1)}, bf16[64,128]{1,0:T(8,128)(2,1)S(1)}, u32[]{:S(2)}, u32[]{:S(2)}) collective-permute-start(bf16[64,128]{1,0:T(8,128)(2,1)S(1)} %get-tuple-element.55), channel_id=1, source_target_pairs={{0,3},{1,2},{2,1},{3,0},{4,7},{5,6},{6,5},{7,4},{8,11},{9,10},{10,... | collective-permute-start | bytes 49160 | tf_op jit(solution)/shard_map/ppermute | solution.py:277
  28.3 11.5 %copy-start.6 = (f32[128]{0:T(128)S(1)}, f32[128]{0:T(128)}, u32[]{:S(2)}) copy-start(f32[128]{0:T(128)} %param.19) | copy-start | bytes 1540
  30.0 1.4 %collective-permute-start.14 = (bf16[128,512]{1,0:T(8,128)(2,1)S(1)}, bf16[128,512]{1,0:T(8,128)(2,1)S(1)}, u32[]{:S(2)}, u32[]{:S(2)}) collective-permute-start(bf16[128,512]{1,0:T(8,128)(2,1)S(1)} %get-tuple-element.52), channel_id=1, source_target_pairs={{0,1},{1,0},{2,3},{3,2},{4,5},{5,4},{6,7},{7,6},{8,9},{9,8},{10,11... | collective-permute-start | bytes 393224 | tf_op jit(solution)/shard_map/ppermute | solution.py:277
  31.5 6.4 %collective-permute-start.15 = (bf16[128,512]{1,0:T(8,128)(2,1)S(1)}, bf16[128,512]{1,0:T(8,128)(2,1)S(1)}, u32[]{:S(2)}, u32[]{:S(2)}) collective-permute-start(bf16[128,512]{1,0:T(8,128)(2,1)S(1)} %shard_map.108.a), channel_id=1, source_target_pairs={{0,2},{1,7},{2,0},{3,5},{4,6},{5,3},{6,4},{7,1},{8,10},{9,15},{10,... | collective-permute-start | bytes 393224 | tf_op jit(solution)/shard_map/ppermute | solution.py:395
  32.3 5.6 %collective-permute-start.16 = (bf16[128,512]{1,0:T(8,128)(2,1)S(1)}, bf16[128,512]{1,0:T(8,128)(2,1)S(1)}, u32[]{:S(2)}, u32[]{:S(2)}) collective-permute-start(bf16[128,512]{1,0:T(8,128)(2,1)S(1)} %shard_map.108.a), channel_id=1, source_target_pairs={{1,5},{3,7},{5,1},{7,3},{9,13},{11,15},{13,9},{15,11},{17,21},{19,... | collective-permute-start | bytes 393224 | tf_op jit(solution)/shard_map/ppermute | solution.py:396
  37.9 2.7 %collective-permute-start.17 = (bf16[128,512]{1,0:T(8,128)(2,1)S(1)}, bf16[128,512]{1,0:T(8,128)(2,1)S(1)}, u32[]{:S(2)}, u32[]{:S(2)}) collective-permute-start(bf16[128,512]{1,0:T(8,128)(2,1)S(1)} %shard_map.109.refs_0_), channel_id=1, source_target_pairs={{0,1},{1,0},{2,3},{3,2},{4,5},{5,4},{6,7},{7,6},{8,9},{9,8},{10,11... | collective-permute-start | bytes 393224 | tf_op jit(solution)/shard_map/ppermute | solution.py:277
  39.7 1.3 %collective-permute-start.18 = (bf16[128,512]{1,0:T(8,128)(2,1)S(1)}, bf16[128,512]{1,0:T(8,128)(2,1)S(1)}, u32[]{:S(2)}, u32[]{:S(2)}) collective-permute-start(bf16[128,512]{1,0:T(8,128)(2,1)S(1)} %collective-permute-done.15.refs_2_), channel_id=1, source_target_pairs={{0,1},{1,0},{2,3},{3,2},{4,5},{5,4},{6,7},{7,6},{8,9},{9,8},{10,11... | collective-permute-start | bytes 393224 | tf_op jit(solution)/shard_map/ppermute | solution.py:277

commit v4 on v3

--- a/solution.py
+++ b/solution.py
@@ -184,21 +184,17 @@
     lax.fori_loop(0, blocks * held // rows, step, 0)
 
 
-def resample_kernel(own, partner, *refs):
-    held, kept, sent = refs[:-2], refs[-2], refs[-1]
-    first = lax.rem(lax.axis_index("ch"), 2) == 0
-    samples = []
-    for sampling in (own, partner):
-        total = jnp.zeros(kept.shape, F32)
-        for m, block in enumerate(held):
-            total = total + jnp.dot(block[...], sampling[m], preferred_element_type=F32)
-        samples.append(total)
-    kept[...] = jnp.where(first, samples[0], samples[1]).astype(BF16)
-    sent[...] = jnp.where(first, samples[1], samples[0]).astype(BF16)
-
-
-def pass_kernel(a, out):
-    out[...] = a[...]
+def resample_kernel(*refs, chosen):
+    samplings, held, out = refs[:2], refs[2:-1], refs[-1]
+    core = lax.rem(lax.axis_index("ch"), 2)
+    for c in range(2):
+
+        @pl.when(core == c)
+        def _(sampling=samplings[chosen ^ c]):
+            total = jnp.zeros(out.shape, F32)
+            for m, block in enumerate(held):
+                total = total + jnp.dot(block[...], sampling[m], preferred_element_type=F32)
+            out[...] = total.astype(BF16)
 
 
 def add_kernel(a, b, out):
@@ -377,14 +373,17 @@
         expand_weight, mine = lax.optimization_barrier((expand_weight, mine))
         slices = expansion_slices(expand_weight)
         held[0], slices = lax.optimization_barrier((held[0], slices))
-        kept, sent = call(
-            resample_kernel,
-            [shape((2 * share, cells), BF16)] * 2,
-            *samplings,
-            *held,
-            flops=4 * share * slots * cells,
-        )
         tile = shape((2 * share, cells), BF16)
+        sent, kept = [
+            call(
+                functools.partial(resample_kernel, chosen=chosen),
+                [tile],
+                *samplings,
+                *held,
+                flops=2 * share * slots * cells,
+            )[0]
+            for chosen in (1, 0)
+        ]
         (kept,) = call(add_kernel, [tile], kept, swap(sent, 1))
         other_plane, same_plane = [], []
         for a in range(n_az):

time: 42 us -> 41.8 us (level)
    ppermute x12, waiting for transfers between devices: 3.86 us -> 3.41 us  [swap(): return lax.ppermute(x, 'ch', [(i, i ^ mask) for i in range(n_ch)])]
    pallas_call x11 -> x12, Pallas kernels: 8.3 us -> 8.47 us  [call(): pl.pallas_call(kernel, out_shape=tuple(outs), in_specs=specs, out_specs=t...]
  transfers between devices with their start and end apart: 19 -> 19, of which waited for: 9 -> 9; matrix products, arithmetic and copies ran while one was open for 3% -> 3% of each run, Pallas kernels for 11% -> 13%
where the time goes in v4:
time: 41.8 us; the launch traced here: 41.6 us
  starting transfers between devices  18.6 us (44%)
  waiting for transfers between devices  12.9 us (31%)
  Pallas kernels  8.47 us (20%)
  local copies, waits for them, and re-layouts  1.33 us (3%)
    ppermute x12, starting transfers between devices, swap(): return lax.ppermute(x, 'ch', [(i, i ^ mask) for i in range(n_ch)])  8.85 us
    pallas_call x12, Pallas kernels, call(): pl.pallas_call(kernel, out_shape=tuple(outs), in_specs=specs, out_specs=t...  8.47 us
    ppermute x5, starting transfers between devices, joint(): return lax.ppermute(x, ('az', 'ch'), pairs)  8.2 us
    ppermute x1, waiting for transfers between devices, local(): far = lax.ppermute(kept, ('az', 'ch'), other_plane)  4.92 us
    ppermute x5, waiting for transfers between devices, joint(): return lax.ppermute(x, ('az', 'ch'), pairs)  4.57 us
    ppermute x12, waiting for transfers between devices, swap(): return lax.ppermute(x, 'ch', [(i, i ^ mask) for i in range(n_ch)])  3.41 us
    unnamed x19, local copies, waits for them, and re-layouts  1.19 us
    ppermute x1, starting transfers between devices, local(): far = lax.ppermute(kept, ('az', 'ch'), other_plane)  0.85 us
  transfers between devices with their start and end apart: 19, of which 9 were waited for; matrix products, arithmetic and copies ran while one was open for 3% of the time, Pallas kernels for 13%

profile of v4, /device:TPU:0, one launch (start us, length us, event | category | flops | bytes accessed | tf_op | source)
XLA Modules:
  0.0 41.6 jit_solution(17046394677347102099)
XLA Ops:
  0.0 3.0 %collective-permute-start.3 = (bf16[3,3,64,256]{3,2,1,0:T(8,128)(2,1)}, bf16[3,3,64,256]{3,2,1,0:T(8,128)(2,1)S(1)}, u32[]{:S(2)}, u32[]{:S(2)}) collective-permute-start(bf16[3,3,64,256]{3,2,1,0:T(8,128)(2,1)} %bitcast.10), channel_id=1, source_target_pairs={{0,2},{1,3},{2,0},{3,1},{4,6},{5,7},{6,4},{7,5},{8,10},{9,11},{10,... | collective-permute-start | bytes 884744 | tf_op jit(solution)/shard_map/ppermute | solution.py:273
  3.0 1.1 %copy.12 = bf16[32,8,4,256]{3,1,2,0:T(8,128)(2,1)S(1)} copy(bf16[32,8,4,256]{3,2,1,0:T(4,128)(2,1)} %bitcast.15) | data formatting | bytes 1048576
  4.1 0.0 copy-start.7
  4.1 0.0 copy-start.8
  4.1 0.0 copy-start
  4.1 0.0 copy-start.1
  4.2 0.0 copy-start.5
  4.2 0.0 copy-start.2
  4.2 0.0 copy-start.3
  4.2 1.5 %collective-permute-start = (bf16[256,512]{1,0:T(8,128)(2,1)S(1)}, bf16[256,512]{1,0:T(8,128)(2,1)S(1)}, u32[]{:S(2)}, u32[]{:S(2)}) collective-permute-start(bf16[256,512]{1,0:T(8,128)(2,1)S(1)} %shard_map.100), channel_id=1, source_target_pairs={{0,4},{1,29},{2,6},{3,31},{4,8},{5,1},{6,10},{7,3},{8,12},{9,5},{1... | collective-permute-start | bytes 786440 | tf_op jit(solution)/shard_map/ppermute | solution.py:280
  5.8 0.1 maximum_bitcast_fusion
  5.9 0.5 %collective-permute-start.4 = (f32[1,128]{1,0:T(1,128)S(1)}, f32[1,128]{1,0:T(1,128)S(1)}, u32[]{:S(2)}, u32[]{:S(2)}) collective-permute-start(f32[1,128]{1,0:T(1,128)S(1)} %maximum_bitcast_fusion), channel_id=1, source_target_pairs={{0,2},{1,3},{2,0},{3,1},{4,6},{5,7},{6,4},{7,5},{8,10},{9,11},{10,... | collective-permute-start | bytes 1544 | tf_op jit(solution)/shard_map/ppermute | solution.py:273
  6.4 2.0 %collective-permute-start.1 = (bf16[3,3,64,256]{3,2,1,0:T(8,128)(2,1)S(1)}, bf16[3,3,64,256]{3,2,1,0:T(8,128)(2,1)S(1)}, u32[]{:S(2)}, u32[]{:S(2)}) collective-permute-start(bf16[3,3,64,256]{3,2,1,0:T(8,128)(2,1)S(1)} %bitcast.11), channel_id=1, source_target_pairs={{0,1},{1,0},{2,3},{3,2},{4,5},{5,4},{6,7},{7,6},{8,9},{9,8},{10,11... | collective-permute-start | bytes 884744 | tf_op jit(solution)/shard_map/ppermute | solution.py:273
  8.4 0.1 collective-permute-start.2
  8.5 0.3 shard_map.103.table
  8.8 1.4 %collective-permute-done.3.w1c = bf16[3,3,64,256]{3,2,1,0:T(8,128)(2,1)S(1)} collective-permute-done((bf16[3,3,64,256]{3,2,1,0:T(8,128)(2,1)}, bf16[3,3,64,256]{3,2,1,0:T(8,128)(2,1)S(1)}, u32[]{:S(2)}, u32[]{:S(2)}) %collective-permute-start.3) | collective-permute-done | bytes 294944 | tf_op jit(solution)/shard_map/ppermute | solution.py:273
  10.2 0.1 collective-permute-done.4
  10.3 0.6 %collective-permute-start.6 = (f32[2,128]{1,0:T(2,128)S(1)}, f32[2,128]{1,0:T(2,128)S(1)}, u32[]{:S(2)}, u32[]{:S(2)}) collective-permute-start(f32[2,128]{1,0:T(2,128)S(1)} %pad_maximum_fusion.bias), channel_id=1, source_target_pairs={{0,1},{1,0},{2,3},{3,2},{4,5},{5,4},{6,7},{7,6},{8,9},{9,8},{10,11... | collective-permute-start | bytes 3080 | tf_op jit(solution)/shard_map/ppermute | solution.py:273
  10.9 0.1 collective-permute-start.5
  10.9 2.4 %collective-permute-done.wide = bf16[256,512]{1,0:T(8,128)(2,1)S(1)} collective-permute-done((bf16[256,512]{1,0:T(8,128)(2,1)S(1)}, bf16[256,512]{1,0:T(8,128)(2,1)S(1)}, u32[]{:S(2)}, u32[]{:S(2)}) %collective-permute-start) | collective-permute-done | bytes 262176 | tf_op jit(solution)/shard_map/ppermute | solution.py:280
  13.4 0.0 collective-permute-done.2.w2b
  13.4 0.6 %shard_map.102 = (bf16[384,768]{1,0:T(8,128)(2,1)S(1)}, bf16[384,768]{1,0:T(8,128)(2,1)S(1)}, f32[2,128,256]{2,1,0:T(8,128)S(1)}) custom-call(bf16[256,1024]{1,0:T(8,128)(2,1)S(1)} %bitcast.8, bf16[3,3,64,256]{3,2,1,0:T(8,128)(2,1)S(1)} %bitcast.12, bf16[3,3,64,256]{3,2,1,0:T(8,128)(2,1)S(1)} %collective-permute-done.1.w1b, ...), custom_call_target="tpu_custom_call" | custom-call | bytes 3145728 | tf_op jit(solution)/shard_map/pallas_call | solution.py:26
  14.0 0.0 copy-start.4
  14.1 1.9 %shard_map.104.refs_2_ = bf16[128,512]{1,0:T(8,128)(2,1)S(1)} custom-call(bf16[256,1024]{1,0:T(8,128)(2,1)S(1)} %bitcast.9, bf16[512,256]{1,0:T(8,128)(2,1)S(1)} %shard_map.101.halo, bf16[384,768]{1,0:T(8,128)(2,1)S(1)} %get-tuple-element.30.near, bf16[384,768]{1,0:T(8,128)(2,1)S(1)} %get-tuple-element.31.w2s, f32[2,128,256]{2,1,0:T(8,128)S(1)} %get-tuple-element.32.inner, ...), custom_call_target="tpu_custom_call" | custom-call | flops 1207959552 | bytes 2951168 | tf_op jit(solution)/shard_map/pallas_call | solution.py:26
  16.0 0.1 collective-permute-start.7
  16.0 0.2 collective-permute-start.11
  16.3 3.1 %collective-permute-start.12 = (bf16[128,512]{1,0:T(8,128)(2,1)S(1)}, bf16[128,512]{1,0:T(8,128)(2,1)S(1)}, u32[]{:S(2)}, u32[]{:S(2)}) collective-permute-start(bf16[128,512]{1,0:T(8,128)(2,1)S(1)} %shard_map.104.refs_2_), channel_id=1, source_target_pairs={{0,16},{1,17},{2,18},{3,19},{4,20},{5,21},{6,22},{7,23},{8,24},{9,... | collective-permute-start | bytes 393224 | tf_op jit(solution)/shard_map/ppermute | solution.py:280
  19.4 0.8 %collective-permute-start.13 = (bf16[128,512]{1,0:T(8,128)(2,1)S(1)}, bf16[128,512]{1,0:T(8,128)(2,1)S(1)}, u32[]{:S(2)}, u32[]{:S(2)}) collective-permute-start(bf16[128,512]{1,0:T(8,128)(2,1)S(1)} %shard_map.104.refs_2_), channel_id=1, source_target_pairs={{0,24},{1,25},{2,26},{3,27},{4,28},{5,29},{6,30},{7,31},{8,0},{9,1... | collective-permute-start | bytes 393224 | tf_op jit(solution)/shard_map/ppermute | solution.py:280
  20.2 2.5 %collective-permute-start.10 = (f32[8,512]{1,0:T(8,128)S(1)}, f32[8,512]{1,0:T(8,128)S(1)}, u32[]{:S(2)}, u32[]{:S(2)}) collective-permute-start(f32[8,512]{1,0:T(8,128)S(1)} %shard_map.103.table), channel_id=1, source_target_pairs={{0,4},{1,5},{2,6},{3,7},{4,0},{5,1},{6,2},{7,3},{8,12},{9,13},{10,... | collective-permute-start | bytes 49160 | tf_op jit(solution)/shard_map/ppermute | solution.py:280
  22.7 0.6 %collective-permute-start.8 = (bf16[64,128]{1,0:T(8,128)(2,1)S(1)}, bf16[64,128]{1,0:T(8,128)(2,1)S(1)}, u32[]{:S(2)}, u32[]{:S(2)}) collective-permute-start(bf16[64,128]{1,0:T(8,128)(2,1)S(1)} %get-tuple-element.52), channel_id=1, source_target_pairs={{0,2},{1,3},{2,0},{3,1},{4,6},{5,7},{6,4},{7,5},{8,10},{9,11},{10,... | collective-permute-start | bytes 49160 | tf_op jit(solution)/shard_map/ppermute | solution.py:273
  23.3 1.1 %collective-permute-done.10.table = f32[8,512]{1,0:T(8,128)S(1)} collective-permute-done((f32[8,512]{1,0:T(8,128)S(1)}, f32[8,512]{1,0:T(8,128)S(1)}, u32[]{:S(2)}, u32[]{:S(2)}) %collective-permute-start.10) | collective-permute-done | bytes 16416 | tf_op jit(solution)/shard_map/ppermute | solution.py:280
  24.4 1.9 %shard_map.105.refs_0_ = bf16[4,512,512]{2,1,0:T(8,128)(2,1)S(1)} custom-call(f32[8,512]{1,0:T(8,128)S(1)} %shard_map.103.table), custom_call_target="tpu_custom_call" | custom-call | tf_op jit(solution)/shard_map/pallas_call | solution.py:26
  26.3 1.9 %shard_map.106.refs_1_ = bf16[4,512,512]{2,1,0:T(8,128)(2,1)S(1)} custom-call(f32[8,512]{1,0:T(8,128)S(1)} %collective-permute-done.10.table), custom_call_target="tpu_custom_call" | custom-call | tf_op jit(solution)/shard_map/pallas_call | solution.py:26
  28.3 1.0 %collective-permute-done.12.refs_4_ = bf16[128,512]{1,0:T(8,128)(2,1)S(1)} collective-permute-done((bf16[128,512]{1,0:T(8,128)(2,1)S(1)}, bf16[128,512]{1,0:T(8,128)(2,1)S(1)}, u32[]{:S(2)}, u32[]{:S(2)}) %collective-permute-start.12) | collective-permute-done | bytes 131104 | tf_op jit(solution)/shard_map/ppermute | solution.py:280
  29.3 0.4 %shard_map.108 = bf16[128,512]{1,0:T(8,128)(2,1)S(1)} custom-call(bf16[4,512,512]{2,1,0:T(8,128)(2,1)S(1)} %shard_map.105.refs_0_, bf16[4,512,512]{2,1,0:T(8,128)(2,1)S(1)} %shard_map.106.refs_1_, bf16[128,512]{1,0:T(8,128)(2,1)S(1)} %shard_map.104.refs_2_, bf16[128,512]{1,0:T(8,128)(2,1)S(1)} %collective-permute-done.11.refs_3_, ...), custom_call_target="tpu_custom_call" | custom-call | flops 268435456 | bytes 4849664 | tf_op jit(solution)/shard_map/pallas_call | solution.py:26
  29.7 0.0 copy-start.6
  29.7 0.1 collective-permute-start.14
  29.9 0.4 %shard_map.107.a = bf16[128,512]{1,0:T(8,128)(2,1)S(1)} custom-call(bf16[4,512,512]{2,1,0:T(8,128)(2,1)S(1)} %shard_map.105.refs_0_, bf16[4,512,512]{2,1,0:T(8,128)(2,1)S(1)} %shard_map.106.refs_1_, bf16[128,512]{1,0:T(8,128)(2,1)S(1)} %shard_map.104.refs_2_, bf16[128,512]{1,0:T(8,128)(2,1)S(1)} %collective-permute-done.11.refs_3_, ...), custom_call_target="tpu_custom_call" | custom-call | flops 268435456 | bytes 4849664 | tf_op jit(solution)/shard_map/pallas_call | solution.py:26
  30.3 0.8 %collective-permute-done.14.b = bf16[128,512]{1,0:T(8,128)(2,1)S(1)} collective-permute-done((bf16[128,512]{1,0:T(8,128)(2,1)S(1)}, bf16[128,512]{1,0:T(8,128)(2,1)S(1)}, u32[]{:S(2)}, u32[]{:S(2)}) %collective-permute-start.14) | collective-permute-done | bytes 131104 | tf_op jit(solution)/shard_map/ppermute | solution.py:273
  31.2 0.9 %collective-permute-start.15 = (bf16[128,512]{1,0:T(8,128)(2,1)S(1)}, bf16[128,512]{1,0:T(8,128)(2,1)S(1)}, u32[]{:S(2)}, u32[]{:S(2)}) collective-permute-start(bf16[128,512]{1,0:T(8,128)(2,1)S(1)} %shard_map.109.a), channel_id=1, source_target_pairs={{0,2},{1,7},{2,0},{3,5},{4,6},{5,3},{6,4},{7,1},{8,10},{9,15},{10,... | collective-permute-start | bytes 393224 | tf_op jit(solution)/shard_map/ppermute | solution.py:394
  32.0 0.7 %collective-permute-start.16 = (bf16[128,512]{1,0:T(8,128)(2,1)S(1)}, bf16[128,512]{1,0:T(8,128)(2,1)S(1)}, u32[]{:S(2)}, u32[]{:S(2)}) collective-permute-start(bf16[128,512]{1,0:T(8,128)(2,1)S(1)} %shard_map.109.a), channel_id=1, source_target_pairs={{1,5},{3,7},{5,1},{7,3},{9,13},{11,15},{13,9},{15,11},{17,21},{19,... | collective-permute-start | bytes 393224 | tf_op jit(solution)/shard_map/ppermute | solution.py:395
  32.7 4.9 %collective-permute-done.15.refs_2_ = bf16[128,512]{1,0:T(8,128)(2,1)S(1)} collective-permute-done((bf16[128,512]{1,0:T(8,128)(2,1)S(1)}, bf16[128,512]{1,0:T(8,128)(2,1)S(1)}, u32[]{:S(2)}, u32[]{:S(2)}) %collective-permute-start.15) | collective-permute-done | bytes 131104 | tf_op jit(solution)/shard_map/ppermute | solution.py:394
  37.7 1.7 %collective-permute-start.17 = (bf16[128,512]{1,0:T(8,128)(2,1)S(1)}, bf16[128,512]{1,0:T(8,128)(2,1)S(1)}, u32[]{:S(2)}, u32[]{:S(2)}) collective-permute-start(bf16[128,512]{1,0:T(8,128)(2,1)S(1)} %shard_map.110.refs_0_), channel_id=1, source_target_pairs={{0,1},{1,0},{2,3},{3,2},{4,5},{5,4},{6,7},{7,6},{8,9},{9,8},{10,11... | collective-permute-start | bytes 393224 | tf_op jit(solution)/shard_map/ppermute | solution.py:273
  39.4 0.1 collective-permute-start.18
  39.5 0.1 copy.11.bias
  39.6 0.8 %collective-permute-done.17.refs_1_ = bf16[128,512]{1,0:T(8,128)(2,1)S(1)} collective-permute-done((bf16[128,512]{1,0:T(8,128)(2,1)S(1)}, bf16[128,512]{1,0:T(8,128)(2,1)S(1)}, u32[]{:S(2)}, u32[]{:S(2)}) %collective-permute-start.17) | collective-permute-done | bytes 131104 | tf_op jit(solution)/shard_map/ppermute | solution.py:273
  40.4 0.4 collective-permute-done.18.refs_3_
  40.7 0.9 %shard_map.111 = bf16[128,512]{1,0:T(8,128)(2,1)} custom-call(bf16[64,128]{1,0:T(8,128)(2,1)S(1)} %get-tuple-element.43.wa, bf16[64,128]{1,0:T(8,128)(2,1)S(1)} %collective-permute-done.7.wb, bf16[64,128]{1,0:T(8,128)(2,1)S(1)} %collective-permute-done.8.wc, bf16[64,128]{1,0:T(8,128)(2,1)S(1)} %collective-permute-done.9.wd, f32[128,1]{1,0:T(8,128)S(1)} %copy.11.bias, ...), custom_call_target="tpu_custom_call" | custom-call | flops 67108864 | bytes 721408 | tf_op jit(solution)/shard_map/pallas_call | solution.py:26
  (27 shorter events, 0.2 us)
Async XLA Ops:
  0.0 10.2 %collective-permute-start.3 = (bf16[3,3,64,256]{3,2,1,0:T(8,128)(2,1)}, bf16[3,3,64,256]{3,2,1,0:T(8,128)(2,1)S(1)}, u32[]{:S(2)}, u32[]{:S(2)}) collective-permute-start(bf16[3,3,64,256]{3,2,1,0:T(8,128)(2,1)} %bitcast.10), channel_id=1, source_target_pairs={{0,2},{1,3},{2,0},{3,1},{4,6},{5,7},{6,4},{7,5},{8,10},{9,11},{10,... | collective-permute-start | bytes 884744 | tf_op jit(solution)/shard_map/ppermute | solution.py:273
  4.1 1.7 %copy-start.7 = (f32[64]{0:T(128)S(1)}, f32[64]{0:T(128)}, u32[]{:S(2)}) copy-start(f32[64]{0:T(128)} %param.14) | copy-start | bytes 772
  4.1 1.7 %copy-start.8 = (f32[64]{0:T(128)S(1)}, f32[64]{0:T(128)}, u32[]{:S(2)}) copy-start(f32[64]{0:T(128)} %param.12) | copy-start | bytes 772
  4.1 2.2 %copy-start = (bf16[64,3,3,256]{3,0,2,1:T(8,128)(2,1)S(1)}, bf16[64,3,3,256]{3,0,2,1:T(8,128)(2,1)}, u32[]{:S(2)}) copy-start(bf16[64,3,3,256]{3,0,2,1:T(8,128)(2,1)} %param.11) | copy-start | bytes 884740
  4.1 4.3 %copy-start.1 = (bf16[64,3,3,256]{3,0,2,1:T(8,128)(2,1)S(1)}, bf16[64,3,3,256]{3,0,2,1:T(8,128)(2,1)}, u32[]{:S(2)}) copy-start(bf16[64,3,3,256]{3,0,2,1:T(8,128)(2,1)} %param.13) | copy-start | bytes 884740
  4.2 4.3 %copy-start.5 = (s32[4096]{0:T(1024)S(1)}, s32[4096]{0:T(1024)}, u32[]{:S(2)}) copy-start(s32[4096]{0:T(1024)} %param.15) | copy-start | bytes 49156
  4.2 4.3 %copy-start.2 = (s32[4,512]{1,0:T(4,128)S(1)}, s32[4,512]{1,0:T(4,128)}, u32[]{:S(2)}) copy-start(s32[4,512]{1,0:T(4,128)} %slot.1) | copy-start | bytes 24580
  4.2 4.3 %copy-start.3 = (f32[2,512]{1,0:T(2,128)S(1)}, f32[2,512]{1,0:T(2,128)}, u32[]{:S(2)}) copy-start(f32[2,512]{1,0:T(2,128)} %frac.1) | copy-start | bytes 12292
  4.2 9.1 %collective-permute-start = (bf16[256,512]{1,0:T(8,128)(2,1)S(1)}, bf16[256,512]{1,0:T(8,128)(2,1)S(1)}, u32[]{:S(2)}, u32[]{:S(2)}) collective-permute-start(bf16[256,512]{1,0:T(8,128)(2,1)S(1)} %shard_map.100), channel_id=1, source_target_pairs={{0,4},{1,29},{2,6},{3,31},{4,8},{5,1},{6,10},{7,3},{8,12},{9,5},{1... | collective-permute-start | bytes 786440 | tf_op jit(solution)/shard_map/ppermute | solution.py:280
  5.9 4.4 %collective-permute-start.4 = (f32[1,128]{1,0:T(1,128)S(1)}, f32[1,128]{1,0:T(1,128)S(1)}, u32[]{:S(2)}, u32[]{:S(2)}) collective-permute-start(f32[1,128]{1,0:T(1,128)S(1)} %maximum_bitcast_fusion), channel_id=1, source_target_pairs={{0,2},{1,3},{2,0},{3,1},{4,6},{5,7},{6,4},{7,5},{8,10},{9,11},{10,... | collective-permute-start | bytes 1544 | tf_op jit(solution)/shard_map/ppermute | solution.py:273
  6.4 7.0 %collective-permute-start.1 = (bf16[3,3,64,256]{3,2,1,0:T(8,128)(2,1)S(1)}, bf16[3,3,64,256]{3,2,1,0:T(8,128)(2,1)S(1)}, u32[]{:S(2)}, u32[]{:S(2)}) collective-permute-start(bf16[3,3,64,256]{3,2,1,0:T(8,128)(2,1)S(1)} %bitcast.11), channel_id=1, source_target_pairs={{0,1},{1,0},{2,3},{3,2},{4,5},{5,4},{6,7},{7,6},{8,9},{9,8},{10,11... | collective-permute-start | bytes 884744 | tf_op jit(solution)/shard_map/ppermute | solution.py:273
  8.4 5.0 %collective-permute-start.2 = (bf16[3,3,64,256]{3,2,1,0:T(8,128)(2,1)S(1)}, bf16[3,3,64,256]{3,2,1,0:T(8,128)(2,1)S(1)}, u32[]{:S(2)}, u32[]{:S(2)}) collective-permute-start(bf16[3,3,64,256]{3,2,1,0:T(8,128)(2,1)S(1)} %bitcast.13), channel_id=1, source_target_pairs={{0,1},{1,0},{2,3},{3,2},{4,5},{5,4},{6,7},{7,6},{8,9},{9,8},{10,11... | collective-permute-start | bytes 884744 | tf_op jit(solution)/shard_map/ppermute | solution.py:273
  10.3 3.8 %collective-permute-start.6 = (f32[2,128]{1,0:T(2,128)S(1)}, f32[2,128]{1,0:T(2,128)S(1)}, u32[]{:S(2)}, u32[]{:S(2)}) collective-permute-start(f32[2,128]{1,0:T(2,128)S(1)} %pad_maximum_fusion.bias), channel_id=1, source_target_pairs={{0,1},{1,0},{2,3},{3,2},{4,5},{5,4},{6,7},{7,6},{8,9},{9,8},{10,11... | collective-permute-start | bytes 3080 | tf_op jit(solution)/shard_map/ppermute | solution.py:273
  10.9 3.2 %collective-permute-start.5 = (bf16[3,3,64,256]{3,2,1,0:T(8,128)(2,1)S(1)}, bf16[3,3,64,256]{3,2,1,0:T(8,128)(2,1)S(1)}, u32[]{:S(2)}, u32[]{:S(2)}) collective-permute-start(bf16[3,3,64,256]{3,2,1,0:T(8,128)(2,1)S(1)} %collective-permute-done.3.w1c), channel_id=1, source_target_pairs={{0,1},{1,0},{2,3},{3,2},{4,5},{5,4},{6,7},{7,6},{8,9},{9,8},{10,11... | collective-permute-start | bytes 884744 | tf_op jit(solution)/shard_map/ppermute | solution.py:273
  14.0 1.9 %copy-start.4 = (bf16[64,512]{1,0:T(8,128)(2,1)S(1)}, bf16[64,512]{1,0:T(8,128)(2,1)}, u32[]{:S(2)}) copy-start(bf16[64,512]{1,0:T(8,128)(2,1)} %param.18) | copy-start | bytes 196612
  16.0 6.7 %collective-permute-start.7 = (bf16[64,128]{1,0:T(8,128)(2,1)S(1)}, bf16[64,128]{1,0:T(8,128)(2,1)S(1)}, u32[]{:S(2)}, u32[]{:S(2)}) collective-permute-start(bf16[64,128]{1,0:T(8,128)(2,1)S(1)} %get-tuple-element.53), channel_id=1, source_target_pairs={{0,1},{1,0},{2,3},{3,2},{4,5},{5,4},{6,7},{7,6},{8,9},{9,8},{10,11... | collective-permute-start | bytes 49160 | tf_op jit(solution)/shard_map/ppermute | solution.py:273
  16.0 12.2 %collective-permute-start.11 = (bf16[128,512]{1,0:T(8,128)(2,1)S(1)}, bf16[128,512]{1,0:T(8,128)(2,1)S(1)}, u32[]{:S(2)}, u32[]{:S(2)}) collective-permute-start(bf16[128,512]{1,0:T(8,128)(2,1)S(1)} %shard_map.104.refs_2_), channel_id=1, source_target_pairs={{0,8},{1,9},{2,10},{3,11},{4,12},{5,13},{6,14},{7,15},{8,16},{9,17... | collective-permute-start | bytes 393224 | tf_op jit(solution)/shard_map/ppermute | solution.py:280
  16.3 13.0 %collective-permute-start.12 = (bf16[128,512]{1,0:T(8,128)(2,1)S(1)}, bf16[128,512]{1,0:T(8,128)(2,1)S(1)}, u32[]{:S(2)}, u32[]{:S(2)}) collective-permute-start(bf16[128,512]{1,0:T(8,128)(2,1)S(1)} %shard_map.104.refs_2_), channel_id=1, source_target_pairs={{0,16},{1,17},{2,18},{3,19},{4,20},{5,21},{6,22},{7,23},{8,24},{9,... | collective-permute-start | bytes 393224 | tf_op jit(solution)/shard_map/ppermute | solution.py:280
  19.4 9.9 %collective-permute-start.13 = (bf16[128,512]{1,0:T(8,128)(2,1)S(1)}, bf16[128,512]{1,0:T(8,128)(2,1)S(1)}, u32[]{:S(2)}, u32[]{:S(2)}) collective-permute-start(bf16[128,512]{1,0:T(8,128)(2,1)S(1)} %shard_map.104.refs_2_), channel_id=1, source_target_pairs={{0,24},{1,25},{2,26},{3,27},{4,28},{5,29},{6,30},{7,31},{8,0},{9,1... | collective-permute-start | bytes 393224 | tf_op jit(solution)/shard_map/ppermute | solution.py:280
  20.2 4.2 %collective-permute-start.10 = (f32[8,512]{1,0:T(8,128)S(1)}, f32[8,512]{1,0:T(8,128)S(1)}, u32[]{:S(2)}, u32[]{:S(2)}) collective-permute-start(f32[8,512]{1,0:T(8,128)S(1)} %shard_map.103.table), channel_id=1, source_target_pairs={{0,4},{1,5},{2,6},{3,7},{4,0},{5,1},{6,2},{7,3},{8,12},{9,13},{10,... | collective-permute-start | bytes 49160 | tf_op jit(solution)/shard_map/ppermute | solution.py:280
  22.7 5.5 %collective-permute-start.8 = (bf16[64,128]{1,0:T(8,128)(2,1)S(1)}, bf16[64,128]{1,0:T(8,128)(2,1)S(1)}, u32[]{:S(2)}, u32[]{:S(2)}) collective-permute-start(bf16[64,128]{1,0:T(8,128)(2,1)S(1)} %get-tuple-element.52), channel_id=1, source_target_pairs={{0,2},{1,3},{2,0},{3,1},{4,6},{5,7},{6,4},{7,5},{8,10},{9,11},{10,... | collective-permute-start | bytes 49160 | tf_op jit(solution)/shard_map/ppermute | solution.py:273
  24.4 3.8 %collective-permute-start.9 = (bf16[64,128]{1,0:T(8,128)(2,1)S(1)}, bf16[64,128]{1,0:T(8,128)(2,1)S(1)}, u32[]{:S(2)}, u32[]{:S(2)}) collective-permute-start(bf16[64,128]{1,0:T(8,128)(2,1)S(1)} %get-tuple-element.51), channel_id=1, source_target_pairs={{0,3},{1,2},{2,1},{3,0},{4,7},{5,6},{6,5},{7,4},{8,11},{9,10},{10,... | collective-permute-start | bytes 49160 | tf_op jit(solution)/shard_map/ppermute | solution.py:273
  29.7 9.7 %copy-start.6 = (f32[128]{0:T(128)S(1)}, f32[128]{0:T(128)}, u32[]{:S(2)}) copy-start(f32[128]{0:T(128)} %param.19) | copy-start | bytes 1540
  29.7 1.4 %collective-permute-start.14 = (bf16[128,512]{1,0:T(8,128)(2,1)S(1)}, bf16[128,512]{1,0:T(8,128)(2,1)S(1)}, u32[]{:S(2)}, u32[]{:S(2)}) collective-permute-start(bf16[128,512]{1,0:T(8,128)(2,1)S(1)} %shard_map.108), channel_id=1, source_target_pairs={{0,1},{1,0},{2,3},{3,2},{4,5},{5,4},{6,7},{7,6},{8,9},{9,8},{10,11... | collective-permute-start | bytes 393224 | tf_op jit(solution)/shard_map/ppermute | solution.py:273
  31.2 6.4 %collective-permute-start.15 = (bf16[128,512]{1,0:T(8,128)(2,1)S(1)}, bf16[128,512]{1,0:T(8,128)(2,1)S(1)}, u32[]{:S(2)}, u32[]{:S(2)}) collective-permute-start(bf16[128,512]{1,0:T(8,128)(2,1)S(1)} %shard_map.109.a), channel_id=1, source_target_pairs={{0,2},{1,7},{2,0},{3,5},{4,6},{5,3},{6,4},{7,1},{8,10},{9,15},{10,... | collective-permute-start | bytes 393224 | tf_op jit(solution)/shard_map/ppermute | solution.py:394
  32.0 5.6 %collective-permute-start.16 = (bf16[128,512]{1,0:T(8,128)(2,1)S(1)}, bf16[128,512]{1,0:T(8,128)(2,1)S(1)}, u32[]{:S(2)}, u32[]{:S(2)}) collective-permute-start(bf16[128,512]{1,0:T(8,128)(2,1)S(1)} %shard_map.109.a), channel_id=1, source_target_pairs={{1,5},{3,7},{5,1},{7,3},{9,13},{11,15},{13,9},{15,11},{17,21},{19,... | collective-permute-start | bytes 393224 | tf_op jit(solution)/shard_map/ppermute | solution.py:395
  37.7 2.7 %collective-permute-start.17 = (bf16[128,512]{1,0:T(8,128)(2,1)S(1)}, bf16[128,512]{1,0:T(8,128)(2,1)S(1)}, u32[]{:S(2)}, u32[]{:S(2)}) collective-permute-start(bf16[128,512]{1,0:T(8,128)(2,1)S(1)} %shard_map.110.refs_0_), channel_id=1, source_target_pairs={{0,1},{1,0},{2,3},{3,2},{4,5},{5,4},{6,7},{7,6},{8,9},{9,8},{10,11... | collective-permute-start | bytes 393224 | tf_op jit(solution)/shard_map/ppermute | solution.py:273
  39.4 1.3 %collective-permute-start.18 = (bf16[128,512]{1,0:T(8,128)(2,1)S(1)}, bf16[128,512]{1,0:T(8,128)(2,1)S(1)}, u32[]{:S(2)}, u32[]{:S(2)}) collective-permute-start(bf16[128,512]{1,0:T(8,128)(2,1)S(1)} %collective-permute-done.15.refs_2_), channel_id=1, source_target_pairs={{0,1},{1,0},{2,3},{3,2},{4,5},{5,4},{6,7},{7,6},{8,9},{9,8},{10,11... | collective-permute-start | bytes 393224 | tf_op jit(solution)/shard_map/ppermute | solution.py:273

commit v5 on v4

--- a/solution.py
+++ b/solution.py
@@ -13,23 +13,18 @@
 TILES = 8
 
 
-def call(kernel, outs, *args, scratch=(), flops=0, left=(), limit=VMEM_LIMIT, touched=None):
+def call(kernel, outs, *args, scratch=(), flops=0, touched=None):
     vmem = pl.BlockSpec(memory_space=pltpu.VMEM)
-    specs = [
-        pl.BlockSpec(memory_space=pltpu.SMEM) if a.ndim == 1 else vmem for a in args
-    ]
-    for n in left:
-        specs[n] = pl.BlockSpec(memory_space=pl.ANY)
     if touched is None:
         touched = sum(a.size * a.dtype.itemsize for a in args)
         touched += sum(o.size * o.dtype.itemsize for o in outs)
     return pl.pallas_call(
         kernel,
         out_shape=tuple(outs),
-        in_specs=specs,
+        in_specs=[vmem] * len(args),
         out_specs=tuple(vmem for _ in outs),
         scratch_shapes=list(scratch),
-        compiler_params=pltpu.CompilerParams(vmem_limit_bytes=limit),
+        compiler_params=pltpu.CompilerParams(vmem_limit_bytes=VMEM_LIMIT),
         cost_estimate=pl.CostEstimate(flops=flops, bytes_accessed=touched, transcendentals=0),
     )(*args)
 
@@ -350,8 +345,6 @@
         for f in range(n_ch):
             part = lax.dynamic_slice_in_dim(expand_weight, (ch ^ f) * outs, outs, 1)
             slices.append(swap(part, f) if f else part)
-            if f == 1:
-                expand_weight, slices[1] = lax.optimization_barrier((expand_weight, slices[1]))
         return slices
 
     if direct:
@@ -361,6 +354,7 @@
         held = [mine]
         for m in range(1, turns):
             held.append(joint(mine, lambda a, k, m=m: (a + 2 * m) % n_az))
+        expand_weight, partner_table = lax.optimization_barrier((expand_weight, partner_table))
         samplings = []
         for entries in (table, partner_table):
             (sampling,) = call(
@@ -370,7 +364,6 @@
                 touched=0,
             )
             samplings.append(sampling)
-        expand_weight, mine = lax.optimization_barrier((expand_weight, mine))
         slices = expansion_slices(expand_weight)
         held[0], slices = lax.optimization_barrier((held[0], slices))
         tile = shape((2 * share, cells), BF16)

time: 41.8 us -> 41.5 us (level)
    ppermute x12, waiting for transfers between devices: 3.41 us -> 5.93 us  [swap(): return lax.ppermute(x, 'ch', [(i, i ^ mask) for i in range(n_ch)])]
    ppermute x5, waiting for transfers between devices: 4.57 us -> 2.43 us  [joint(): return lax.ppermute(x, ('az', 'ch'), pairs)]
    ppermute x12, starting transfers between devices: 8.85 us -> 8.17 us  [swap(): return lax.ppermute(x, 'ch', [(i, i ^ mask) for i in range(n_ch)])]
    ppermute x1, starting transfers between devices: 0.85 us -> 1.49 us  [local(): far = lax.ppermute(kept, ('az', 'ch'), other_plane)]
    ppermute x1, waiting for transfers between devices: 4.92 us -> 4.28 us  [local(): far = lax.ppermute(kept, ('az', 'ch'), other_plane)]
  transfers between devices with their start and end apart: 19 -> 19, of which waited for: 9 -> 8; matrix products, arithmetic and copies ran while one was open for 3% -> 3% of each run, Pallas kernels for 13% -> 13%
where the time goes in v5:
time: 41.5 us; the launch traced here: 41.4 us
  starting transfers between devices  18.5 us (45%)
  waiting for transfers between devices  12.6 us (30%)
  Pallas kernels  8.5 us (20%)
  local copies, waits for them, and re-layouts  1.32 us (3%)
    pallas_call x12, Pallas kernels, call(): pl.pallas_call(kernel, out_shape=tuple(outs), in_specs=[vmem] * len(args)...  8.5 us
    ppermute x5, starting transfers between devices, joint(): return lax.ppermute(x, ('az', 'ch'), pairs)  8.21 us
    ppermute x12, starting transfers between devices, swap(): return lax.ppermute(x, 'ch', [(i, i ^ mask) for i in range(n_ch)])  8.17 us
    ppermute x12, waiting for transfers between devices, swap(): return lax.ppermute(x, 'ch', [(i, i ^ mask) for i in range(n_ch)])  5.93 us
    ppermute x1, waiting for transfers between devices, local(): far = lax.ppermute(kept, ('az', 'ch'), other_plane)  4.28 us
    ppermute x5, waiting for transfers between devices, joint(): return lax.ppermute(x, ('az', 'ch'), pairs)  2.43 us
    ppermute x1, starting transfers between devices, local(): far = lax.ppermute(kept, ('az', 'ch'), other_plane)  1.49 us
    unnamed x19, local copies, waits for them, and re-layouts  1.19 us
  transfers between devices with their start and end apart: 19, of which 8 were waited for; matrix products, arithmetic and copies ran while one was open for 3% of the time, Pallas kernels for 13%

profile of v5, /device:TPU:0, one launch (start us, length us, event | category | flops | bytes accessed | tf_op | source)
XLA Modules:
  0.0 41.4 jit_solution(14143442918933434070)
XLA Ops:
  0.0 3.0 %collective-permute-start.3 = (bf16[3,3,64,256]{3,2,1,0:T(8,128)(2,1)}, bf16[3,3,64,256]{3,2,1,0:T(8,128)(2,1)S(1)}, u32[]{:S(2)}, u32[]{:S(2)}) collective-permute-start(bf16[3,3,64,256]{3,2,1,0:T(8,128)(2,1)} %bitcast.10), channel_id=1, source_target_pairs={{0,2},{1,3},{2,0},{3,1},{4,6},{5,7},{6,4},{7,5},{8,10},{9,11},{10,... | collective-permute-start | bytes 884744 | tf_op jit(solution)/shard_map/ppermute | solution.py:268
  3.0 1.1 %copy.12 = bf16[32,8,4,256]{3,1,2,0:T(8,128)(2,1)S(1)} copy(bf16[32,8,4,256]{3,2,1,0:T(4,128)(2,1)} %bitcast.15) | data formatting | bytes 1048576
  4.1 0.0 copy-start.7
  4.1 0.0 copy-start.8
  4.1 0.0 copy-start
  4.1 0.0 copy-start.1
  4.2 0.0 copy-start.5
  4.2 0.0 copy-start.2
  4.2 0.0 copy-start.3
  4.2 1.5 %collective-permute-start = (bf16[256,512]{1,0:T(8,128)(2,1)S(1)}, bf16[256,512]{1,0:T(8,128)(2,1)S(1)}, u32[]{:S(2)}, u32[]{:S(2)}) collective-permute-start(bf16[256,512]{1,0:T(8,128)(2,1)S(1)} %shard_map.100), channel_id=1, source_target_pairs={{0,4},{1,29},{2,6},{3,31},{4,8},{5,1},{6,10},{7,3},{8,12},{9,5},{1... | collective-permute-start | bytes 786440 | tf_op jit(solution)/shard_map/ppermute | solution.py:275
  5.8 0.1 maximum_bitcast_fusion
  5.9 0.5 %collective-permute-start.4 = (f32[1,128]{1,0:T(1,128)S(1)}, f32[1,128]{1,0:T(1,128)S(1)}, u32[]{:S(2)}, u32[]{:S(2)}) collective-permute-start(f32[1,128]{1,0:T(1,128)S(1)} %maximum_bitcast_fusion), channel_id=1, source_target_pairs={{0,2},{1,3},{2,0},{3,1},{4,6},{5,7},{6,4},{7,5},{8,10},{9,11},{10,... | collective-permute-start | bytes 1544 | tf_op jit(solution)/shard_map/ppermute | solution.py:268
  6.4 2.0 %collective-permute-start.1 = (bf16[3,3,64,256]{3,2,1,0:T(8,128)(2,1)S(1)}, bf16[3,3,64,256]{3,2,1,0:T(8,128)(2,1)S(1)}, u32[]{:S(2)}, u32[]{:S(2)}) collective-permute-start(bf16[3,3,64,256]{3,2,1,0:T(8,128)(2,1)S(1)} %bitcast.11), channel_id=1, source_target_pairs={{0,1},{1,0},{2,3},{3,2},{4,5},{5,4},{6,7},{7,6},{8,9},{9,8},{10,11... | collective-permute-start | bytes 884744 | tf_op jit(solution)/shard_map/ppermute | solution.py:268
  8.4 0.1 collective-permute-start.2
  8.5 0.3 shard_map.103.table
  8.8 1.4 %collective-permute-done.3.w1c = bf16[3,3,64,256]{3,2,1,0:T(8,128)(2,1)S(1)} collective-permute-done((bf16[3,3,64,256]{3,2,1,0:T(8,128)(2,1)}, bf16[3,3,64,256]{3,2,1,0:T(8,128)(2,1)S(1)}, u32[]{:S(2)}, u32[]{:S(2)}) %collective-permute-start.3) | collective-permute-done | bytes 294944 | tf_op jit(solution)/shard_map/ppermute | solution.py:268
  10.2 0.1 collective-permute-done.4
  10.3 0.6 %collective-permute-start.6 = (f32[2,128]{1,0:T(2,128)S(1)}, f32[2,128]{1,0:T(2,128)S(1)}, u32[]{:S(2)}, u32[]{:S(2)}) collective-permute-start(f32[2,128]{1,0:T(2,128)S(1)} %pad_maximum_fusion.bias), channel_id=1, source_target_pairs={{0,1},{1,0},{2,3},{3,2},{4,5},{5,4},{6,7},{7,6},{8,9},{9,8},{10,11... | collective-permute-start | bytes 3080 | tf_op jit(solution)/shard_map/ppermute | solution.py:268
  10.9 0.1 collective-permute-start.5
  10.9 2.4 %collective-permute-done.wide = bf16[256,512]{1,0:T(8,128)(2,1)S(1)} collective-permute-done((bf16[256,512]{1,0:T(8,128)(2,1)S(1)}, bf16[256,512]{1,0:T(8,128)(2,1)S(1)}, u32[]{:S(2)}, u32[]{:S(2)}) %collective-permute-start) | collective-permute-done | bytes 262176 | tf_op jit(solution)/shard_map/ppermute | solution.py:275
  13.4 0.6 %shard_map.102 = (bf16[384,768]{1,0:T(8,128)(2,1)S(1)}, bf16[384,768]{1,0:T(8,128)(2,1)S(1)}, f32[2,128,256]{2,1,0:T(8,128)S(1)}) custom-call(bf16[256,1024]{1,0:T(8,128)(2,1)S(1)} %bitcast.8, bf16[3,3,64,256]{3,2,1,0:T(8,128)(2,1)S(1)} %bitcast.12, bf16[3,3,64,256]{3,2,1,0:T(8,128)(2,1)S(1)} %collective-permute-done.1.w1b, ...), custom_call_target="tpu_custom_call" | custom-call | bytes 3145728 | tf_op jit(solution)/shard_map/pallas_call | solution.py:21
  14.0 0.0 collective-permute-done.5.w1d
  14.0 0.0 copy-start.4
  14.1 1.9 %shard_map.104.refs_2_ = bf16[128,512]{1,0:T(8,128)(2,1)S(1)} custom-call(bf16[256,1024]{1,0:T(8,128)(2,1)S(1)} %bitcast.9, bf16[512,256]{1,0:T(8,128)(2,1)S(1)} %shard_map.101.halo, bf16[384,768]{1,0:T(8,128)(2,1)S(1)} %get-tuple-element.29.near, bf16[384,768]{1,0:T(8,128)(2,1)S(1)} %get-tuple-element.30.w2s, f32[2,128,256]{2,1,0:T(8,128)S(1)} %get-tuple-element.31.inner, ...), custom_call_target="tpu_custom_call" | custom-call | flops 1207959552 | bytes 2951168 | tf_op jit(solution)/shard_map/pallas_call | solution.py:21
  15.9 1.2 %collective-permute-start.7 = (f32[8,512]{1,0:T(8,128)S(1)}, f32[8,512]{1,0:T(8,128)S(1)}, u32[]{:S(2)}, u32[]{:S(2)}) collective-permute-start(f32[8,512]{1,0:T(8,128)S(1)} %shard_map.103.table), channel_id=1, source_target_pairs={{0,4},{1,5},{2,6},{3,7},{4,0},{5,1},{6,2},{7,3},{8,12},{9,13},{10,... | collective-permute-start | bytes 49160 | tf_op jit(solution)/shard_map/ppermute | solution.py:275
  17.1 1.6 %collective-permute-start.11 = (bf16[128,512]{1,0:T(8,128)(2,1)S(1)}, bf16[128,512]{1,0:T(8,128)(2,1)S(1)}, u32[]{:S(2)}, u32[]{:S(2)}) collective-permute-start(bf16[128,512]{1,0:T(8,128)(2,1)S(1)} %shard_map.104.refs_2_), channel_id=1, source_target_pairs={{0,8},{1,9},{2,10},{3,11},{4,12},{5,13},{6,14},{7,15},{8,16},{9,17... | collective-permute-start | bytes 393224 | tf_op jit(solution)/shard_map/ppermute | solution.py:275
  18.7 3.1 %collective-permute-start.12 = (bf16[128,512]{1,0:T(8,128)(2,1)S(1)}, bf16[128,512]{1,0:T(8,128)(2,1)S(1)}, u32[]{:S(2)}, u32[]{:S(2)}) collective-permute-start(bf16[128,512]{1,0:T(8,128)(2,1)S(1)} %shard_map.104.refs_2_), channel_id=1, source_target_pairs={{0,16},{1,17},{2,18},{3,19},{4,20},{5,21},{6,22},{7,23},{8,24},{9,... | collective-permute-start | bytes 393224 | tf_op jit(solution)/shard_map/ppermute | solution.py:275
  21.8 0.8 %collective-permute-start.13 = (bf16[128,512]{1,0:T(8,128)(2,1)S(1)}, bf16[128,512]{1,0:T(8,128)(2,1)S(1)}, u32[]{:S(2)}, u32[]{:S(2)}) collective-permute-start(bf16[128,512]{1,0:T(8,128)(2,1)S(1)} %shard_map.104.refs_2_), channel_id=1, source_target_pairs={{0,24},{1,25},{2,26},{3,27},{4,28},{5,29},{6,30},{7,31},{8,0},{9,1... | collective-permute-start | bytes 393224 | tf_op jit(solution)/shard_map/ppermute | solution.py:275
  22.6 0.1 collective-permute-start.10
  22.7 0.6 %collective-permute-start.8 = (bf16[64,128]{1,0:T(8,128)(2,1)S(1)}, bf16[64,128]{1,0:T(8,128)(2,1)S(1)}, u32[]{:S(2)}, u32[]{:S(2)}) collective-permute-start(bf16[64,128]{1,0:T(8,128)(2,1)S(1)} %get-tuple-element.51), channel_id=1, source_target_pairs={{0,1},{1,0},{2,3},{3,2},{4,5},{5,4},{6,7},{7,6},{8,9},{9,8},{10,11... | collective-permute-start | bytes 49160 | tf_op jit(solution)/shard_map/ppermute | solution.py:268
  23.3 2.5 %collective-permute-done.10.wd = bf16[64,128]{1,0:T(8,128)(2,1)S(1)} collective-permute-done((bf16[64,128]{1,0:T(8,128)(2,1)S(1)}, bf16[64,128]{1,0:T(8,128)(2,1)S(1)}, u32[]{:S(2)}, u32[]{:S(2)}) %collective-permute-start.10) | collective-permute-done | bytes 16416 | tf_op jit(solution)/shard_map/ppermute | solution.py:268
  25.9 0.6 %collective-permute-start.9 = (bf16[64,128]{1,0:T(8,128)(2,1)S(1)}, bf16[64,128]{1,0:T(8,128)(2,1)S(1)}, u32[]{:S(2)}, u32[]{:S(2)}) collective-permute-start(bf16[64,128]{1,0:T(8,128)(2,1)S(1)} %get-tuple-element.50), channel_id=1, source_target_pairs={{0,2},{1,3},{2,0},{3,1},{4,6},{5,7},{6,4},{7,5},{8,10},{9,11},{10,... | collective-permute-start | bytes 49160 | tf_op jit(solution)/shard_map/ppermute | solution.py:268
  26.4 1.9 %shard_map.105.refs_0_ = bf16[4,512,512]{2,1,0:T(8,128)(2,1)S(1)} custom-call(f32[8,512]{1,0:T(8,128)S(1)} %shard_map.103.table), custom_call_target="tpu_custom_call" | custom-call | tf_op jit(solution)/shard_map/pallas_call | solution.py:21
  28.4 1.9 %shard_map.106.refs_1_ = bf16[4,512,512]{2,1,0:T(8,128)(2,1)S(1)} custom-call(f32[8,512]{1,0:T(8,128)S(1)} %collective-permute-done.7.table), custom_call_target="tpu_custom_call" | custom-call | tf_op jit(solution)/shard_map/pallas_call | solution.py:21
  30.3 0.5 %shard_map.108 = bf16[128,512]{1,0:T(8,128)(2,1)S(1)} custom-call(bf16[4,512,512]{2,1,0:T(8,128)(2,1)S(1)} %shard_map.105.refs_0_, bf16[4,512,512]{2,1,0:T(8,128)(2,1)S(1)} %shard_map.106.refs_1_, bf16[128,512]{1,0:T(8,128)(2,1)S(1)} %shard_map.104.refs_2_, bf16[128,512]{1,0:T(8,128)(2,1)S(1)} %collective-permute-done.11.refs_3_, ...), custom_call_target="tpu_custom_call" | custom-call | flops 268435456 | bytes 4849664 | tf_op jit(solution)/shard_map/pallas_call | solution.py:21
  30.8 0.0 copy-start.6
  30.8 0.1 collective-permute-start.14
  30.9 0.5 %shard_map.107.a = bf16[128,512]{1,0:T(8,128)(2,1)S(1)} custom-call(bf16[4,512,512]{2,1,0:T(8,128)(2,1)S(1)} %shard_map.105.refs_0_, bf16[4,512,512]{2,1,0:T(8,128)(2,1)S(1)} %shard_map.106.refs_1_, bf16[128,512]{1,0:T(8,128)(2,1)S(1)} %shard_map.104.refs_2_, bf16[128,512]{1,0:T(8,128)(2,1)S(1)} %collective-permute-done.11.refs_3_, ...), custom_call_target="tpu_custom_call" | custom-call | flops 268435456 | bytes 4849664 | tf_op jit(solution)/shard_map/pallas_call | solution.py:21
  31.3 0.9 %collective-permute-done.14.b = bf16[128,512]{1,0:T(8,128)(2,1)S(1)} collective-permute-done((bf16[128,512]{1,0:T(8,128)(2,1)S(1)}, bf16[128,512]{1,0:T(8,128)(2,1)S(1)}, u32[]{:S(2)}, u32[]{:S(2)}) %collective-permute-start.14) | collective-permute-done | bytes 131104 | tf_op jit(solution)/shard_map/ppermute | solution.py:268
  32.2 1.5 %collective-permute-start.15 = (bf16[128,512]{1,0:T(8,128)(2,1)S(1)}, bf16[128,512]{1,0:T(8,128)(2,1)S(1)}, u32[]{:S(2)}, u32[]{:S(2)}) collective-permute-start(bf16[128,512]{1,0:T(8,128)(2,1)S(1)} %shard_map.109.a), channel_id=1, source_target_pairs={{0,2},{1,7},{2,0},{3,5},{4,6},{5,3},{6,4},{7,1},{8,10},{9,15},{10,... | collective-permute-start | bytes 393224 | tf_op jit(solution)/shard_map/ppermute | solution.py:387
  33.7 0.7 %collective-permute-start.16 = (bf16[128,512]{1,0:T(8,128)(2,1)S(1)}, bf16[128,512]{1,0:T(8,128)(2,1)S(1)}, u32[]{:S(2)}, u32[]{:S(2)}) collective-permute-start(bf16[128,512]{1,0:T(8,128)(2,1)S(1)} %shard_map.109.a), channel_id=1, source_target_pairs={{1,5},{3,7},{5,1},{7,3},{9,13},{11,15},{13,9},{15,11},{17,21},{19,... | collective-permute-start | bytes 393224 | tf_op jit(solution)/shard_map/ppermute | solution.py:388
  34.4 4.3 %collective-permute-done.15.refs_2_ = bf16[128,512]{1,0:T(8,128)(2,1)S(1)} collective-permute-done((bf16[128,512]{1,0:T(8,128)(2,1)S(1)}, bf16[128,512]{1,0:T(8,128)(2,1)S(1)}, u32[]{:S(2)}, u32[]{:S(2)}) %collective-permute-start.15) | collective-permute-done | bytes 131104 | tf_op jit(solution)/shard_map/ppermute | solution.py:387
  38.7 0.4 collective-permute-start.17
  39.1 0.2 collective-permute-start.18
  39.3 0.1 copy.11.bias
  39.4 0.7 %collective-permute-done.17.refs_1_ = bf16[128,512]{1,0:T(8,128)(2,1)S(1)} collective-permute-done((bf16[128,512]{1,0:T(8,128)(2,1)S(1)}, bf16[128,512]{1,0:T(8,128)(2,1)S(1)}, u32[]{:S(2)}, u32[]{:S(2)}) %collective-permute-start.17) | collective-permute-done | bytes 131104 | tf_op jit(solution)/shard_map/ppermute | solution.py:268
  40.1 0.3 collective-permute-done.18.refs_3_
  40.5 0.9 %shard_map.111 = bf16[128,512]{1,0:T(8,128)(2,1)} custom-call(bf16[64,128]{1,0:T(8,128)(2,1)S(1)} %get-tuple-element.41.wa, bf16[64,128]{1,0:T(8,128)(2,1)S(1)} %collective-permute-done.8.wb, bf16[64,128]{1,0:T(8,128)(2,1)S(1)} %collective-permute-done.9.wc, bf16[64,128]{1,0:T(8,128)(2,1)S(1)} %collective-permute-done.10.wd, f32[128,1]{1,0:T(8,128)S(1)} %copy.11.bias, ...), custom_call_target="tpu_custom_call" | custom-call | flops 67108864 | bytes 721408 | tf_op jit(solution)/shard_map/pallas_call | solution.py:21
  (26 shorter events, 0.2 us)
Async XLA Ops:
  0.0 10.2 %collective-permute-start.3 = (bf16[3,3,64,256]{3,2,1,0:T(8,128)(2,1)}, bf16[3,3,64,256]{3,2,1,0:T(8,128)(2,1)S(1)}, u32[]{:S(2)}, u32[]{:S(2)}) collective-permute-start(bf16[3,3,64,256]{3,2,1,0:T(8,128)(2,1)} %bitcast.10), channel_id=1, source_target_pairs={{0,2},{1,3},{2,0},{3,1},{4,6},{5,7},{6,4},{7,5},{8,10},{9,11},{10,... | collective-permute-start | bytes 884744 | tf_op jit(solution)/shard_map/ppermute | solution.py:268
  4.1 1.7 %copy-start.7 = (f32[64]{0:T(128)S(1)}, f32[64]{0:T(128)}, u32[]{:S(2)}) copy-start(f32[64]{0:T(128)} %param.14) | copy-start | bytes 772
  4.1 1.7 %copy-start.8 = (f32[64]{0:T(128)S(1)}, f32[64]{0:T(128)}, u32[]{:S(2)}) copy-start(f32[64]{0:T(128)} %param.12) | copy-start | bytes 772
  4.1 2.2 %copy-start = (bf16[64,3,3,256]{3,0,2,1:T(8,128)(2,1)S(1)}, bf16[64,3,3,256]{3,0,2,1:T(8,128)(2,1)}, u32[]{:S(2)}) copy-start(bf16[64,3,3,256]{3,0,2,1:T(8,128)(2,1)} %param.11) | copy-start | bytes 884740
  4.1 4.3 %copy-start.1 = (bf16[64,3,3,256]{3,0,2,1:T(8,128)(2,1)S(1)}, bf16[64,3,3,256]{3,0,2,1:T(8,128)(2,1)}, u32[]{:S(2)}) copy-start(bf16[64,3,3,256]{3,0,2,1:T(8,128)(2,1)} %param.13) | copy-start | bytes 884740
  4.2 4.3 %copy-start.5 = (s32[4096]{0:T(1024)S(1)}, s32[4096]{0:T(1024)}, u32[]{:S(2)}) copy-start(s32[4096]{0:T(1024)} %param.15) | copy-start | bytes 49156
  4.2 4.3 %copy-start.2 = (s32[4,512]{1,0:T(4,128)S(1)}, s32[4,512]{1,0:T(4,128)}, u32[]{:S(2)}) copy-start(s32[4,512]{1,0:T(4,128)} %slot.1) | copy-start | bytes 24580
  4.2 4.3 %copy-start.3 = (f32[2,512]{1,0:T(2,128)S(1)}, f32[2,512]{1,0:T(2,128)}, u32[]{:S(2)}) copy-start(f32[2,512]{1,0:T(2,128)} %frac.1) | copy-start | bytes 12292
  4.2 9.1 %collective-permute-start = (bf16[256,512]{1,0:T(8,128)(2,1)S(1)}, bf16[256,512]{1,0:T(8,128)(2,1)S(1)}, u32[]{:S(2)}, u32[]{:S(2)}) collective-permute-start(bf16[256,512]{1,0:T(8,128)(2,1)S(1)} %shard_map.100), channel_id=1, source_target_pairs={{0,4},{1,29},{2,6},{3,31},{4,8},{5,1},{6,10},{7,3},{8,12},{9,5},{1... | collective-permute-start | bytes 786440 | tf_op jit(solution)/shard_map/ppermute | solution.py:275
  5.9 4.4 %collective-permute-start.4 = (f32[1,128]{1,0:T(1,128)S(1)}, f32[1,128]{1,0:T(1,128)S(1)}, u32[]{:S(2)}, u32[]{:S(2)}) collective-permute-start(f32[1,128]{1,0:T(1,128)S(1)} %maximum_bitcast_fusion), channel_id=1, source_target_pairs={{0,2},{1,3},{2,0},{3,1},{4,6},{5,7},{6,4},{7,5},{8,10},{9,11},{10,... | collective-permute-start | bytes 1544 | tf_op jit(solution)/shard_map/ppermute | solution.py:268
  6.4 7.0 %collective-permute-start.1 = (bf16[3,3,64,256]{3,2,1,0:T(8,128)(2,1)S(1)}, bf16[3,3,64,256]{3,2,1,0:T(8,128)(2,1)S(1)}, u32[]{:S(2)}, u32[]{:S(2)}) collective-permute-start(bf16[3,3,64,256]{3,2,1,0:T(8,128)(2,1)S(1)} %bitcast.11), channel_id=1, source_target_pairs={{0,1},{1,0},{2,3},{3,2},{4,5},{5,4},{6,7},{7,6},{8,9},{9,8},{10,11... | collective-permute-start | bytes 884744 | tf_op jit(solution)/shard_map/ppermute | solution.py:268
  8.4 5.0 %collective-permute-start.2 = (bf16[3,3,64,256]{3,2,1,0:T(8,128)(2,1)S(1)}, bf16[3,3,64,256]{3,2,1,0:T(8,128)(2,1)S(1)}, u32[]{:S(2)}, u32[]{:S(2)}) collective-permute-start(bf16[3,3,64,256]{3,2,1,0:T(8,128)(2,1)S(1)} %bitcast.13), channel_id=1, source_target_pairs={{0,1},{1,0},{2,3},{3,2},{4,5},{5,4},{6,7},{7,6},{8,9},{9,8},{10,11... | collective-permute-start | bytes 884744 | tf_op jit(solution)/shard_map/ppermute | solution.py:268
  10.3 3.8 %collective-permute-start.6 = (f32[2,128]{1,0:T(2,128)S(1)}, f32[2,128]{1,0:T(2,128)S(1)}, u32[]{:S(2)}, u32[]{:S(2)}) collective-permute-start(f32[2,128]{1,0:T(2,128)S(1)} %pad_maximum_fusion.bias), channel_id=1, source_target_pairs={{0,1},{1,0},{2,3},{3,2},{4,5},{5,4},{6,7},{7,6},{8,9},{9,8},{10,11... | collective-permute-start | bytes 3080 | tf_op jit(solution)/shard_map/ppermute | solution.py:268
  10.9 3.2 %collective-permute-start.5 = (bf16[3,3,64,256]{3,2,1,0:T(8,128)(2,1)S(1)}, bf16[3,3,64,256]{3,2,1,0:T(8,128)(2,1)S(1)}, u32[]{:S(2)}, u32[]{:S(2)}) collective-permute-start(bf16[3,3,64,256]{3,2,1,0:T(8,128)(2,1)S(1)} %collective-permute-done.3.w1c), channel_id=1, source_target_pairs={{0,1},{1,0},{2,3},{3,2},{4,5},{5,4},{6,7},{7,6},{8,9},{9,8},{10,11... | collective-permute-start | bytes 884744 | tf_op jit(solution)/shard_map/ppermute | solution.py:268
  14.0 8.6 %copy-start.4 = (bf16[64,512]{1,0:T(8,128)(2,1)S(1)}, bf16[64,512]{1,0:T(8,128)(2,1)}, u32[]{:S(2)}) copy-start(bf16[64,512]{1,0:T(8,128)(2,1)} %param.18) | copy-start | bytes 196612
  15.9 6.7 %collective-permute-start.7 = (f32[8,512]{1,0:T(8,128)S(1)}, f32[8,512]{1,0:T(8,128)S(1)}, u32[]{:S(2)}, u32[]{:S(2)}) collective-permute-start(f32[8,512]{1,0:T(8,128)S(1)} %shard_map.103.table), channel_id=1, source_target_pairs={{0,4},{1,5},{2,6},{3,7},{4,0},{5,1},{6,2},{7,3},{8,12},{9,13},{10,... | collective-permute-start | bytes 49160 | tf_op jit(solution)/shard_map/ppermute | solution.py:275
  17.1 13.2 %collective-permute-start.11 = (bf16[128,512]{1,0:T(8,128)(2,1)S(1)}, bf16[128,512]{1,0:T(8,128)(2,1)S(1)}, u32[]{:S(2)}, u32[]{:S(2)}) collective-permute-start(bf16[128,512]{1,0:T(8,128)(2,1)S(1)} %shard_map.104.refs_2_), channel_id=1, source_target_pairs={{0,8},{1,9},{2,10},{3,11},{4,12},{5,13},{6,14},{7,15},{8,16},{9,17... | collective-permute-start | bytes 393224 | tf_op jit(solution)/shard_map/ppermute | solution.py:275
  18.7 11.6 %collective-permute-start.12 = (bf16[128,512]{1,0:T(8,128)(2,1)S(1)}, bf16[128,512]{1,0:T(8,128)(2,1)S(1)}, u32[]{:S(2)}, u32[]{:S(2)}) collective-permute-start(bf16[128,512]{1,0:T(8,128)(2,1)S(1)} %shard_map.104.refs_2_), channel_id=1, source_target_pairs={{0,16},{1,17},{2,18},{3,19},{4,20},{5,21},{6,22},{7,23},{8,24},{9,... | collective-permute-start | bytes 393224 | tf_op jit(solution)/shard_map/ppermute | solution.py:275
  21.8 8.5 %collective-permute-start.13 = (bf16[128,512]{1,0:T(8,128)(2,1)S(1)}, bf16[128,512]{1,0:T(8,128)(2,1)S(1)}, u32[]{:S(2)}, u32[]{:S(2)}) collective-permute-start(bf16[128,512]{1,0:T(8,128)(2,1)S(1)} %shard_map.104.refs_2_), channel_id=1, source_target_pairs={{0,24},{1,25},{2,26},{3,27},{4,28},{5,29},{6,30},{7,31},{8,0},{9,1... | collective-permute-start | bytes 393224 | tf_op jit(solution)/shard_map/ppermute | solution.py:275
  22.6 3.2 %collective-permute-start.10 = (bf16[64,128]{1,0:T(8,128)(2,1)S(1)}, bf16[64,128]{1,0:T(8,128)(2,1)S(1)}, u32[]{:S(2)}, u32[]{:S(2)}) collective-permute-start(bf16[64,128]{1,0:T(8,128)(2,1)S(1)} %get-tuple-element.49), channel_id=1, source_target_pairs={{0,3},{1,2},{2,1},{3,0},{4,7},{5,6},{6,5},{7,4},{8,11},{9,10},{10,... | collective-permute-start | bytes 49160 | tf_op jit(solution)/shard_map/ppermute | solution.py:268
  22.7 7.6 %collective-permute-start.8 = (bf16[64,128]{1,0:T(8,128)(2,1)S(1)}, bf16[64,128]{1,0:T(8,128)(2,1)S(1)}, u32[]{:S(2)}, u32[]{:S(2)}) collective-permute-start(bf16[64,128]{1,0:T(8,128)(2,1)S(1)} %get-tuple-element.51), channel_id=1, source_target_pairs={{0,1},{1,0},{2,3},{3,2},{4,5},{5,4},{6,7},{7,6},{8,9},{9,8},{10,11... | collective-permute-start | bytes 49160 | tf_op jit(solution)/shard_map/ppermute | solution.py:268
  25.9 4.4 %collective-permute-start.9 = (bf16[64,128]{1,0:T(8,128)(2,1)S(1)}, bf16[64,128]{1,0:T(8,128)(2,1)S(1)}, u32[]{:S(2)}, u32[]{:S(2)}) collective-permute-start(bf16[64,128]{1,0:T(8,128)(2,1)S(1)} %get-tuple-element.50), channel_id=1, source_target_pairs={{0,2},{1,3},{2,0},{3,1},{4,6},{5,7},{6,4},{7,5},{8,10},{9,11},{10,... | collective-permute-start | bytes 49160 | tf_op jit(solution)/shard_map/ppermute | solution.py:268
  30.8 8.5 %copy-start.6 = (f32[128]{0:T(128)S(1)}, f32[128]{0:T(128)}, u32[]{:S(2)}) copy-start(f32[128]{0:T(128)} %param.19) | copy-start | bytes 1540
  30.8 1.4 %collective-permute-start.14 = (bf16[128,512]{1,0:T(8,128)(2,1)S(1)}, bf16[128,512]{1,0:T(8,128)(2,1)S(1)}, u32[]{:S(2)}, u32[]{:S(2)}) collective-permute-start(bf16[128,512]{1,0:T(8,128)(2,1)S(1)} %shard_map.108), channel_id=1, source_target_pairs={{0,1},{1,0},{2,3},{3,2},{4,5},{5,4},{6,7},{7,6},{8,9},{9,8},{10,11... | collective-permute-start | bytes 393224 | tf_op jit(solution)/shard_map/ppermute | solution.py:268
  32.2 6.4 %collective-permute-start.15 = (bf16[128,512]{1,0:T(8,128)(2,1)S(1)}, bf16[128,512]{1,0:T(8,128)(2,1)S(1)}, u32[]{:S(2)}, u32[]{:S(2)}) collective-permute-start(bf16[128,512]{1,0:T(8,128)(2,1)S(1)} %shard_map.109.a), channel_id=1, source_target_pairs={{0,2},{1,7},{2,0},{3,5},{4,6},{5,3},{6,4},{7,1},{8,10},{9,15},{10,... | collective-permute-start | bytes 393224 | tf_op jit(solution)/shard_map/ppermute | solution.py:387
  33.7 5.0 %collective-permute-start.16 = (bf16[128,512]{1,0:T(8,128)(2,1)S(1)}, bf16[128,512]{1,0:T(8,128)(2,1)S(1)}, u32[]{:S(2)}, u32[]{:S(2)}) collective-permute-start(bf16[128,512]{1,0:T(8,128)(2,1)S(1)} %shard_map.109.a), channel_id=1, source_target_pairs={{1,5},{3,7},{5,1},{7,3},{9,13},{11,15},{13,9},{15,11},{17,21},{19,... | collective-permute-start | bytes 393224 | tf_op jit(solution)/shard_map/ppermute | solution.py:388
  38.7 1.4 %collective-permute-start.17 = (bf16[128,512]{1,0:T(8,128)(2,1)S(1)}, bf16[128,512]{1,0:T(8,128)(2,1)S(1)}, u32[]{:S(2)}, u32[]{:S(2)}) collective-permute-start(bf16[128,512]{1,0:T(8,128)(2,1)S(1)} %shard_map.110.refs_0_), channel_id=1, source_target_pairs={{0,1},{1,0},{2,3},{3,2},{4,5},{5,4},{6,7},{7,6},{8,9},{9,8},{10,11... | collective-permute-start | bytes 393224 | tf_op jit(solution)/shard_map/ppermute | solution.py:268
  39.1 1.3 %collective-permute-start.18 = (bf16[128,512]{1,0:T(8,128)(2,1)S(1)}, bf16[128,512]{1,0:T(8,128)(2,1)S(1)}, u32[]{:S(2)}, u32[]{:S(2)}) collective-permute-start(bf16[128,512]{1,0:T(8,128)(2,1)S(1)} %collective-permute-done.15.refs_2_), channel_id=1, source_target_pairs={{0,1},{1,0},{2,3},{3,2},{4,5},{5,4},{6,7},{7,6},{8,9},{9,8},{10,11... | collective-permute-start | bytes 393224 | tf_op jit(solution)/shard_map/ppermute | solution.py:268

commit v6 on v5

--- a/solution.py
+++ b/solution.py
@@ -62,17 +62,34 @@
         rows[a * channels : (a + 1) * channels, :] = wide[:, a * length : (a + 1) * length]
 
 
-def prepare_kernel(own, w1a, w1b, w2a, w2b, near, plane, inner, xs):
-    core = lax.rem(lax.axis_index("ch"), 2)
-    share, inputs, length = w1a.shape[2], w1a.shape[3], xs.shape[1]
-    places = [pl.multiple_of((core ^ f) * share, share) for f in range(2)]
-    stack_weights(near, (w1a, w1b), places, inputs)
-    stack_weights(plane, (w2a, w2b), places, w2a.shape[3])
+def own_rows_kernel(own, weight, xs, stack, inner):
+    share, inputs, length = weight.shape[2], weight.shape[3], xs.shape[1]
+    for i in range(3):
+        for j in range(3):
+            stack[j * share : (j + 1) * share, i * inputs : (i + 1) * inputs] = weight[i, j]
     for a in range(own.shape[1] // length):
         xs[a * inputs : (a + 1) * inputs, :] = own[:, a * length : (a + 1) * length]
     for n in range(inner.shape[0]):
-        z = jnp.dot(near[...], xs[n * inputs : (n + 3) * inputs, :], preferred_element_type=F32)
-        inner[n] = range_sum(z, 2 * share)
+        z = jnp.dot(stack[...], xs[n * inputs : (n + 3) * inputs, :], preferred_element_type=F32)
+        inner[n] = range_sum(z, share)
+
+
+def prepare_kernel(xs, own_stack, own_inner, w1b, w2a, w2b, near, plane, inner, stack):
+    core = lax.rem(lax.axis_index("ch"), 2)
+    share, inputs = w1b.shape[2], w1b.shape[3]
+    places = [pl.multiple_of((core ^ f) * share, share) for f in range(2)]
+    stack_weights(plane, (w2a, w2b), places, w2a.shape[3])
+    for i in range(3):
+        for j in range(3):
+            stack[j * share : (j + 1) * share, i * inputs : (i + 1) * inputs] = w1b[i, j]
+    for j in range(3):
+        rows = slice(j * share, (j + 1) * share)
+        for source, place in zip((own_stack, stack), places):
+            near[pl.ds(2 * j * share + place, share), :] = source[rows, :]
+    for n in range(inner.shape[0]):
+        z = jnp.dot(stack[...], xs[n * inputs : (n + 3) * inputs, :], preferred_element_type=F32)
+        inner[n, pl.ds(places[0], share), :] = own_inner[n]
+        inner[n, pl.ds(places[1], share), :] = range_sum(z, share)
 
 
 def conv_kernel(
@@ -296,7 +313,18 @@
             touched=0,
         )
         w1_y, table = lax.optimization_barrier((w1_y, table))
-    w1_y, bias_y = lax.optimization_barrier((w1_y, bias_y))
+    own_rows, own_stack, own_inner = call(
+        own_rows_kernel,
+        [
+            shape((columns * inputs, length), BF16),
+            shape((3 * share, 3 * inputs), BF16),
+            shape((columns - 2, share, length), F32),
+        ],
+        own,
+        w1,
+        touched=0,
+    )
+    w1_y, bias_y, own_inner = lax.optimization_barrier((w1_y, bias_y, own_inner))
     bias = jnp.concatenate([bias, bias_y])
     bias_core = swap(bias, 1)
 
@@ -310,12 +338,13 @@
             shape((3 * 2 * share, 3 * total), BF16),
             shape((columns - 2, 2 * share, length), F32),
         ],
-        own,
-        w1,
+        own_rows,
+        own_stack,
+        own_inner,
         w1_core,
         w2,
         w2_core,
-        scratch=[pltpu.VMEM((columns * inputs, length), BF16)],
+        scratch=[pltpu.VMEM((3 * share, 3 * inputs), BF16)],
     )
     (halo,) = call(rows_kernel, [shape((half * inputs, length), BF16)], halo, flops=10**10)
     (mine,) = call(

time: 41.5 us -> 41.3 us (level)
    ppermute x12, waiting for transfers between devices: 5.93 us -> 5.45 us  [swap(): return lax.ppermute(x, 'ch', [(i, i ^ mask) for i in range(n_ch)])]
    pallas_call x12 -> x13, Pallas kernels: 8.5 us -> 8.76 us  [call(): pl.pallas_call(kernel, out_shape=tuple(outs), in_specs=[vmem] * len(args)...]
where the time goes in v6:
time: 41.3 us; the launch traced here: 41.2 us
  starting transfers between devices  18.5 us (45%)
  waiting for transfers between devices  12.2 us (30%)
  Pallas kernels  8.76 us (21%)
  local copies, waits for them, and re-layouts  1.32 us (3%)
    pallas_call x13, Pallas kernels, call(): pl.pallas_call(kernel, out_shape=tuple(outs), in_specs=[vmem] * len(args)...  8.76 us
    ppermute x5, starting transfers between devices, joint(): return lax.ppermute(x, ('az', 'ch'), pairs)  8.21 us
    ppermute x12, starting transfers between devices, swap(): return lax.ppermute(x, 'ch', [(i, i ^ mask) for i in range(n_ch)])  8.2 us
    ppermute x12, waiting for transfers between devices, swap(): return lax.ppermute(x, 'ch', [(i, i ^ mask) for i in range(n_ch)])  5.45 us
    ppermute x1, waiting for transfers between devices, local(): far = lax.ppermute(kept, ('az', 'ch'), other_plane)  4.29 us
    ppermute x5, waiting for transfers between devices, joint(): return lax.ppermute(x, ('az', 'ch'), pairs)  2.43 us
    ppermute x1, starting transfers between devices, local(): far = lax.ppermute(kept, ('az', 'ch'), other_plane)  1.48 us
    unnamed x19, local copies, waits for them, and re-layouts  1.19 us
  transfers between devices with their start and end apart: 19, of which 8 were waited for; matrix products, arithmetic and copies ran while one was open for 3% of the time, Pallas kernels for 13%

profile of v6, /device:TPU:0, one launch (start us, length us, event | category | flops | bytes accessed | tf_op | source)
XLA Modules:
  0.0 41.2 jit_solution(17026239278431863737)
XLA Ops:
  0.0 3.0 %collective-permute-start.1 = (bf16[3,3,64,256]{3,2,1,0:T(8,128)(2,1)}, bf16[3,3,64,256]{3,2,1,0:T(8,128)(2,1)S(1)}, u32[]{:S(2)}, u32[]{:S(2)}) collective-permute-start(bf16[3,3,64,256]{3,2,1,0:T(8,128)(2,1)} %bitcast.10), channel_id=1, source_target_pairs={{0,2},{1,3},{2,0},{3,1},{4,6},{5,7},{6,4},{7,5},{8,10},{9,11},{10,... | collective-permute-start | bytes 884744 | tf_op jit(solution)/shard_map/ppermute | solution.py:285
  3.0 1.1 %copy.12 = bf16[32,8,4,256]{3,1,2,0:T(8,128)(2,1)S(1)} copy(bf16[32,8,4,256]{3,2,1,0:T(4,128)(2,1)} %bitcast.15) | data formatting | bytes 1048576
  4.1 0.0 copy-start.7
  4.1 0.0 copy-start.8
  4.1 0.0 copy-start
  4.1 0.0 copy-start.1
  4.2 0.0 copy-start.5
  4.2 0.0 copy-start.2
  4.2 0.0 copy-start.3
  4.2 1.5 %collective-permute-start = (bf16[256,512]{1,0:T(8,128)(2,1)S(1)}, bf16[256,512]{1,0:T(8,128)(2,1)S(1)}, u32[]{:S(2)}, u32[]{:S(2)}) collective-permute-start(bf16[256,512]{1,0:T(8,128)(2,1)S(1)} %shard_map.100), channel_id=1, source_target_pairs={{0,4},{1,29},{2,6},{3,31},{4,8},{5,1},{6,10},{7,3},{8,12},{9,5},{1... | collective-permute-start | bytes 786440 | tf_op jit(solution)/shard_map/ppermute | solution.py:292
  5.8 0.1 maximum_bitcast_fusion
  5.9 0.5 %collective-permute-start.2 = (f32[1,128]{1,0:T(1,128)S(1)}, f32[1,128]{1,0:T(1,128)S(1)}, u32[]{:S(2)}, u32[]{:S(2)}) collective-permute-start(f32[1,128]{1,0:T(1,128)S(1)} %maximum_bitcast_fusion), channel_id=1, source_target_pairs={{0,2},{1,3},{2,0},{3,1},{4,6},{5,7},{6,4},{7,5},{8,10},{9,11},{10,... | collective-permute-start | bytes 1544 | tf_op jit(solution)/shard_map/ppermute | solution.py:285
  6.4 2.0 %collective-permute-start.3 = (bf16[3,3,64,256]{3,2,1,0:T(8,128)(2,1)S(1)}, bf16[3,3,64,256]{3,2,1,0:T(8,128)(2,1)S(1)}, u32[]{:S(2)}, u32[]{:S(2)}) collective-permute-start(bf16[3,3,64,256]{3,2,1,0:T(8,128)(2,1)S(1)} %bitcast.11), channel_id=1, source_target_pairs={{0,1},{1,0},{2,3},{3,2},{4,5},{5,4},{6,7},{7,6},{8,9},{9,8},{10,11... | collective-permute-start | bytes 884744 | tf_op jit(solution)/shard_map/ppermute | solution.py:285
  8.4 0.1 collective-permute-start.4
  8.5 0.4 %shard_map.102 = (bf16[1024,256]{1,0:T(8,128)(2,1)S(1)}, bf16[192,768]{1,0:T(8,128)(2,1)S(1)}, f32[2,64,256]{2,1,0:T(8,128)S(1)}) custom-call(bf16[256,1024]{1,0:T(8,128)(2,1)S(1)} %bitcast.8, bf16[3,3,64,256]{3,2,1,0:T(8,128)(2,1)S(1)} %bitcast.12), custom_call_target="tpu_custom_call" | custom-call | tf_op jit(solution)/shard_map/pallas_call | solution.py:21
  9.0 0.3 shard_map.103.table
  9.3 0.9 %collective-permute-done.1.w1c = bf16[3,3,64,256]{3,2,1,0:T(8,128)(2,1)S(1)} collective-permute-done((bf16[3,3,64,256]{3,2,1,0:T(8,128)(2,1)}, bf16[3,3,64,256]{3,2,1,0:T(8,128)(2,1)S(1)}, u32[]{:S(2)}, u32[]{:S(2)}) %collective-permute-start.1) | collective-permute-done | bytes 294944 | tf_op jit(solution)/shard_map/ppermute | solution.py:285
  10.2 0.1 collective-permute-done.2
  10.3 0.6 %collective-permute-start.6 = (f32[2,128]{1,0:T(2,128)S(1)}, f32[2,128]{1,0:T(2,128)S(1)}, u32[]{:S(2)}, u32[]{:S(2)}) collective-permute-start(f32[2,128]{1,0:T(2,128)S(1)} %pad_maximum_fusion.bias), channel_id=1, source_target_pairs={{0,1},{1,0},{2,3},{3,2},{4,5},{5,4},{6,7},{7,6},{8,9},{9,8},{10,11... | collective-permute-start | bytes 3080 | tf_op jit(solution)/shard_map/ppermute | solution.py:285
  10.9 0.1 collective-permute-start.5
  10.9 2.4 %collective-permute-done.wide = bf16[256,512]{1,0:T(8,128)(2,1)S(1)} collective-permute-done((bf16[256,512]{1,0:T(8,128)(2,1)S(1)}, bf16[256,512]{1,0:T(8,128)(2,1)S(1)}, u32[]{:S(2)}, u32[]{:S(2)}) %collective-permute-start) | collective-permute-done | bytes 262176 | tf_op jit(solution)/shard_map/ppermute | solution.py:292
  13.4 0.4 %shard_map.104 = (bf16[384,768]{1,0:T(8,128)(2,1)S(1)}, bf16[384,768]{1,0:T(8,128)(2,1)S(1)}, f32[2,128,256]{2,1,0:T(8,128)S(1)}) custom-call(bf16[1024,256]{1,0:T(8,128)(2,1)S(1)} %get-tuple-element.31.xs, bf16[192,768]{1,0:T(8,128)(2,1)S(1)} %get-tuple-element.32.own_stack, f32[2,64,256]{2,1,0:T(8,128)S(1)} %get-tuple-element.37.own_inner, ...), custom_call_target="tpu_custom_call" | custom-call | bytes 3276800 | tf_op jit(solution)/shard_map/pallas_call | solution.py:21
  13.9 0.0 copy-start.4
  13.9 1.9 %shard_map.105.refs_2_ = bf16[128,512]{1,0:T(8,128)(2,1)S(1)} custom-call(bf16[256,1024]{1,0:T(8,128)(2,1)S(1)} %bitcast.9, bf16[512,256]{1,0:T(8,128)(2,1)S(1)} %shard_map.101.halo, bf16[384,768]{1,0:T(8,128)(2,1)S(1)} %get-tuple-element.40.near, bf16[384,768]{1,0:T(8,128)(2,1)S(1)} %get-tuple-element.41.w2s, f32[2,128,256]{2,1,0:T(8,128)S(1)} %get-tuple-element.42.inner, ...), custom_call_target="tpu_custom_call" | custom-call | flops 1207959552 | bytes 2951168 | tf_op jit(solution)/shard_map/pallas_call | solution.py:21
  15.8 1.1 %collective-permute-start.7 = (f32[8,512]{1,0:T(8,128)S(1)}, f32[8,512]{1,0:T(8,128)S(1)}, u32[]{:S(2)}, u32[]{:S(2)}) collective-permute-start(f32[8,512]{1,0:T(8,128)S(1)} %shard_map.103.table), channel_id=1, source_target_pairs={{0,4},{1,5},{2,6},{3,7},{4,0},{5,1},{6,2},{7,3},{8,12},{9,13},{10,... | collective-permute-start | bytes 49160 | tf_op jit(solution)/shard_map/ppermute | solution.py:292
  16.9 1.6 %collective-permute-start.11 = (bf16[128,512]{1,0:T(8,128)(2,1)S(1)}, bf16[128,512]{1,0:T(8,128)(2,1)S(1)}, u32[]{:S(2)}, u32[]{:S(2)}) collective-permute-start(bf16[128,512]{1,0:T(8,128)(2,1)S(1)} %shard_map.105.refs_2_), channel_id=1, source_target_pairs={{0,8},{1,9},{2,10},{3,11},{4,12},{5,13},{6,14},{7,15},{8,16},{9,17... | collective-permute-start | bytes 393224 | tf_op jit(solution)/shard_map/ppermute | solution.py:292
  18.5 3.1 %collective-permute-start.12 = (bf16[128,512]{1,0:T(8,128)(2,1)S(1)}, bf16[128,512]{1,0:T(8,128)(2,1)S(1)}, u32[]{:S(2)}, u32[]{:S(2)}) collective-permute-start(bf16[128,512]{1,0:T(8,128)(2,1)S(1)} %shard_map.105.refs_2_), channel_id=1, source_target_pairs={{0,16},{1,17},{2,18},{3,19},{4,20},{5,21},{6,22},{7,23},{8,24},{9,... | collective-permute-start | bytes 393224 | tf_op jit(solution)/shard_map/ppermute | solution.py:292
  21.6 0.8 %collective-permute-start.13 = (bf16[128,512]{1,0:T(8,128)(2,1)S(1)}, bf16[128,512]{1,0:T(8,128)(2,1)S(1)}, u32[]{:S(2)}, u32[]{:S(2)}) collective-permute-start(bf16[128,512]{1,0:T(8,128)(2,1)S(1)} %shard_map.105.refs_2_), channel_id=1, source_target_pairs={{0,24},{1,25},{2,26},{3,27},{4,28},{5,29},{6,30},{7,31},{8,0},{9,1... | collective-permute-start | bytes 393224 | tf_op jit(solution)/shard_map/ppermute | solution.py:292
  22.4 0.1 collective-permute-start.10
  22.5 0.6 %collective-permute-start.8 = (bf16[64,128]{1,0:T(8,128)(2,1)S(1)}, bf16[64,128]{1,0:T(8,128)(2,1)S(1)}, u32[]{:S(2)}, u32[]{:S(2)}) collective-permute-start(bf16[64,128]{1,0:T(8,128)(2,1)S(1)} %get-tuple-element.59), channel_id=1, source_target_pairs={{0,1},{1,0},{2,3},{3,2},{4,5},{5,4},{6,7},{7,6},{8,9},{9,8},{10,11... | collective-permute-start | bytes 49160 | tf_op jit(solution)/shard_map/ppermute | solution.py:285
  23.1 2.5 %collective-permute-done.10.wd = bf16[64,128]{1,0:T(8,128)(2,1)S(1)} collective-permute-done((bf16[64,128]{1,0:T(8,128)(2,1)S(1)}, bf16[64,128]{1,0:T(8,128)(2,1)S(1)}, u32[]{:S(2)}, u32[]{:S(2)}) %collective-permute-start.10) | collective-permute-done | bytes 16416 | tf_op jit(solution)/shard_map/ppermute | solution.py:285
  25.7 0.6 %collective-permute-start.9 = (bf16[64,128]{1,0:T(8,128)(2,1)S(1)}, bf16[64,128]{1,0:T(8,128)(2,1)S(1)}, u32[]{:S(2)}, u32[]{:S(2)}) collective-permute-start(bf16[64,128]{1,0:T(8,128)(2,1)S(1)} %get-tuple-element.58), channel_id=1, source_target_pairs={{0,2},{1,3},{2,0},{3,1},{4,6},{5,7},{6,4},{7,5},{8,10},{9,11},{10,... | collective-permute-start | bytes 49160 | tf_op jit(solution)/shard_map/ppermute | solution.py:285
  26.3 1.9 %shard_map.106.refs_0_ = bf16[4,512,512]{2,1,0:T(8,128)(2,1)S(1)} custom-call(f32[8,512]{1,0:T(8,128)S(1)} %shard_map.103.table), custom_call_target="tpu_custom_call" | custom-call | tf_op jit(solution)/shard_map/pallas_call | solution.py:21
  28.2 1.9 %shard_map.107.refs_1_ = bf16[4,512,512]{2,1,0:T(8,128)(2,1)S(1)} custom-call(f32[8,512]{1,0:T(8,128)S(1)} %collective-permute-done.7.table), custom_call_target="tpu_custom_call" | custom-call | tf_op jit(solution)/shard_map/pallas_call | solution.py:21
  30.1 0.5 %shard_map.109 = bf16[128,512]{1,0:T(8,128)(2,1)S(1)} custom-call(bf16[4,512,512]{2,1,0:T(8,128)(2,1)S(1)} %shard_map.106.refs_0_, bf16[4,512,512]{2,1,0:T(8,128)(2,1)S(1)} %shard_map.107.refs_1_, bf16[128,512]{1,0:T(8,128)(2,1)S(1)} %shard_map.105.refs_2_, bf16[128,512]{1,0:T(8,128)(2,1)S(1)} %collective-permute-done.11.refs_3_, ...), custom_call_target="tpu_custom_call" | custom-call | flops 268435456 | bytes 4849664 | tf_op jit(solution)/shard_map/pallas_call | solution.py:21
  30.6 0.0 copy-start.6
  30.6 0.1 collective-permute-start.14
  30.7 0.5 %shard_map.108.a = bf16[128,512]{1,0:T(8,128)(2,1)S(1)} custom-call(bf16[4,512,512]{2,1,0:T(8,128)(2,1)S(1)} %shard_map.106.refs_0_, bf16[4,512,512]{2,1,0:T(8,128)(2,1)S(1)} %shard_map.107.refs_1_, bf16[128,512]{1,0:T(8,128)(2,1)S(1)} %shard_map.105.refs_2_, bf16[128,512]{1,0:T(8,128)(2,1)S(1)} %collective-permute-done.11.refs_3_, ...), custom_call_target="tpu_custom_call" | custom-call | flops 268435456 | bytes 4849664 | tf_op jit(solution)/shard_map/pallas_call | solution.py:21
  31.2 0.9 %collective-permute-done.14.b = bf16[128,512]{1,0:T(8,128)(2,1)S(1)} collective-permute-done((bf16[128,512]{1,0:T(8,128)(2,1)S(1)}, bf16[128,512]{1,0:T(8,128)(2,1)S(1)}, u32[]{:S(2)}, u32[]{:S(2)}) %collective-permute-start.14) | collective-permute-done | bytes 131104 | tf_op jit(solution)/shard_map/ppermute | solution.py:285
  32.1 1.5 %collective-permute-start.15 = (bf16[128,512]{1,0:T(8,128)(2,1)S(1)}, bf16[128,512]{1,0:T(8,128)(2,1)S(1)}, u32[]{:S(2)}, u32[]{:S(2)}) collective-permute-start(bf16[128,512]{1,0:T(8,128)(2,1)S(1)} %shard_map.110.a), channel_id=1, source_target_pairs={{0,2},{1,7},{2,0},{3,5},{4,6},{5,3},{6,4},{7,1},{8,10},{9,15},{10,... | collective-permute-start | bytes 393224 | tf_op jit(solution)/shard_map/ppermute | solution.py:416
  33.6 0.7 %collective-permute-start.16 = (bf16[128,512]{1,0:T(8,128)(2,1)S(1)}, bf16[128,512]{1,0:T(8,128)(2,1)S(1)}, u32[]{:S(2)}, u32[]{:S(2)}) collective-permute-start(bf16[128,512]{1,0:T(8,128)(2,1)S(1)} %shard_map.110.a), channel_id=1, source_target_pairs={{1,5},{3,7},{5,1},{7,3},{9,13},{11,15},{13,9},{15,11},{17,21},{19,... | collective-permute-start | bytes 393224 | tf_op jit(solution)/shard_map/ppermute | solution.py:417
  34.2 4.3 %collective-permute-done.15.refs_2_ = bf16[128,512]{1,0:T(8,128)(2,1)S(1)} collective-permute-done((bf16[128,512]{1,0:T(8,128)(2,1)S(1)}, bf16[128,512]{1,0:T(8,128)(2,1)S(1)}, u32[]{:S(2)}, u32[]{:S(2)}) %collective-permute-start.15) | collective-permute-done | bytes 131104 | tf_op jit(solution)/shard_map/ppermute | solution.py:416
  38.5 0.4 collective-permute-start.17
  38.9 0.2 collective-permute-start.18
  39.1 0.1 copy.11.bias
  39.2 0.7 %collective-permute-done.17.refs_1_ = bf16[128,512]{1,0:T(8,128)(2,1)S(1)} collective-permute-done((bf16[128,512]{1,0:T(8,128)(2,1)S(1)}, bf16[128,512]{1,0:T(8,128)(2,1)S(1)}, u32[]{:S(2)}, u32[]{:S(2)}) %collective-permute-start.17) | collective-permute-done | bytes 131104 | tf_op jit(solution)/shard_map/ppermute | solution.py:285
  40.0 0.3 collective-permute-done.18.refs_3_
  40.3 0.9 %shard_map.112 = bf16[128,512]{1,0:T(8,128)(2,1)} custom-call(bf16[64,128]{1,0:T(8,128)(2,1)S(1)} %get-tuple-element.49.wa, bf16[64,128]{1,0:T(8,128)(2,1)S(1)} %collective-permute-done.8.wb, bf16[64,128]{1,0:T(8,128)(2,1)S(1)} %collective-permute-done.9.wc, bf16[64,128]{1,0:T(8,128)(2,1)S(1)} %collective-permute-done.10.wd, f32[128,1]{1,0:T(8,128)S(1)} %copy.11.bias, ...), custom_call_target="tpu_custom_call" | custom-call | flops 67108864 | bytes 721408 | tf_op jit(solution)/shard_map/pallas_call | solution.py:21
  (27 shorter events, 0.2 us)
Async XLA Ops:
  0.0 10.2 %collective-permute-start.1 = (bf16[3,3,64,256]{3,2,1,0:T(8,128)(2,1)}, bf16[3,3,64,256]{3,2,1,0:T(8,128)(2,1)S(1)}, u32[]{:S(2)}, u32[]{:S(2)}) collective-permute-start(bf16[3,3,64,256]{3,2,1,0:T(8,128)(2,1)} %bitcast.10), channel_id=1, source_target_pairs={{0,2},{1,3},{2,0},{3,1},{4,6},{5,7},{6,4},{7,5},{8,10},{9,11},{10,... | collective-permute-start | bytes 884744 | tf_op jit(solution)/shard_map/ppermute | solution.py:285
  4.1 1.7 %copy-start.7 = (f32[64]{0:T(128)S(1)}, f32[64]{0:T(128)}, u32[]{:S(2)}) copy-start(f32[64]{0:T(128)} %param.14) | copy-start | bytes 772
  4.1 1.7 %copy-start.8 = (f32[64]{0:T(128)S(1)}, f32[64]{0:T(128)}, u32[]{:S(2)}) copy-start(f32[64]{0:T(128)} %param.12) | copy-start | bytes 772
  4.1 2.2 %copy-start = (bf16[64,3,3,256]{3,0,2,1:T(8,128)(2,1)S(1)}, bf16[64,3,3,256]{3,0,2,1:T(8,128)(2,1)}, u32[]{:S(2)}) copy-start(bf16[64,3,3,256]{3,0,2,1:T(8,128)(2,1)} %param.11) | copy-start | bytes 884740
  4.1 4.3 %copy-start.1 = (bf16[64,3,3,256]{3,0,2,1:T(8,128)(2,1)S(1)}, bf16[64,3,3,256]{3,0,2,1:T(8,128)(2,1)}, u32[]{:S(2)}) copy-start(bf16[64,3,3,256]{3,0,2,1:T(8,128)(2,1)} %param.13) | copy-start | bytes 884740
  4.2 4.8 %copy-start.5 = (s32[4096]{0:T(1024)S(1)}, s32[4096]{0:T(1024)}, u32[]{:S(2)}) copy-start(s32[4096]{0:T(1024)} %param.15) | copy-start | bytes 49156
  4.2 4.8 %copy-start.2 = (s32[4,512]{1,0:T(4,128)S(1)}, s32[4,512]{1,0:T(4,128)}, u32[]{:S(2)}) copy-start(s32[4,512]{1,0:T(4,128)} %slot.1) | copy-start | bytes 24580
  4.2 4.8 %copy-start.3 = (f32[2,512]{1,0:T(2,128)S(1)}, f32[2,512]{1,0:T(2,128)}, u32[]{:S(2)}) copy-start(f32[2,512]{1,0:T(2,128)} %frac.1) | copy-start | bytes 12292
  4.2 9.1 %collective-permute-start = (bf16[256,512]{1,0:T(8,128)(2,1)S(1)}, bf16[256,512]{1,0:T(8,128)(2,1)S(1)}, u32[]{:S(2)}, u32[]{:S(2)}) collective-permute-start(bf16[256,512]{1,0:T(8,128)(2,1)S(1)} %shard_map.100), channel_id=1, source_target_pairs={{0,4},{1,29},{2,6},{3,31},{4,8},{5,1},{6,10},{7,3},{8,12},{9,5},{1... | collective-permute-start | bytes 786440 | tf_op jit(solution)/shard_map/ppermute | solution.py:292
  5.9 4.4 %collective-permute-start.2 = (f32[1,128]{1,0:T(1,128)S(1)}, f32[1,128]{1,0:T(1,128)S(1)}, u32[]{:S(2)}, u32[]{:S(2)}) collective-permute-start(f32[1,128]{1,0:T(1,128)S(1)} %maximum_bitcast_fusion), channel_id=1, source_target_pairs={{0,2},{1,3},{2,0},{3,1},{4,6},{5,7},{6,4},{7,5},{8,10},{9,11},{10,... | collective-permute-start | bytes 1544 | tf_op jit(solution)/shard_map/ppermute | solution.py:285
  6.4 7.0 %collective-permute-start.3 = (bf16[3,3,64,256]{3,2,1,0:T(8,128)(2,1)S(1)}, bf16[3,3,64,256]{3,2,1,0:T(8,128)(2,1)S(1)}, u32[]{:S(2)}, u32[]{:S(2)}) collective-permute-start(bf16[3,3,64,256]{3,2,1,0:T(8,128)(2,1)S(1)} %bitcast.11), channel_id=1, source_target_pairs={{0,1},{1,0},{2,3},{3,2},{4,5},{5,4},{6,7},{7,6},{8,9},{9,8},{10,11... | collective-permute-start | bytes 884744 | tf_op jit(solution)/shard_map/ppermute | solution.py:285
  8.4 5.0 %collective-permute-start.4 = (bf16[3,3,64,256]{3,2,1,0:T(8,128)(2,1)S(1)}, bf16[3,3,64,256]{3,2,1,0:T(8,128)(2,1)S(1)}, u32[]{:S(2)}, u32[]{:S(2)}) collective-permute-start(bf16[3,3,64,256]{3,2,1,0:T(8,128)(2,1)S(1)} %bitcast.13), channel_id=1, source_target_pairs={{0,1},{1,0},{2,3},{3,2},{4,5},{5,4},{6,7},{7,6},{8,9},{9,8},{10,11... | collective-permute-start | bytes 884744 | tf_op jit(solution)/shard_map/ppermute | solution.py:285
  10.3 3.6 %collective-permute-start.6 = (f32[2,128]{1,0:T(2,128)S(1)}, f32[2,128]{1,0:T(2,128)S(1)}, u32[]{:S(2)}, u32[]{:S(2)}) collective-permute-start(f32[2,128]{1,0:T(2,128)S(1)} %pad_maximum_fusion.bias), channel_id=1, source_target_pairs={{0,1},{1,0},{2,3},{3,2},{4,5},{5,4},{6,7},{7,6},{8,9},{9,8},{10,11... | collective-permute-start | bytes 3080 | tf_op jit(solution)/shard_map/ppermute | solution.py:285
  10.9 3.0 %collective-permute-start.5 = (bf16[3,3,64,256]{3,2,1,0:T(8,128)(2,1)S(1)}, bf16[3,3,64,256]{3,2,1,0:T(8,128)(2,1)S(1)}, u32[]{:S(2)}, u32[]{:S(2)}) collective-permute-start(bf16[3,3,64,256]{3,2,1,0:T(8,128)(2,1)S(1)} %collective-permute-done.1.w1c), channel_id=1, source_target_pairs={{0,1},{1,0},{2,3},{3,2},{4,5},{5,4},{6,7},{7,6},{8,9},{9,8},{10,11... | collective-permute-start | bytes 884744 | tf_op jit(solution)/shard_map/ppermute | solution.py:285
  13.9 8.6 %copy-start.4 = (bf16[64,512]{1,0:T(8,128)(2,1)S(1)}, bf16[64,512]{1,0:T(8,128)(2,1)}, u32[]{:S(2)}) copy-start(bf16[64,512]{1,0:T(8,128)(2,1)} %param.18) | copy-start | bytes 196612
  15.8 6.7 %collective-permute-start.7 = (f32[8,512]{1,0:T(8,128)S(1)}, f32[8,512]{1,0:T(8,128)S(1)}, u32[]{:S(2)}, u32[]{:S(2)}) collective-permute-start(f32[8,512]{1,0:T(8,128)S(1)} %shard_map.103.table), channel_id=1, source_target_pairs={{0,4},{1,5},{2,6},{3,7},{4,0},{5,1},{6,2},{7,3},{8,12},{9,13},{10,... | collective-permute-start | bytes 49160 | tf_op jit(solution)/shard_map/ppermute | solution.py:292
  16.9 13.2 %collective-permute-start.11 = (bf16[128,512]{1,0:T(8,128)(2,1)S(1)}, bf16[128,512]{1,0:T(8,128)(2,1)S(1)}, u32[]{:S(2)}, u32[]{:S(2)}) collective-permute-start(bf16[128,512]{1,0:T(8,128)(2,1)S(1)} %shard_map.105.refs_2_), channel_id=1, source_target_pairs={{0,8},{1,9},{2,10},{3,11},{4,12},{5,13},{6,14},{7,15},{8,16},{9,17... | collective-permute-start | bytes 393224 | tf_op jit(solution)/shard_map/ppermute | solution.py:292
  18.5 11.6 %collective-permute-start.12 = (bf16[128,512]{1,0:T(8,128)(2,1)S(1)}, bf16[128,512]{1,0:T(8,128)(2,1)S(1)}, u32[]{:S(2)}, u32[]{:S(2)}) collective-permute-start(bf16[128,512]{1,0:T(8,128)(2,1)S(1)} %shard_map.105.refs_2_), channel_id=1, source_target_pairs={{0,16},{1,17},{2,18},{3,19},{4,20},{5,21},{6,22},{7,23},{8,24},{9,... | collective-permute-start | bytes 393224 | tf_op jit(solution)/shard_map/ppermute | solution.py:292
  21.6 8.6 %collective-permute-start.13 = (bf16[128,512]{1,0:T(8,128)(2,1)S(1)}, bf16[128,512]{1,0:T(8,128)(2,1)S(1)}, u32[]{:S(2)}, u32[]{:S(2)}) collective-permute-start(bf16[128,512]{1,0:T(8,128)(2,1)S(1)} %shard_map.105.refs_2_), channel_id=1, source_target_pairs={{0,24},{1,25},{2,26},{3,27},{4,28},{5,29},{6,30},{7,31},{8,0},{9,1... | collective-permute-start | bytes 393224 | tf_op jit(solution)/shard_map/ppermute | solution.py:292
  22.4 3.2 %collective-permute-start.10 = (bf16[64,128]{1,0:T(8,128)(2,1)S(1)}, bf16[64,128]{1,0:T(8,128)(2,1)S(1)}, u32[]{:S(2)}, u32[]{:S(2)}) collective-permute-start(bf16[64,128]{1,0:T(8,128)(2,1)S(1)} %get-tuple-element.57), channel_id=1, source_target_pairs={{0,3},{1,2},{2,1},{3,0},{4,7},{5,6},{6,5},{7,4},{8,11},{9,10},{10,... | collective-permute-start | bytes 49160 | tf_op jit(solution)/shard_map/ppermute | solution.py:285
  22.5 7.6 %collective-permute-start.8 = (bf16[64,128]{1,0:T(8,128)(2,1)S(1)}, bf16[64,128]{1,0:T(8,128)(2,1)S(1)}, u32[]{:S(2)}, u32[]{:S(2)}) collective-permute-start(bf16[64,128]{1,0:T(8,128)(2,1)S(1)} %get-tuple-element.59), channel_id=1, source_target_pairs={{0,1},{1,0},{2,3},{3,2},{4,5},{5,4},{6,7},{7,6},{8,9},{9,8},{10,11... | collective-permute-start | bytes 49160 | tf_op jit(solution)/shard_map/ppermute | solution.py:285
  25.7 4.4 %collective-permute-start.9 = (bf16[64,128]{1,0:T(8,128)(2,1)S(1)}, bf16[64,128]{1,0:T(8,128)(2,1)S(1)}, u32[]{:S(2)}, u32[]{:S(2)}) collective-permute-start(bf16[64,128]{1,0:T(8,128)(2,1)S(1)} %get-tuple-element.58), channel_id=1, source_target_pairs={{0,2},{1,3},{2,0},{3,1},{4,6},{5,7},{6,4},{7,5},{8,10},{9,11},{10,... | collective-permute-start | bytes 49160 | tf_op jit(solution)/shard_map/ppermute | solution.py:285
  30.6 8.5 %copy-start.6 = (f32[128]{0:T(128)S(1)}, f32[128]{0:T(128)}, u32[]{:S(2)}) copy-start(f32[128]{0:T(128)} %param.19) | copy-start | bytes 1540
  30.6 1.4 %collective-permute-start.14 = (bf16[128,512]{1,0:T(8,128)(2,1)S(1)}, bf16[128,512]{1,0:T(8,128)(2,1)S(1)}, u32[]{:S(2)}, u32[]{:S(2)}) collective-permute-start(bf16[128,512]{1,0:T(8,128)(2,1)S(1)} %shard_map.109), channel_id=1, source_target_pairs={{0,1},{1,0},{2,3},{3,2},{4,5},{5,4},{6,7},{7,6},{8,9},{9,8},{10,11... | collective-permute-start | bytes 393224 | tf_op jit(solution)/shard_map/ppermute | solution.py:285
  32.1 6.4 %collective-permute-start.15 = (bf16[128,512]{1,0:T(8,128)(2,1)S(1)}, bf16[128,512]{1,0:T(8,128)(2,1)S(1)}, u32[]{:S(2)}, u32[]{:S(2)}) collective-permute-start(bf16[128,512]{1,0:T(8,128)(2,1)S(1)} %shard_map.110.a), channel_id=1, source_target_pairs={{0,2},{1,7},{2,0},{3,5},{4,6},{5,3},{6,4},{7,1},{8,10},{9,15},{10,... | collective-permute-start | bytes 393224 | tf_op jit(solution)/shard_map/ppermute | solution.py:416
  33.6 5.0 %collective-permute-start.16 = (bf16[128,512]{1,0:T(8,128)(2,1)S(1)}, bf16[128,512]{1,0:T(8,128)(2,1)S(1)}, u32[]{:S(2)}, u32[]{:S(2)}) collective-permute-start(bf16[128,512]{1,0:T(8,128)(2,1)S(1)} %shard_map.110.a), channel_id=1, source_target_pairs={{1,5},{3,7},{5,1},{7,3},{9,13},{11,15},{13,9},{15,11},{17,21},{19,... | collective-permute-start | bytes 393224 | tf_op jit(solution)/shard_map/ppermute | solution.py:417
  38.5 1.4 %collective-permute-start.17 = (bf16[128,512]{1,0:T(8,128)(2,1)S(1)}, bf16[128,512]{1,0:T(8,128)(2,1)S(1)}, u32[]{:S(2)}, u32[]{:S(2)}) collective-permute-start(bf16[128,512]{1,0:T(8,128)(2,1)S(1)} %shard_map.111.refs_0_), channel_id=1, source_target_pairs={{0,1},{1,0},{2,3},{3,2},{4,5},{5,4},{6,7},{7,6},{8,9},{9,8},{10,11... | collective-permute-start | bytes 393224 | tf_op jit(solution)/shard_map/ppermute | solution.py:285
  38.9 1.3 %collective-permute-start.18 = (bf16[128,512]{1,0:T(8,128)(2,1)S(1)}, bf16[128,512]{1,0:T(8,128)(2,1)S(1)}, u32[]{:S(2)}, u32[]{:S(2)}) collective-permute-start(bf16[128,512]{1,0:T(8,128)(2,1)S(1)} %collective-permute-done.15.refs_2_), channel_id=1, source_target_pairs={{0,1},{1,0},{2,3},{3,2},{4,5},{5,4},{6,7},{7,6},{8,9},{9,8},{10,11... | collective-permute-start | bytes 393224 | tf_op jit(solution)/shard_map/ppermute | solution.py:285

commit v7 on v6

--- a/solution.py
+++ b/solution.py
@@ -370,10 +370,12 @@
     outs = expand_weight.shape[1] // n_ch
 
     def expansion_slices(expand_weight):
-        slices = []
-        for f in range(n_ch):
-            part = lax.dynamic_slice_in_dim(expand_weight, (ch ^ f) * outs, outs, 1)
-            slices.append(swap(part, f) if f else part)
+        slices = [
+            lax.dynamic_slice_in_dim(expand_weight, (ch ^ f) * outs, outs, 1) for f in range(n_ch)
+        ]
+        slices[1], slices[3] = swap(slices[1], 1), swap(slices[3], 3)
+        slices[1], slices[2] = lax.optimization_barrier((slices[1], slices[2]))
+        slices[2] = swap(slices[2], 2)
         return slices
 
     if direct:

time: 41.3 us -> 40.9 us (level); the launches traced: 41.2 us -> 40.1 us
  waiting for transfers between devices: 12.2 us -> 10.7 us
  starting transfers between devices: 18.5 us -> 19 us
    ppermute x12, waiting for transfers between devices: 5.45 us -> 3.55 us  [swap(): return lax.ppermute(x, 'ch', [(i, i ^ mask) for i in range(n_ch)])]
    ppermute x12, starting transfers between devices: 8.2 us -> 8.68 us  [swap(): return lax.ppermute(x, 'ch', [(i, i ^ mask) for i in range(n_ch)])]
  transfers between devices with their start and end apart: 19 -> 19, of which waited for: 8 -> 10; matrix products, arithmetic and copies ran while one was open for 3% -> 3% of each run, Pallas kernels for 13% -> 14%
where the time goes in v7:
time: 40.9 us; the launch traced here: 40.1 us
  starting transfers between devices  19 us (46%)
  waiting for transfers between devices  10.7 us (26%)
  Pallas kernels  8.74 us (21%)
  local copies, waits for them, and re-layouts  1.32 us (3%)
    pallas_call x13, Pallas kernels, call(): pl.pallas_call(kernel, out_shape=tuple(outs), in_specs=[vmem] * len(args)...  8.74 us
    ppermute x12, starting transfers between devices, swap(): return lax.ppermute(x, 'ch', [(i, i ^ mask) for i in range(n_ch)])  8.68 us
    ppermute x5, starting transfers between devices, joint(): return lax.ppermute(x, ('az', 'ch'), pairs)  8.21 us
    ppermute x1, waiting for transfers between devices, local(): far = lax.ppermute(kept, ('az', 'ch'), other_plane)  4.3 us
    ppermute x12, waiting for transfers between devices, swap(): return lax.ppermute(x, 'ch', [(i, i ^ mask) for i in range(n_ch)])  3.55 us
    ppermute x5, waiting for transfers between devices, joint(): return lax.ppermute(x, ('az', 'ch'), pairs)  2.8 us
    ppermute x1, starting transfers between devices, local(): far = lax.ppermute(kept, ('az', 'ch'), other_plane)  1.47 us
    unnamed x19, local copies, waits for them, and re-layouts  1.19 us
  transfers between devices with their start and end apart: 19, of which 10 were waited for; matrix products, arithmetic and copies ran while one was open for 3% of the time, Pallas kernels for 14%

profile of v7, /device:TPU:0, one launch (start us, length us, event | category | flops | bytes accessed | tf_op | source)
XLA Modules:
  0.0 40.1 jit_solution(9862208472208588968)
XLA Ops:
  0.0 3.0 %collective-permute-start.1 = (bf16[3,3,64,256]{3,2,1,0:T(8,128)(2,1)}, bf16[3,3,64,256]{3,2,1,0:T(8,128)(2,1)S(1)}, u32[]{:S(2)}, u32[]{:S(2)}) collective-permute-start(bf16[3,3,64,256]{3,2,1,0:T(8,128)(2,1)} %bitcast.10), channel_id=1, source_target_pairs={{0,2},{1,3},{2,0},{3,1},{4,6},{5,7},{6,4},{7,5},{8,10},{9,11},{10,... | collective-permute-start | bytes 884744 | tf_op jit(solution)/shard_map/ppermute | solution.py:285
  3.0 1.1 %copy.12 = bf16[32,8,4,256]{3,1,2,0:T(8,128)(2,1)S(1)} copy(bf16[32,8,4,256]{3,2,1,0:T(4,128)(2,1)} %bitcast.15) | data formatting | bytes 1048576
  4.1 0.0 copy-start.7
  4.1 0.0 copy-start.8
  4.1 0.0 copy-start
  4.1 0.0 copy-start.1
  4.2 0.0 copy-start.5
  4.2 0.0 copy-start.3
  4.2 1.5 %collective-permute-start = (bf16[256,512]{1,0:T(8,128)(2,1)S(1)}, bf16[256,512]{1,0:T(8,128)(2,1)S(1)}, u32[]{:S(2)}, u32[]{:S(2)}) collective-permute-start(bf16[256,512]{1,0:T(8,128)(2,1)S(1)} %shard_map.100), channel_id=1, source_target_pairs={{0,4},{1,29},{2,6},{3,31},{4,8},{5,1},{6,10},{7,3},{8,12},{9,5},{1... | collective-permute-start | bytes 786440 | tf_op jit(solution)/shard_map/ppermute | solution.py:292
  5.8 0.1 maximum_bitcast_fusion
  5.9 0.5 %collective-permute-start.2 = (f32[1,128]{1,0:T(1,128)S(1)}, f32[1,128]{1,0:T(1,128)S(1)}, u32[]{:S(2)}, u32[]{:S(2)}) collective-permute-start(f32[1,128]{1,0:T(1,128)S(1)} %maximum_bitcast_fusion), channel_id=1, source_target_pairs={{0,2},{1,3},{2,0},{3,1},{4,6},{5,7},{6,4},{7,5},{8,10},{9,11},{10,... | collective-permute-start | bytes 1544 | tf_op jit(solution)/shard_map/ppermute | solution.py:285
  6.4 2.0 %collective-permute-start.3 = (bf16[3,3,64,256]{3,2,1,0:T(8,128)(2,1)S(1)}, bf16[3,3,64,256]{3,2,1,0:T(8,128)(2,1)S(1)}, u32[]{:S(2)}, u32[]{:S(2)}) collective-permute-start(bf16[3,3,64,256]{3,2,1,0:T(8,128)(2,1)S(1)} %bitcast.11), channel_id=1, source_target_pairs={{0,1},{1,0},{2,3},{3,2},{4,5},{5,4},{6,7},{7,6},{8,9},{9,8},{10,11... | collective-permute-start | bytes 884744 | tf_op jit(solution)/shard_map/ppermute | solution.py:285
  8.4 0.1 collective-permute-start.4
  8.5 0.4 %shard_map.102 = (bf16[1024,256]{1,0:T(8,128)(2,1)S(1)}, bf16[192,768]{1,0:T(8,128)(2,1)S(1)}, f32[2,64,256]{2,1,0:T(8,128)S(1)}) custom-call(bf16[256,1024]{1,0:T(8,128)(2,1)S(1)} %bitcast.8, bf16[3,3,64,256]{3,2,1,0:T(8,128)(2,1)S(1)} %bitcast.12), custom_call_target="tpu_custom_call" | custom-call | tf_op jit(solution)/shard_map/pallas_call | solution.py:21
  9.0 0.3 shard_map.103.table
  9.3 0.9 %collective-permute-done.1.w1c = bf16[3,3,64,256]{3,2,1,0:T(8,128)(2,1)S(1)} collective-permute-done((bf16[3,3,64,256]{3,2,1,0:T(8,128)(2,1)}, bf16[3,3,64,256]{3,2,1,0:T(8,128)(2,1)S(1)}, u32[]{:S(2)}, u32[]{:S(2)}) %collective-permute-start.1) | collective-permute-done | bytes 294944 | tf_op jit(solution)/shard_map/ppermute | solution.py:285
  10.2 0.1 collective-permute-done.2
  10.3 0.6 %collective-permute-start.6 = (f32[2,128]{1,0:T(2,128)S(1)}, f32[2,128]{1,0:T(2,128)S(1)}, u32[]{:S(2)}, u32[]{:S(2)}) collective-permute-start(f32[2,128]{1,0:T(2,128)S(1)} %pad_maximum_fusion.bias), channel_id=1, source_target_pairs={{0,1},{1,0},{2,3},{3,2},{4,5},{5,4},{6,7},{7,6},{8,9},{9,8},{10,11... | collective-permute-start | bytes 3080 | tf_op jit(solution)/shard_map/ppermute | solution.py:285
  10.9 0.1 collective-permute-start.5
  10.9 2.4 %collective-permute-done.wide = bf16[256,512]{1,0:T(8,128)(2,1)S(1)} collective-permute-done((bf16[256,512]{1,0:T(8,128)(2,1)S(1)}, bf16[256,512]{1,0:T(8,128)(2,1)S(1)}, u32[]{:S(2)}, u32[]{:S(2)}) %collective-permute-start) | collective-permute-done | bytes 262176 | tf_op jit(solution)/shard_map/ppermute | solution.py:292
  13.4 0.4 %shard_map.104 = (bf16[384,768]{1,0:T(8,128)(2,1)S(1)}, bf16[384,768]{1,0:T(8,128)(2,1)S(1)}, f32[2,128,256]{2,1,0:T(8,128)S(1)}) custom-call(bf16[1024,256]{1,0:T(8,128)(2,1)S(1)} %get-tuple-element.33.xs, bf16[192,768]{1,0:T(8,128)(2,1)S(1)} %get-tuple-element.34.own_stack, f32[2,64,256]{2,1,0:T(8,128)S(1)} %get-tuple-element.39.own_inner, ...), custom_call_target="tpu_custom_call" | custom-call | bytes 3276800 | tf_op jit(solution)/shard_map/pallas_call | solution.py:21
  13.9 0.0 copy-start.4
  13.9 1.9 %shard_map.105.refs_2_ = bf16[128,512]{1,0:T(8,128)(2,1)S(1)} custom-call(bf16[256,1024]{1,0:T(8,128)(2,1)S(1)} %bitcast.9, bf16[512,256]{1,0:T(8,128)(2,1)S(1)} %shard_map.101.halo, bf16[384,768]{1,0:T(8,128)(2,1)S(1)} %get-tuple-element.42.near, bf16[384,768]{1,0:T(8,128)(2,1)S(1)} %get-tuple-element.43.w2s, f32[2,128,256]{2,1,0:T(8,128)S(1)} %get-tuple-element.44.inner, ...), custom_call_target="tpu_custom_call" | custom-call | flops 1207959552 | bytes 2951168 | tf_op jit(solution)/shard_map/pallas_call | solution.py:21
  15.8 1.1 %collective-permute-start.7 = (f32[8,512]{1,0:T(8,128)S(1)}, f32[8,512]{1,0:T(8,128)S(1)}, u32[]{:S(2)}, u32[]{:S(2)}) collective-permute-start(f32[8,512]{1,0:T(8,128)S(1)} %shard_map.103.table), channel_id=1, source_target_pairs={{0,4},{1,5},{2,6},{3,7},{4,0},{5,1},{6,2},{7,3},{8,12},{9,13},{10,... | collective-permute-start | bytes 49160 | tf_op jit(solution)/shard_map/ppermute | solution.py:292
  16.9 1.6 %collective-permute-start.11 = (bf16[128,512]{1,0:T(8,128)(2,1)S(1)}, bf16[128,512]{1,0:T(8,128)(2,1)S(1)}, u32[]{:S(2)}, u32[]{:S(2)}) collective-permute-start(bf16[128,512]{1,0:T(8,128)(2,1)S(1)} %shard_map.105.refs_2_), channel_id=1, source_target_pairs={{0,8},{1,9},{2,10},{3,11},{4,12},{5,13},{6,14},{7,15},{8,16},{9,17... | collective-permute-start | bytes 393224 | tf_op jit(solution)/shard_map/ppermute | solution.py:292
  18.5 3.1 %collective-permute-start.12 = (bf16[128,512]{1,0:T(8,128)(2,1)S(1)}, bf16[128,512]{1,0:T(8,128)(2,1)S(1)}, u32[]{:S(2)}, u32[]{:S(2)}) collective-permute-start(bf16[128,512]{1,0:T(8,128)(2,1)S(1)} %shard_map.105.refs_2_), channel_id=1, source_target_pairs={{0,16},{1,17},{2,18},{3,19},{4,20},{5,21},{6,22},{7,23},{8,24},{9,... | collective-permute-start | bytes 393224 | tf_op jit(solution)/shard_map/ppermute | solution.py:292
  21.6 0.8 %collective-permute-start.13 = (bf16[128,512]{1,0:T(8,128)(2,1)S(1)}, bf16[128,512]{1,0:T(8,128)(2,1)S(1)}, u32[]{:S(2)}, u32[]{:S(2)}) collective-permute-start(bf16[128,512]{1,0:T(8,128)(2,1)S(1)} %shard_map.105.refs_2_), channel_id=1, source_target_pairs={{0,24},{1,25},{2,26},{3,27},{4,28},{5,29},{6,30},{7,31},{8,0},{9,1... | collective-permute-start | bytes 393224 | tf_op jit(solution)/shard_map/ppermute | solution.py:292
  22.4 0.1 collective-permute-start.8
  22.5 0.6 %collective-permute-start.10 = (bf16[64,128]{1,0:T(8,128)(2,1)S(1)}, bf16[64,128]{1,0:T(8,128)(2,1)S(1)}, u32[]{:S(2)}, u32[]{:S(2)}) collective-permute-start(bf16[64,128]{1,0:T(8,128)(2,1)S(1)} %get-tuple-element.61), channel_id=1, source_target_pairs={{0,3},{1,2},{2,1},{3,0},{4,7},{5,6},{6,5},{7,4},{8,11},{9,10},{10,... | collective-permute-start | bytes 49160 | tf_op jit(solution)/shard_map/ppermute | solution.py:285
  23.1 0.5 %collective-permute-done.8.wb = bf16[64,128]{1,0:T(8,128)(2,1)S(1)} collective-permute-done((bf16[64,128]{1,0:T(8,128)(2,1)S(1)}, bf16[64,128]{1,0:T(8,128)(2,1)S(1)}, u32[]{:S(2)}, u32[]{:S(2)}) %collective-permute-start.8) | collective-permute-done | bytes 16416 | tf_op jit(solution)/shard_map/ppermute | solution.py:285
  23.7 1.0 %collective-permute-start.9 = (bf16[64,128]{1,0:T(8,128)(2,1)S(1)}, bf16[64,128]{1,0:T(8,128)(2,1)S(1)}, u32[]{:S(2)}, u32[]{:S(2)}) collective-permute-start(bf16[64,128]{1,0:T(8,128)(2,1)S(1)} %get-tuple-element.52), channel_id=1, source_target_pairs={{0,2},{1,3},{2,0},{3,1},{4,6},{5,7},{6,4},{7,5},{8,10},{9,11},{10,... | collective-permute-start | bytes 49160 | tf_op jit(solution)/shard_map/ppermute | solution.py:285
  24.7 1.9 %shard_map.106.refs_0_ = bf16[4,512,512]{2,1,0:T(8,128)(2,1)S(1)} custom-call(f32[8,512]{1,0:T(8,128)S(1)} %shard_map.103.table), custom_call_target="tpu_custom_call" | custom-call | tf_op jit(solution)/shard_map/pallas_call | solution.py:21
  26.6 1.9 %shard_map.107.refs_1_ = bf16[4,512,512]{2,1,0:T(8,128)(2,1)S(1)} custom-call(f32[8,512]{1,0:T(8,128)S(1)} %collective-permute-done.7.table), custom_call_target="tpu_custom_call" | custom-call | tf_op jit(solution)/shard_map/pallas_call | solution.py:21
  28.5 0.3 collective-permute-done.12.refs_4_
  28.8 0.1 collective-permute-done.13.refs_5_
  28.9 0.4 %shard_map.109 = bf16[128,512]{1,0:T(8,128)(2,1)S(1)} custom-call(bf16[4,512,512]{2,1,0:T(8,128)(2,1)S(1)} %shard_map.106.refs_0_, bf16[4,512,512]{2,1,0:T(8,128)(2,1)S(1)} %shard_map.107.refs_1_, bf16[128,512]{1,0:T(8,128)(2,1)S(1)} %shard_map.105.refs_2_, bf16[128,512]{1,0:T(8,128)(2,1)S(1)} %collective-permute-done.11.refs_3_, ...), custom_call_target="tpu_custom_call" | custom-call | flops 268435456 | bytes 4849664 | tf_op jit(solution)/shard_map/pallas_call | solution.py:21
  29.4 0.1 collective-permute-start.14
  29.4 0.5 %shard_map.108.a = bf16[128,512]{1,0:T(8,128)(2,1)S(1)} custom-call(bf16[4,512,512]{2,1,0:T(8,128)(2,1)S(1)} %shard_map.106.refs_0_, bf16[4,512,512]{2,1,0:T(8,128)(2,1)S(1)} %shard_map.107.refs_1_, bf16[128,512]{1,0:T(8,128)(2,1)S(1)} %shard_map.105.refs_2_, bf16[128,512]{1,0:T(8,128)(2,1)S(1)} %collective-permute-done.11.refs_3_, ...), custom_call_target="tpu_custom_call" | custom-call | flops 268435456 | bytes 4849664 | tf_op jit(solution)/shard_map/pallas_call | solution.py:21
  29.9 0.9 %collective-permute-done.14.b = bf16[128,512]{1,0:T(8,128)(2,1)S(1)} collective-permute-done((bf16[128,512]{1,0:T(8,128)(2,1)S(1)}, bf16[128,512]{1,0:T(8,128)(2,1)S(1)}, u32[]{:S(2)}, u32[]{:S(2)}) %collective-permute-start.14) | collective-permute-done | bytes 131104 | tf_op jit(solution)/shard_map/ppermute | solution.py:285
  30.8 1.5 %collective-permute-start.15 = (bf16[128,512]{1,0:T(8,128)(2,1)S(1)}, bf16[128,512]{1,0:T(8,128)(2,1)S(1)}, u32[]{:S(2)}, u32[]{:S(2)}) collective-permute-start(bf16[128,512]{1,0:T(8,128)(2,1)S(1)} %shard_map.110.a), channel_id=1, source_target_pairs={{0,2},{1,7},{2,0},{3,5},{4,6},{5,3},{6,4},{7,1},{8,10},{9,15},{10,... | collective-permute-start | bytes 393224 | tf_op jit(solution)/shard_map/ppermute | solution.py:418
  32.3 0.7 %collective-permute-start.16 = (bf16[128,512]{1,0:T(8,128)(2,1)S(1)}, bf16[128,512]{1,0:T(8,128)(2,1)S(1)}, u32[]{:S(2)}, u32[]{:S(2)}) collective-permute-start(bf16[128,512]{1,0:T(8,128)(2,1)S(1)} %shard_map.110.a), channel_id=1, source_target_pairs={{1,5},{3,7},{5,1},{7,3},{9,13},{11,15},{13,9},{15,11},{17,21},{19,... | collective-permute-start | bytes 393224 | tf_op jit(solution)/shard_map/ppermute | solution.py:419
  33.0 4.3 %collective-permute-done.15.refs_2_ = bf16[128,512]{1,0:T(8,128)(2,1)S(1)} collective-permute-done((bf16[128,512]{1,0:T(8,128)(2,1)S(1)}, bf16[128,512]{1,0:T(8,128)(2,1)S(1)}, u32[]{:S(2)}, u32[]{:S(2)}) %collective-permute-start.15) | collective-permute-done | bytes 131104 | tf_op jit(solution)/shard_map/ppermute | solution.py:418
  37.3 0.6 %collective-permute-start.17 = (bf16[128,512]{1,0:T(8,128)(2,1)S(1)}, bf16[128,512]{1,0:T(8,128)(2,1)S(1)}, u32[]{:S(2)}, u32[]{:S(2)}) collective-permute-start(bf16[128,512]{1,0:T(8,128)(2,1)S(1)} %shard_map.111.refs_0_), channel_id=1, source_target_pairs={{0,1},{1,0},{2,3},{3,2},{4,5},{5,4},{6,7},{7,6},{8,9},{9,8},{10,11... | collective-permute-start | bytes 393224 | tf_op jit(solution)/shard_map/ppermute | solution.py:285
  37.9 0.1 collective-permute-start.18
  38.0 0.1 copy.11.bias
  38.1 0.8 %collective-permute-done.17.refs_1_ = bf16[128,512]{1,0:T(8,128)(2,1)S(1)} collective-permute-done((bf16[128,512]{1,0:T(8,128)(2,1)S(1)}, bf16[128,512]{1,0:T(8,128)(2,1)S(1)}, u32[]{:S(2)}, u32[]{:S(2)}) %collective-permute-start.17) | collective-permute-done | bytes 131104 | tf_op jit(solution)/shard_map/ppermute | solution.py:285
  38.9 0.4 collective-permute-done.18.refs_3_
  39.2 0.9 %shard_map.112 = bf16[128,512]{1,0:T(8,128)(2,1)} custom-call(bf16[64,128]{1,0:T(8,128)(2,1)S(1)} %get-tuple-element.53.wa, bf16[64,128]{1,0:T(8,128)(2,1)S(1)} %collective-permute-done.8.wb, bf16[64,128]{1,0:T(8,128)(2,1)S(1)} %collective-permute-done.9.wc, bf16[64,128]{1,0:T(8,128)(2,1)S(1)} %collective-permute-done.10.wd, f32[128,1]{1,0:T(8,128)S(1)} %copy.11.bias, ...), custom_call_target="tpu_custom_call" | custom-call | flops 67108864 | bytes 721408 | tf_op jit(solution)/shard_map/pallas_call | solution.py:21
  (27 shorter events, 0.2 us)
Async XLA Ops:
  0.0 10.2 %collective-permute-start.1 = (bf16[3,3,64,256]{3,2,1,0:T(8,128)(2,1)}, bf16[3,3,64,256]{3,2,1,0:T(8,128)(2,1)S(1)}, u32[]{:S(2)}, u32[]{:S(2)}) collective-permute-start(bf16[3,3,64,256]{3,2,1,0:T(8,128)(2,1)} %bitcast.10), channel_id=1, source_target_pairs={{0,2},{1,3},{2,0},{3,1},{4,6},{5,7},{6,4},{7,5},{8,10},{9,11},{10,... | collective-permute-start | bytes 884744 | tf_op jit(solution)/shard_map/ppermute | solution.py:285
  4.1 1.7 %copy-start.7 = (f32[64]{0:T(128)S(1)}, f32[64]{0:T(128)}, u32[]{:S(2)}) copy-start(f32[64]{0:T(128)} %param.14) | copy-start | bytes 772
  4.1 1.7 %copy-start.8 = (f32[64]{0:T(128)S(1)}, f32[64]{0:T(128)}, u32[]{:S(2)}) copy-start(f32[64]{0:T(128)} %param.12) | copy-start | bytes 772
  4.1 2.2 %copy-start = (bf16[64,3,3,256]{3,0,2,1:T(8,128)(2,1)S(1)}, bf16[64,3,3,256]{3,0,2,1:T(8,128)(2,1)}, u32[]{:S(2)}) copy-start(bf16[64,3,3,256]{3,0,2,1:T(8,128)(2,1)} %param.11) | copy-start | bytes 884740
  4.1 4.3 %copy-start.1 = (bf16[64,3,3,256]{3,0,2,1:T(8,128)(2,1)S(1)}, bf16[64,3,3,256]{3,0,2,1:T(8,128)(2,1)}, u32[]{:S(2)}) copy-start(bf16[64,3,3,256]{3,0,2,1:T(8,128)(2,1)} %param.13) | copy-start | bytes 884740
  4.2 4.8 %copy-start.5 = (s32[4096]{0:T(1024)S(1)}, s32[4096]{0:T(1024)}, u32[]{:S(2)}) copy-start(s32[4096]{0:T(1024)} %param.15) | copy-start | bytes 49156
  4.2 4.8 %copy-start.2 = (s32[4,512]{1,0:T(4,128)S(1)}, s32[4,512]{1,0:T(4,128)}, u32[]{:S(2)}) copy-start(s32[4,512]{1,0:T(4,128)} %slot.1) | copy-start | bytes 24580
  4.2 4.8 %copy-start.3 = (f32[2,512]{1,0:T(2,128)S(1)}, f32[2,512]{1,0:T(2,128)}, u32[]{:S(2)}) copy-start(f32[2,512]{1,0:T(2,128)} %frac.1) | copy-start | bytes 12292
  4.2 9.1 %collective-permute-start = (bf16[256,512]{1,0:T(8,128)(2,1)S(1)}, bf16[256,512]{1,0:T(8,128)(2,1)S(1)}, u32[]{:S(2)}, u32[]{:S(2)}) collective-permute-start(bf16[256,512]{1,0:T(8,128)(2,1)S(1)} %shard_map.100), channel_id=1, source_target_pairs={{0,4},{1,29},{2,6},{3,31},{4,8},{5,1},{6,10},{7,3},{8,12},{9,5},{1... | collective-permute-start | bytes 786440 | tf_op jit(solution)/shard_map/ppermute | solution.py:292
  5.9 4.4 %collective-permute-start.2 = (f32[1,128]{1,0:T(1,128)S(1)}, f32[1,128]{1,0:T(1,128)S(1)}, u32[]{:S(2)}, u32[]{:S(2)}) collective-permute-start(f32[1,128]{1,0:T(1,128)S(1)} %maximum_bitcast_fusion), channel_id=1, source_target_pairs={{0,2},{1,3},{2,0},{3,1},{4,6},{5,7},{6,4},{7,5},{8,10},{9,11},{10,... | collective-permute-start | bytes 1544 | tf_op jit(solution)/shard_map/ppermute | solution.py:285
  6.4 7.0 %collective-permute-start.3 = (bf16[3,3,64,256]{3,2,1,0:T(8,128)(2,1)S(1)}, bf16[3,3,64,256]{3,2,1,0:T(8,128)(2,1)S(1)}, u32[]{:S(2)}, u32[]{:S(2)}) collective-permute-start(bf16[3,3,64,256]{3,2,1,0:T(8,128)(2,1)S(1)} %bitcast.11), channel_id=1, source_target_pairs={{0,1},{1,0},{2,3},{3,2},{4,5},{5,4},{6,7},{7,6},{8,9},{9,8},{10,11... | collective-permute-start | bytes 884744 | tf_op jit(solution)/shard_map/ppermute | solution.py:285
  8.4 5.0 %collective-permute-start.4 = (bf16[3,3,64,256]{3,2,1,0:T(8,128)(2,1)S(1)}, bf16[3,3,64,256]{3,2,1,0:T(8,128)(2,1)S(1)}, u32[]{:S(2)}, u32[]{:S(2)}) collective-permute-start(bf16[3,3,64,256]{3,2,1,0:T(8,128)(2,1)S(1)} %bitcast.13), channel_id=1, source_target_pairs={{0,1},{1,0},{2,3},{3,2},{4,5},{5,4},{6,7},{7,6},{8,9},{9,8},{10,11... | collective-permute-start | bytes 884744 | tf_op jit(solution)/shard_map/ppermute | solution.py:285
  10.3 3.6 %collective-permute-start.6 = (f32[2,128]{1,0:T(2,128)S(1)}, f32[2,128]{1,0:T(2,128)S(1)}, u32[]{:S(2)}, u32[]{:S(2)}) collective-permute-start(f32[2,128]{1,0:T(2,128)S(1)} %pad_maximum_fusion.bias), channel_id=1, source_target_pairs={{0,1},{1,0},{2,3},{3,2},{4,5},{5,4},{6,7},{7,6},{8,9},{9,8},{10,11... | collective-permute-start | bytes 3080 | tf_op jit(solution)/shard_map/ppermute | solution.py:285
  10.9 3.0 %collective-permute-start.5 = (bf16[3,3,64,256]{3,2,1,0:T(8,128)(2,1)S(1)}, bf16[3,3,64,256]{3,2,1,0:T(8,128)(2,1)S(1)}, u32[]{:S(2)}, u32[]{:S(2)}) collective-permute-start(bf16[3,3,64,256]{3,2,1,0:T(8,128)(2,1)S(1)} %collective-permute-done.1.w1c), channel_id=1, source_target_pairs={{0,1},{1,0},{2,3},{3,2},{4,5},{5,4},{6,7},{7,6},{8,9},{9,8},{10,11... | collective-permute-start | bytes 884744 | tf_op jit(solution)/shard_map/ppermute | solution.py:285
  13.9 8.6 %copy-start.4 = (bf16[64,512]{1,0:T(8,128)(2,1)S(1)}, bf16[64,512]{1,0:T(8,128)(2,1)}, u32[]{:S(2)}) copy-start(bf16[64,512]{1,0:T(8,128)(2,1)} %param.18) | copy-start | bytes 196612
  15.8 6.7 %collective-permute-start.7 = (f32[8,512]{1,0:T(8,128)S(1)}, f32[8,512]{1,0:T(8,128)S(1)}, u32[]{:S(2)}, u32[]{:S(2)}) collective-permute-start(f32[8,512]{1,0:T(8,128)S(1)} %shard_map.103.table), channel_id=1, source_target_pairs={{0,4},{1,5},{2,6},{3,7},{4,0},{5,1},{6,2},{7,3},{8,12},{9,13},{10,... | collective-permute-start | bytes 49160 | tf_op jit(solution)/shard_map/ppermute | solution.py:292
  16.9 11.6 %collective-permute-start.11 = (bf16[128,512]{1,0:T(8,128)(2,1)S(1)}, bf16[128,512]{1,0:T(8,128)(2,1)S(1)}, u32[]{:S(2)}, u32[]{:S(2)}) collective-permute-start(bf16[128,512]{1,0:T(8,128)(2,1)S(1)} %shard_map.105.refs_2_), channel_id=1, source_target_pairs={{0,8},{1,9},{2,10},{3,11},{4,12},{5,13},{6,14},{7,15},{8,16},{9,17... | collective-permute-start | bytes 393224 | tf_op jit(solution)/shard_map/ppermute | solution.py:292
  18.5 10.3 %collective-permute-start.12 = (bf16[128,512]{1,0:T(8,128)(2,1)S(1)}, bf16[128,512]{1,0:T(8,128)(2,1)S(1)}, u32[]{:S(2)}, u32[]{:S(2)}) collective-permute-start(bf16[128,512]{1,0:T(8,128)(2,1)S(1)} %shard_map.105.refs_2_), channel_id=1, source_target_pairs={{0,16},{1,17},{2,18},{3,19},{4,20},{5,21},{6,22},{7,23},{8,24},{9,... | collective-permute-start | bytes 393224 | tf_op jit(solution)/shard_map/ppermute | solution.py:292
  21.6 7.3 %collective-permute-start.13 = (bf16[128,512]{1,0:T(8,128)(2,1)S(1)}, bf16[128,512]{1,0:T(8,128)(2,1)S(1)}, u32[]{:S(2)}, u32[]{:S(2)}) collective-permute-start(bf16[128,512]{1,0:T(8,128)(2,1)S(1)} %shard_map.105.refs_2_), channel_id=1, source_target_pairs={{0,24},{1,25},{2,26},{3,27},{4,28},{5,29},{6,30},{7,31},{8,0},{9,1... | collective-permute-start | bytes 393224 | tf_op jit(solution)/shard_map/ppermute | solution.py:292
  22.4 1.2 %collective-permute-start.8 = (bf16[64,128]{1,0:T(8,128)(2,1)S(1)}, bf16[64,128]{1,0:T(8,128)(2,1)S(1)}, u32[]{:S(2)}, u32[]{:S(2)}) collective-permute-start(bf16[64,128]{1,0:T(8,128)(2,1)S(1)} %get-tuple-element.63), channel_id=1, source_target_pairs={{0,1},{1,0},{2,3},{3,2},{4,5},{5,4},{6,7},{7,6},{8,9},{9,8},{10,11... | collective-permute-start | bytes 49160 | tf_op jit(solution)/shard_map/ppermute | solution.py:285
  22.5 6.0 %collective-permute-start.10 = (bf16[64,128]{1,0:T(8,128)(2,1)S(1)}, bf16[64,128]{1,0:T(8,128)(2,1)S(1)}, u32[]{:S(2)}, u32[]{:S(2)}) collective-permute-start(bf16[64,128]{1,0:T(8,128)(2,1)S(1)} %get-tuple-element.61), channel_id=1, source_target_pairs={{0,3},{1,2},{2,1},{3,0},{4,7},{5,6},{6,5},{7,4},{8,11},{9,10},{10,... | collective-permute-start | bytes 49160 | tf_op jit(solution)/shard_map/ppermute | solution.py:285
  23.7 4.8 %collective-permute-start.9 = (bf16[64,128]{1,0:T(8,128)(2,1)S(1)}, bf16[64,128]{1,0:T(8,128)(2,1)S(1)}, u32[]{:S(2)}, u32[]{:S(2)}) collective-permute-start(bf16[64,128]{1,0:T(8,128)(2,1)S(1)} %get-tuple-element.52), channel_id=1, source_target_pairs={{0,2},{1,3},{2,0},{3,1},{4,6},{5,7},{6,4},{7,5},{8,10},{9,11},{10,... | collective-permute-start | bytes 49160 | tf_op jit(solution)/shard_map/ppermute | solution.py:285
  29.3 8.6 %copy-start.6 = (f32[128]{0:T(128)S(1)}, f32[128]{0:T(128)}, u32[]{:S(2)}) copy-start(f32[128]{0:T(128)} %param.19) | copy-start | bytes 1540
  29.4 1.4 %collective-permute-start.14 = (bf16[128,512]{1,0:T(8,128)(2,1)S(1)}, bf16[128,512]{1,0:T(8,128)(2,1)S(1)}, u32[]{:S(2)}, u32[]{:S(2)}) collective-permute-start(bf16[128,512]{1,0:T(8,128)(2,1)S(1)} %shard_map.109), channel_id=1, source_target_pairs={{0,1},{1,0},{2,3},{3,2},{4,5},{5,4},{6,7},{7,6},{8,9},{9,8},{10,11... | collective-permute-start | bytes 393224 | tf_op jit(solution)/shard_map/ppermute | solution.py:285
  30.8 6.4 %collective-permute-start.15 = (bf16[128,512]{1,0:T(8,128)(2,1)S(1)}, bf16[128,512]{1,0:T(8,128)(2,1)S(1)}, u32[]{:S(2)}, u32[]{:S(2)}) collective-permute-start(bf16[128,512]{1,0:T(8,128)(2,1)S(1)} %shard_map.110.a), channel_id=1, source_target_pairs={{0,2},{1,7},{2,0},{3,5},{4,6},{5,3},{6,4},{7,1},{8,10},{9,15},{10,... | collective-permute-start | bytes 393224 | tf_op jit(solution)/shard_map/ppermute | solution.py:418
  32.3 5.0 %collective-permute-start.16 = (bf16[128,512]{1,0:T(8,128)(2,1)S(1)}, bf16[128,512]{1,0:T(8,128)(2,1)S(1)}, u32[]{:S(2)}, u32[]{:S(2)}) collective-permute-start(bf16[128,512]{1,0:T(8,128)(2,1)S(1)} %shard_map.110.a), channel_id=1, source_target_pairs={{1,5},{3,7},{5,1},{7,3},{9,13},{11,15},{13,9},{15,11},{17,21},{19,... | collective-permute-start | bytes 393224 | tf_op jit(solution)/shard_map/ppermute | solution.py:419
  37.3 1.6 %collective-permute-start.17 = (bf16[128,512]{1,0:T(8,128)(2,1)S(1)}, bf16[128,512]{1,0:T(8,128)(2,1)S(1)}, u32[]{:S(2)}, u32[]{:S(2)}) collective-permute-start(bf16[128,512]{1,0:T(8,128)(2,1)S(1)} %shard_map.111.refs_0_), channel_id=1, source_target_pairs={{0,1},{1,0},{2,3},{3,2},{4,5},{5,4},{6,7},{7,6},{8,9},{9,8},{10,11... | collective-permute-start | bytes 393224 | tf_op jit(solution)/shard_map/ppermute | solution.py:285
  37.9 1.3 %collective-permute-start.18 = (bf16[128,512]{1,0:T(8,128)(2,1)S(1)}, bf16[128,512]{1,0:T(8,128)(2,1)S(1)}, u32[]{:S(2)}, u32[]{:S(2)}) collective-permute-start(bf16[128,512]{1,0:T(8,128)(2,1)S(1)} %collective-permute-done.15.refs_2_), channel_id=1, source_target_pairs={{0,1},{1,0},{2,3},{3,2},{4,5},{5,4},{6,7},{7,6},{8,9},{9,8},{10,11... | collective-permute-start | bytes 393224 | tf_op jit(solution)/shard_map/ppermute | solution.py:285

commit v8 on v7

--- a/solution.py
+++ b/solution.py
@@ -174,7 +174,7 @@
     az, core = lax.axis_index("az"), lax.rem(lax.axis_index("ch"), 2)
     blocks, held, cells = sampling.shape
     z, x = lax.div(az, 2), lax.rem(az, 2)
-    rows = 64
+    rows = 32
     places, weights = [], []
     for k in range(4):
         at = table[k : k + 1, :].astype(jnp.int32)

time: 40.9 us -> 40.9 us (level)
  Pallas kernels: 8.74 us -> 9.33 us
    pallas_call x13, Pallas kernels: 8.74 us -> 9.33 us  [call(): pl.pallas_call(kernel, out_shape=tuple(outs), in_specs=[vmem] * len(args)...]
  transfers between devices with their start and end apart: 19 -> 19, of which waited for: 10 -> 8; matrix products, arithmetic and copies ran while one was open for 3% -> 3% of each run, Pallas kernels for 14% -> 15%
where the time goes in v8:
time: 40.9 us; the launch traced here: 40.1 us
  starting transfers between devices  18.7 us (46%)
  waiting for transfers between devices  10.4 us (25%)
  Pallas kernels  9.33 us (23%)
  local copies, waits for them, and re-layouts  1.32 us (3%)
    pallas_call x13, Pallas kernels, call(): pl.pallas_call(kernel, out_shape=tuple(outs), in_specs=[vmem] * len(args)...  9.33 us
    ppermute x12, starting transfers between devices, swap(): return lax.ppermute(x, 'ch', [(i, i ^ mask) for i in range(n_ch)])  8.58 us
    ppermute x5, starting transfers between devices, joint(): return lax.ppermute(x, ('az', 'ch'), pairs)  8.21 us
    ppermute x1, waiting for transfers between devices, local(): far = lax.ppermute(kept, ('az', 'ch'), other_plane)  4.53 us
    ppermute x12, waiting for transfers between devices, swap(): return lax.ppermute(x, 'ch', [(i, i ^ mask) for i in range(n_ch)])  3.43 us
    ppermute x5, waiting for transfers between devices, joint(): return lax.ppermute(x, ('az', 'ch'), pairs)  2.43 us
    ppermute x1, starting transfers between devices, local(): far = lax.ppermute(kept, ('az', 'ch'), other_plane)  1.25 us
    unnamed x19, local copies, waits for them, and re-layouts  1.19 us
  transfers between devices with their start and end apart: 19, of which 8 were waited for; matrix products, arithmetic and copies ran while one was open for 3% of the time, Pallas kernels for 15%

profile of v8, /device:TPU:0, one launch (start us, length us, event | category | flops | bytes accessed | tf_op | source)
XLA Modules:
  0.0 40.1 jit_solution(3090955700778398756)
XLA Ops:
  0.0 3.0 %collective-permute-start.1 = (bf16[3,3,64,256]{3,2,1,0:T(8,128)(2,1)}, bf16[3,3,64,256]{3,2,1,0:T(8,128)(2,1)S(1)}, u32[]{:S(2)}, u32[]{:S(2)}) collective-permute-start(bf16[3,3,64,256]{3,2,1,0:T(8,128)(2,1)} %bitcast.10), channel_id=1, source_target_pairs={{0,2},{1,3},{2,0},{3,1},{4,6},{5,7},{6,4},{7,5},{8,10},{9,11},{10,... | collective-permute-start | bytes 884744 | tf_op jit(solution)/shard_map/ppermute | solution.py:285
  3.0 1.1 %copy.12 = bf16[32,8,4,256]{3,1,2,0:T(8,128)(2,1)S(1)} copy(bf16[32,8,4,256]{3,2,1,0:T(4,128)(2,1)} %bitcast.15) | data formatting | bytes 1048576
  4.1 0.0 copy-start.7
  4.1 0.0 copy-start.8
  4.1 0.0 copy-start
  4.1 0.0 copy-start.1
  4.2 0.0 copy-start.5
  4.2 0.0 copy-start.2
  4.2 0.0 copy-start.3
  4.2 1.5 %collective-permute-start = (bf16[256,512]{1,0:T(8,128)(2,1)S(1)}, bf16[256,512]{1,0:T(8,128)(2,1)S(1)}, u32[]{:S(2)}, u32[]{:S(2)}) collective-permute-start(bf16[256,512]{1,0:T(8,128)(2,1)S(1)} %shard_map.100), channel_id=1, source_target_pairs={{0,4},{1,29},{2,6},{3,31},{4,8},{5,1},{6,10},{7,3},{8,12},{9,5},{1... | collective-permute-start | bytes 786440 | tf_op jit(solution)/shard_map/ppermute | solution.py:292
  5.8 0.1 maximum_bitcast_fusion
  5.9 0.5 %collective-permute-start.2 = (f32[1,128]{1,0:T(1,128)S(1)}, f32[1,128]{1,0:T(1,128)S(1)}, u32[]{:S(2)}, u32[]{:S(2)}) collective-permute-start(f32[1,128]{1,0:T(1,128)S(1)} %maximum_bitcast_fusion), channel_id=1, source_target_pairs={{0,2},{1,3},{2,0},{3,1},{4,6},{5,7},{6,4},{7,5},{8,10},{9,11},{10,... | collective-permute-start | bytes 1544 | tf_op jit(solution)/shard_map/ppermute | solution.py:285
  6.4 2.0 %collective-permute-start.3 = (bf16[3,3,64,256]{3,2,1,0:T(8,128)(2,1)S(1)}, bf16[3,3,64,256]{3,2,1,0:T(8,128)(2,1)S(1)}, u32[]{:S(2)}, u32[]{:S(2)}) collective-permute-start(bf16[3,3,64,256]{3,2,1,0:T(8,128)(2,1)S(1)} %bitcast.11), channel_id=1, source_target_pairs={{0,1},{1,0},{2,3},{3,2},{4,5},{5,4},{6,7},{7,6},{8,9},{9,8},{10,11... | collective-permute-start | bytes 884744 | tf_op jit(solution)/shard_map/ppermute | solution.py:285
  8.4 0.1 collective-permute-start.4
  8.5 0.4 %shard_map.102 = (bf16[1024,256]{1,0:T(8,128)(2,1)S(1)}, bf16[192,768]{1,0:T(8,128)(2,1)S(1)}, f32[2,64,256]{2,1,0:T(8,128)S(1)}) custom-call(bf16[256,1024]{1,0:T(8,128)(2,1)S(1)} %bitcast.8, bf16[3,3,64,256]{3,2,1,0:T(8,128)(2,1)S(1)} %bitcast.12), custom_call_target="tpu_custom_call" | custom-call | tf_op jit(solution)/shard_map/pallas_call | solution.py:21
  9.0 0.3 shard_map.103.table
  9.3 0.9 %collective-permute-done.1.w1c = bf16[3,3,64,256]{3,2,1,0:T(8,128)(2,1)S(1)} collective-permute-done((bf16[3,3,64,256]{3,2,1,0:T(8,128)(2,1)}, bf16[3,3,64,256]{3,2,1,0:T(8,128)(2,1)S(1)}, u32[]{:S(2)}, u32[]{:S(2)}) %collective-permute-start.1) | collective-permute-done | bytes 294944 | tf_op jit(solution)/shard_map/ppermute | solution.py:285
  10.2 0.1 collective-permute-done.2
  10.3 0.6 %collective-permute-start.6 = (f32[2,128]{1,0:T(2,128)S(1)}, f32[2,128]{1,0:T(2,128)S(1)}, u32[]{:S(2)}, u32[]{:S(2)}) collective-permute-start(f32[2,128]{1,0:T(2,128)S(1)} %pad_maximum_fusion.bias), channel_id=1, source_target_pairs={{0,1},{1,0},{2,3},{3,2},{4,5},{5,4},{6,7},{7,6},{8,9},{9,8},{10,11... | collective-permute-start | bytes 3080 | tf_op jit(solution)/shard_map/ppermute | solution.py:285
  10.9 0.1 collective-permute-start.5
  10.9 2.4 %collective-permute-done.wide = bf16[256,512]{1,0:T(8,128)(2,1)S(1)} collective-permute-done((bf16[256,512]{1,0:T(8,128)(2,1)S(1)}, bf16[256,512]{1,0:T(8,128)(2,1)S(1)}, u32[]{:S(2)}, u32[]{:S(2)}) %collective-permute-start) | collective-permute-done | bytes 262176 | tf_op jit(solution)/shard_map/ppermute | solution.py:292
  13.4 0.4 %shard_map.104 = (bf16[384,768]{1,0:T(8,128)(2,1)S(1)}, bf16[384,768]{1,0:T(8,128)(2,1)S(1)}, f32[2,128,256]{2,1,0:T(8,128)S(1)}) custom-call(bf16[1024,256]{1,0:T(8,128)(2,1)S(1)} %get-tuple-element.33.xs, bf16[192,768]{1,0:T(8,128)(2,1)S(1)} %get-tuple-element.34.own_stack, f32[2,64,256]{2,1,0:T(8,128)S(1)} %get-tuple-element.39.own_inner, ...), custom_call_target="tpu_custom_call" | custom-call | bytes 3276800 | tf_op jit(solution)/shard_map/pallas_call | solution.py:21
  13.9 0.0 copy-start.4
  13.9 1.9 %shard_map.105.refs_2_ = bf16[128,512]{1,0:T(8,128)(2,1)S(1)} custom-call(bf16[256,1024]{1,0:T(8,128)(2,1)S(1)} %bitcast.9, bf16[512,256]{1,0:T(8,128)(2,1)S(1)} %shard_map.101.halo, bf16[384,768]{1,0:T(8,128)(2,1)S(1)} %get-tuple-element.42.near, bf16[384,768]{1,0:T(8,128)(2,1)S(1)} %get-tuple-element.43.w2s, f32[2,128,256]{2,1,0:T(8,128)S(1)} %get-tuple-element.44.inner, ...), custom_call_target="tpu_custom_call" | custom-call | flops 1207959552 | bytes 2951168 | tf_op jit(solution)/shard_map/pallas_call | solution.py:21
  15.8 1.1 %collective-permute-start.7 = (f32[8,512]{1,0:T(8,128)S(1)}, f32[8,512]{1,0:T(8,128)S(1)}, u32[]{:S(2)}, u32[]{:S(2)}) collective-permute-start(f32[8,512]{1,0:T(8,128)S(1)} %shard_map.103.table), channel_id=1, source_target_pairs={{0,4},{1,5},{2,6},{3,7},{4,0},{5,1},{6,2},{7,3},{8,12},{9,13},{10,... | collective-permute-start | bytes 49160 | tf_op jit(solution)/shard_map/ppermute | solution.py:292
  16.9 1.6 %collective-permute-start.11 = (bf16[128,512]{1,0:T(8,128)(2,1)S(1)}, bf16[128,512]{1,0:T(8,128)(2,1)S(1)}, u32[]{:S(2)}, u32[]{:S(2)}) collective-permute-start(bf16[128,512]{1,0:T(8,128)(2,1)S(1)} %shard_map.105.refs_2_), channel_id=1, source_target_pairs={{0,8},{1,9},{2,10},{3,11},{4,12},{5,13},{6,14},{7,15},{8,16},{9,17... | collective-permute-start | bytes 393224 | tf_op jit(solution)/shard_map/ppermute | solution.py:292
  18.5 3.1 %collective-permute-start.12 = (bf16[128,512]{1,0:T(8,128)(2,1)S(1)}, bf16[128,512]{1,0:T(8,128)(2,1)S(1)}, u32[]{:S(2)}, u32[]{:S(2)}) collective-permute-start(bf16[128,512]{1,0:T(8,128)(2,1)S(1)} %shard_map.105.refs_2_), channel_id=1, source_target_pairs={{0,16},{1,17},{2,18},{3,19},{4,20},{5,21},{6,22},{7,23},{8,24},{9,... | collective-permute-start | bytes 393224 | tf_op jit(solution)/shard_map/ppermute | solution.py:292
  21.6 0.8 %collective-permute-start.13 = (bf16[128,512]{1,0:T(8,128)(2,1)S(1)}, bf16[128,512]{1,0:T(8,128)(2,1)S(1)}, u32[]{:S(2)}, u32[]{:S(2)}) collective-permute-start(bf16[128,512]{1,0:T(8,128)(2,1)S(1)} %shard_map.105.refs_2_), channel_id=1, source_target_pairs={{0,24},{1,25},{2,26},{3,27},{4,28},{5,29},{6,30},{7,31},{8,0},{9,1... | collective-permute-start | bytes 393224 | tf_op jit(solution)/shard_map/ppermute | solution.py:292
  22.4 0.1 collective-permute-start.8
  22.5 0.6 %collective-permute-start.10 = (bf16[64,128]{1,0:T(8,128)(2,1)S(1)}, bf16[64,128]{1,0:T(8,128)(2,1)S(1)}, u32[]{:S(2)}, u32[]{:S(2)}) collective-permute-start(bf16[64,128]{1,0:T(8,128)(2,1)S(1)} %get-tuple-element.61), channel_id=1, source_target_pairs={{0,3},{1,2},{2,1},{3,0},{4,7},{5,6},{6,5},{7,4},{8,11},{9,10},{10,... | collective-permute-start | bytes 49160 | tf_op jit(solution)/shard_map/ppermute | solution.py:285
  23.1 0.5 %collective-permute-done.8.wb = bf16[64,128]{1,0:T(8,128)(2,1)S(1)} collective-permute-done((bf16[64,128]{1,0:T(8,128)(2,1)S(1)}, bf16[64,128]{1,0:T(8,128)(2,1)S(1)}, u32[]{:S(2)}, u32[]{:S(2)}) %collective-permute-start.8) | collective-permute-done | bytes 16416 | tf_op jit(solution)/shard_map/ppermute | solution.py:285
  23.7 1.0 %collective-permute-start.9 = (bf16[64,128]{1,0:T(8,128)(2,1)S(1)}, bf16[64,128]{1,0:T(8,128)(2,1)S(1)}, u32[]{:S(2)}, u32[]{:S(2)}) collective-permute-start(bf16[64,128]{1,0:T(8,128)(2,1)S(1)} %get-tuple-element.52), channel_id=1, source_target_pairs={{0,2},{1,3},{2,0},{3,1},{4,6},{5,7},{6,4},{7,5},{8,10},{9,11},{10,... | collective-permute-start | bytes 49160 | tf_op jit(solution)/shard_map/ppermute | solution.py:285
  24.7 2.2 %shard_map.106.refs_0_ = bf16[4,512,512]{2,1,0:T(8,128)(2,1)S(1)} custom-call(f32[8,512]{1,0:T(8,128)S(1)} %shard_map.103.table), custom_call_target="tpu_custom_call" | custom-call | tf_op jit(solution)/shard_map/pallas_call | solution.py:21
  26.9 2.2 %shard_map.107.refs_1_ = bf16[4,512,512]{2,1,0:T(8,128)(2,1)S(1)} custom-call(f32[8,512]{1,0:T(8,128)S(1)} %collective-permute-done.7.table), custom_call_target="tpu_custom_call" | custom-call | tf_op jit(solution)/shard_map/pallas_call | solution.py:21
  29.1 0.5 %shard_map.109 = bf16[128,512]{1,0:T(8,128)(2,1)S(1)} custom-call(bf16[4,512,512]{2,1,0:T(8,128)(2,1)S(1)} %shard_map.106.refs_0_, bf16[4,512,512]{2,1,0:T(8,128)(2,1)S(1)} %shard_map.107.refs_1_, bf16[128,512]{1,0:T(8,128)(2,1)S(1)} %shard_map.105.refs_2_, bf16[128,512]{1,0:T(8,128)(2,1)S(1)} %collective-permute-done.11.refs_3_, ...), custom_call_target="tpu_custom_call" | custom-call | flops 268435456 | bytes 4849664 | tf_op jit(solution)/shard_map/pallas_call | solution.py:21
  29.6 0.0 copy-start.6
  29.6 0.1 collective-permute-start.14
  29.7 0.5 %shard_map.108.a = bf16[128,512]{1,0:T(8,128)(2,1)S(1)} custom-call(bf16[4,512,512]{2,1,0:T(8,128)(2,1)S(1)} %shard_map.106.refs_0_, bf16[4,512,512]{2,1,0:T(8,128)(2,1)S(1)} %shard_map.107.refs_1_, bf16[128,512]{1,0:T(8,128)(2,1)S(1)} %shard_map.105.refs_2_, bf16[128,512]{1,0:T(8,128)(2,1)S(1)} %collective-permute-done.11.refs_3_, ...), custom_call_target="tpu_custom_call" | custom-call | flops 268435456 | bytes 4849664 | tf_op jit(solution)/shard_map/pallas_call | solution.py:21
  30.1 0.9 %collective-permute-done.14.b = bf16[128,512]{1,0:T(8,128)(2,1)S(1)} collective-permute-done((bf16[128,512]{1,0:T(8,128)(2,1)S(1)}, bf16[128,512]{1,0:T(8,128)(2,1)S(1)}, u32[]{:S(2)}, u32[]{:S(2)}) %collective-permute-start.14) | collective-permute-done | bytes 131104 | tf_op jit(solution)/shard_map/ppermute | solution.py:285
  31.0 1.2 %collective-permute-start.15 = (bf16[128,512]{1,0:T(8,128)(2,1)S(1)}, bf16[128,512]{1,0:T(8,128)(2,1)S(1)}, u32[]{:S(2)}, u32[]{:S(2)}) collective-permute-start(bf16[128,512]{1,0:T(8,128)(2,1)S(1)} %shard_map.110.a), channel_id=1, source_target_pairs={{0,2},{1,7},{2,0},{3,5},{4,6},{5,3},{6,4},{7,1},{8,10},{9,15},{10,... | collective-permute-start | bytes 393224 | tf_op jit(solution)/shard_map/ppermute | solution.py:418
  32.3 0.7 %collective-permute-start.16 = (bf16[128,512]{1,0:T(8,128)(2,1)S(1)}, bf16[128,512]{1,0:T(8,128)(2,1)S(1)}, u32[]{:S(2)}, u32[]{:S(2)}) collective-permute-start(bf16[128,512]{1,0:T(8,128)(2,1)S(1)} %shard_map.110.a), channel_id=1, source_target_pairs={{1,5},{3,7},{5,1},{7,3},{9,13},{11,15},{13,9},{15,11},{17,21},{19,... | collective-permute-start | bytes 393224 | tf_op jit(solution)/shard_map/ppermute | solution.py:419
  33.0 4.5 %collective-permute-done.15.refs_2_ = bf16[128,512]{1,0:T(8,128)(2,1)S(1)} collective-permute-done((bf16[128,512]{1,0:T(8,128)(2,1)S(1)}, bf16[128,512]{1,0:T(8,128)(2,1)S(1)}, u32[]{:S(2)}, u32[]{:S(2)}) %collective-permute-start.15) | collective-permute-done | bytes 131104 | tf_op jit(solution)/shard_map/ppermute | solution.py:418
  37.5 0.4 collective-permute-start.17
  37.9 0.2 collective-permute-start.18
  38.1 0.1 copy.11.bias
  38.2 0.7 %collective-permute-done.17.refs_1_ = bf16[128,512]{1,0:T(8,128)(2,1)S(1)} collective-permute-done((bf16[128,512]{1,0:T(8,128)(2,1)S(1)}, bf16[128,512]{1,0:T(8,128)(2,1)S(1)}, u32[]{:S(2)}, u32[]{:S(2)}) %collective-permute-start.17) | collective-permute-done | bytes 131104 | tf_op jit(solution)/shard_map/ppermute | solution.py:285
  38.9 0.3 collective-permute-done.18.refs_3_
  39.2 0.9 %shard_map.112 = bf16[128,512]{1,0:T(8,128)(2,1)} custom-call(bf16[64,128]{1,0:T(8,128)(2,1)S(1)} %get-tuple-element.53.wa, bf16[64,128]{1,0:T(8,128)(2,1)S(1)} %collective-permute-done.8.wb, bf16[64,128]{1,0:T(8,128)(2,1)S(1)} %collective-permute-done.9.wc, bf16[64,128]{1,0:T(8,128)(2,1)S(1)} %collective-permute-done.10.wd, f32[128,1]{1,0:T(8,128)S(1)} %copy.11.bias, ...), custom_call_target="tpu_custom_call" | custom-call | flops 67108864 | bytes 721408 | tf_op jit(solution)/shard_map/pallas_call | solution.py:21
  (27 shorter events, 0.2 us)
Async XLA Ops:
  0.0 10.2 %collective-permute-start.1 = (bf16[3,3,64,256]{3,2,1,0:T(8,128)(2,1)}, bf16[3,3,64,256]{3,2,1,0:T(8,128)(2,1)S(1)}, u32[]{:S(2)}, u32[]{:S(2)}) collective-permute-start(bf16[3,3,64,256]{3,2,1,0:T(8,128)(2,1)} %bitcast.10), channel_id=1, source_target_pairs={{0,2},{1,3},{2,0},{3,1},{4,6},{5,7},{6,4},{7,5},{8,10},{9,11},{10,... | collective-permute-start | bytes 884744 | tf_op jit(solution)/shard_map/ppermute | solution.py:285
  4.1 1.7 %copy-start.7 = (f32[64]{0:T(128)S(1)}, f32[64]{0:T(128)}, u32[]{:S(2)}) copy-start(f32[64]{0:T(128)} %param.14) | copy-start | bytes 772
  4.1 1.7 %copy-start.8 = (f32[64]{0:T(128)S(1)}, f32[64]{0:T(128)}, u32[]{:S(2)}) copy-start(f32[64]{0:T(128)} %param.12) | copy-start | bytes 772
  4.1 2.2 %copy-start = (bf16[64,3,3,256]{3,0,2,1:T(8,128)(2,1)S(1)}, bf16[64,3,3,256]{3,0,2,1:T(8,128)(2,1)}, u32[]{:S(2)}) copy-start(bf16[64,3,3,256]{3,0,2,1:T(8,128)(2,1)} %param.11) | copy-start | bytes 884740
  4.1 4.3 %copy-start.1 = (bf16[64,3,3,256]{3,0,2,1:T(8,128)(2,1)S(1)}, bf16[64,3,3,256]{3,0,2,1:T(8,128)(2,1)}, u32[]{:S(2)}) copy-start(bf16[64,3,3,256]{3,0,2,1:T(8,128)(2,1)} %param.13) | copy-start | bytes 884740
  4.2 4.8 %copy-start.5 = (s32[4096]{0:T(1024)S(1)}, s32[4096]{0:T(1024)}, u32[]{:S(2)}) copy-start(s32[4096]{0:T(1024)} %param.15) | copy-start | bytes 49156
  4.2 4.8 %copy-start.2 = (s32[4,512]{1,0:T(4,128)S(1)}, s32[4,512]{1,0:T(4,128)}, u32[]{:S(2)}) copy-start(s32[4,512]{1,0:T(4,128)} %slot.1) | copy-start | bytes 24580
  4.2 4.8 %copy-start.3 = (f32[2,512]{1,0:T(2,128)S(1)}, f32[2,512]{1,0:T(2,128)}, u32[]{:S(2)}) copy-start(f32[2,512]{1,0:T(2,128)} %frac.1) | copy-start | bytes 12292
  4.2 9.1 %collective-permute-start = (bf16[256,512]{1,0:T(8,128)(2,1)S(1)}, bf16[256,512]{1,0:T(8,128)(2,1)S(1)}, u32[]{:S(2)}, u32[]{:S(2)}) collective-permute-start(bf16[256,512]{1,0:T(8,128)(2,1)S(1)} %shard_map.100), channel_id=1, source_target_pairs={{0,4},{1,29},{2,6},{3,31},{4,8},{5,1},{6,10},{7,3},{8,12},{9,5},{1... | collective-permute-start | bytes 786440 | tf_op jit(solution)/shard_map/ppermute | solution.py:292
  5.9 4.4 %collective-permute-start.2 = (f32[1,128]{1,0:T(1,128)S(1)}, f32[1,128]{1,0:T(1,128)S(1)}, u32[]{:S(2)}, u32[]{:S(2)}) collective-permute-start(f32[1,128]{1,0:T(1,128)S(1)} %maximum_bitcast_fusion), channel_id=1, source_target_pairs={{0,2},{1,3},{2,0},{3,1},{4,6},{5,7},{6,4},{7,5},{8,10},{9,11},{10,... | collective-permute-start | bytes 1544 | tf_op jit(solution)/shard_map/ppermute | solution.py:285
  6.4 7.0 %collective-permute-start.3 = (bf16[3,3,64,256]{3,2,1,0:T(8,128)(2,1)S(1)}, bf16[3,3,64,256]{3,2,1,0:T(8,128)(2,1)S(1)}, u32[]{:S(2)}, u32[]{:S(2)}) collective-permute-start(bf16[3,3,64,256]{3,2,1,0:T(8,128)(2,1)S(1)} %bitcast.11), channel_id=1, source_target_pairs={{0,1},{1,0},{2,3},{3,2},{4,5},{5,4},{6,7},{7,6},{8,9},{9,8},{10,11... | collective-permute-start | bytes 884744 | tf_op jit(solution)/shard_map/ppermute | solution.py:285
  8.4 5.0 %collective-permute-start.4 = (bf16[3,3,64,256]{3,2,1,0:T(8,128)(2,1)S(1)}, bf16[3,3,64,256]{3,2,1,0:T(8,128)(2,1)S(1)}, u32[]{:S(2)}, u32[]{:S(2)}) collective-permute-start(bf16[3,3,64,256]{3,2,1,0:T(8,128)(2,1)S(1)} %bitcast.13), channel_id=1, source_target_pairs={{0,1},{1,0},{2,3},{3,2},{4,5},{5,4},{6,7},{7,6},{8,9},{9,8},{10,11... | collective-permute-start | bytes 884744 | tf_op jit(solution)/shard_map/ppermute | solution.py:285
  10.3 3.6 %collective-permute-start.6 = (f32[2,128]{1,0:T(2,128)S(1)}, f32[2,128]{1,0:T(2,128)S(1)}, u32[]{:S(2)}, u32[]{:S(2)}) collective-permute-start(f32[2,128]{1,0:T(2,128)S(1)} %pad_maximum_fusion.bias), channel_id=1, source_target_pairs={{0,1},{1,0},{2,3},{3,2},{4,5},{5,4},{6,7},{7,6},{8,9},{9,8},{10,11... | collective-permute-start | bytes 3080 | tf_op jit(solution)/shard_map/ppermute | solution.py:285
  10.9 3.0 %collective-permute-start.5 = (bf16[3,3,64,256]{3,2,1,0:T(8,128)(2,1)S(1)}, bf16[3,3,64,256]{3,2,1,0:T(8,128)(2,1)S(1)}, u32[]{:S(2)}, u32[]{:S(2)}) collective-permute-start(bf16[3,3,64,256]{3,2,1,0:T(8,128)(2,1)S(1)} %collective-permute-done.1.w1c), channel_id=1, source_target_pairs={{0,1},{1,0},{2,3},{3,2},{4,5},{5,4},{6,7},{7,6},{8,9},{9,8},{10,11... | collective-permute-start | bytes 884744 | tf_op jit(solution)/shard_map/ppermute | solution.py:285
  13.9 8.6 %copy-start.4 = (bf16[64,512]{1,0:T(8,128)(2,1)S(1)}, bf16[64,512]{1,0:T(8,128)(2,1)}, u32[]{:S(2)}) copy-start(bf16[64,512]{1,0:T(8,128)(2,1)} %param.18) | copy-start | bytes 196612
  15.8 6.7 %collective-permute-start.7 = (f32[8,512]{1,0:T(8,128)S(1)}, f32[8,512]{1,0:T(8,128)S(1)}, u32[]{:S(2)}, u32[]{:S(2)}) collective-permute-start(f32[8,512]{1,0:T(8,128)S(1)} %shard_map.103.table), channel_id=1, source_target_pairs={{0,4},{1,5},{2,6},{3,7},{4,0},{5,1},{6,2},{7,3},{8,12},{9,13},{10,... | collective-permute-start | bytes 49160 | tf_op jit(solution)/shard_map/ppermute | solution.py:292
  16.9 12.2 %collective-permute-start.11 = (bf16[128,512]{1,0:T(8,128)(2,1)S(1)}, bf16[128,512]{1,0:T(8,128)(2,1)S(1)}, u32[]{:S(2)}, u32[]{:S(2)}) collective-permute-start(bf16[128,512]{1,0:T(8,128)(2,1)S(1)} %shard_map.105.refs_2_), channel_id=1, source_target_pairs={{0,8},{1,9},{2,10},{3,11},{4,12},{5,13},{6,14},{7,15},{8,16},{9,17... | collective-permute-start | bytes 393224 | tf_op jit(solution)/shard_map/ppermute | solution.py:292
  18.5 10.6 %collective-permute-start.12 = (bf16[128,512]{1,0:T(8,128)(2,1)S(1)}, bf16[128,512]{1,0:T(8,128)(2,1)S(1)}, u32[]{:S(2)}, u32[]{:S(2)}) collective-permute-start(bf16[128,512]{1,0:T(8,128)(2,1)S(1)} %shard_map.105.refs_2_), channel_id=1, source_target_pairs={{0,16},{1,17},{2,18},{3,19},{4,20},{5,21},{6,22},{7,23},{8,24},{9,... | collective-permute-start | bytes 393224 | tf_op jit(solution)/shard_map/ppermute | solution.py:292
  21.6 7.5 %collective-permute-start.13 = (bf16[128,512]{1,0:T(8,128)(2,1)S(1)}, bf16[128,512]{1,0:T(8,128)(2,1)S(1)}, u32[]{:S(2)}, u32[]{:S(2)}) collective-permute-start(bf16[128,512]{1,0:T(8,128)(2,1)S(1)} %shard_map.105.refs_2_), channel_id=1, source_target_pairs={{0,24},{1,25},{2,26},{3,27},{4,28},{5,29},{6,30},{7,31},{8,0},{9,1... | collective-permute-start | bytes 393224 | tf_op jit(solution)/shard_map/ppermute | solution.py:292
  22.4 1.2 %collective-permute-start.8 = (bf16[64,128]{1,0:T(8,128)(2,1)S(1)}, bf16[64,128]{1,0:T(8,128)(2,1)S(1)}, u32[]{:S(2)}, u32[]{:S(2)}) collective-permute-start(bf16[64,128]{1,0:T(8,128)(2,1)S(1)} %get-tuple-element.63), channel_id=1, source_target_pairs={{0,1},{1,0},{2,3},{3,2},{4,5},{5,4},{6,7},{7,6},{8,9},{9,8},{10,11... | collective-permute-start | bytes 49160 | tf_op jit(solution)/shard_map/ppermute | solution.py:285
  22.5 6.5 %collective-permute-start.10 = (bf16[64,128]{1,0:T(8,128)(2,1)S(1)}, bf16[64,128]{1,0:T(8,128)(2,1)S(1)}, u32[]{:S(2)}, u32[]{:S(2)}) collective-permute-start(bf16[64,128]{1,0:T(8,128)(2,1)S(1)} %get-tuple-element.61), channel_id=1, source_target_pairs={{0,3},{1,2},{2,1},{3,0},{4,7},{5,6},{6,5},{7,4},{8,11},{9,10},{10,... | collective-permute-start | bytes 49160 | tf_op jit(solution)/shard_map/ppermute | solution.py:285
  23.7 5.4 %collective-permute-start.9 = (bf16[64,128]{1,0:T(8,128)(2,1)S(1)}, bf16[64,128]{1,0:T(8,128)(2,1)S(1)}, u32[]{:S(2)}, u32[]{:S(2)}) collective-permute-start(bf16[64,128]{1,0:T(8,128)(2,1)S(1)} %get-tuple-element.52), channel_id=1, source_target_pairs={{0,2},{1,3},{2,0},{3,1},{4,6},{5,7},{6,4},{7,5},{8,10},{9,11},{10,... | collective-permute-start | bytes 49160 | tf_op jit(solution)/shard_map/ppermute | solution.py:285
  29.6 8.5 %copy-start.6 = (f32[128]{0:T(128)S(1)}, f32[128]{0:T(128)}, u32[]{:S(2)}) copy-start(f32[128]{0:T(128)} %param.19) | copy-start | bytes 1540
  29.6 1.4 %collective-permute-start.14 = (bf16[128,512]{1,0:T(8,128)(2,1)S(1)}, bf16[128,512]{1,0:T(8,128)(2,1)S(1)}, u32[]{:S(2)}, u32[]{:S(2)}) collective-permute-start(bf16[128,512]{1,0:T(8,128)(2,1)S(1)} %shard_map.109), channel_id=1, source_target_pairs={{0,1},{1,0},{2,3},{3,2},{4,5},{5,4},{6,7},{7,6},{8,9},{9,8},{10,11... | collective-permute-start | bytes 393224 | tf_op jit(solution)/shard_map/ppermute | solution.py:285
  31.0 6.4 %collective-permute-start.15 = (bf16[128,512]{1,0:T(8,128)(2,1)S(1)}, bf16[128,512]{1,0:T(8,128)(2,1)S(1)}, u32[]{:S(2)}, u32[]{:S(2)}) collective-permute-start(bf16[128,512]{1,0:T(8,128)(2,1)S(1)} %shard_map.110.a), channel_id=1, source_target_pairs={{0,2},{1,7},{2,0},{3,5},{4,6},{5,3},{6,4},{7,1},{8,10},{9,15},{10,... | collective-permute-start | bytes 393224 | tf_op jit(solution)/shard_map/ppermute | solution.py:418
  32.3 5.2 %collective-permute-start.16 = (bf16[128,512]{1,0:T(8,128)(2,1)S(1)}, bf16[128,512]{1,0:T(8,128)(2,1)S(1)}, u32[]{:S(2)}, u32[]{:S(2)}) collective-permute-start(bf16[128,512]{1,0:T(8,128)(2,1)S(1)} %shard_map.110.a), channel_id=1, source_target_pairs={{1,5},{3,7},{5,1},{7,3},{9,13},{11,15},{13,9},{15,11},{17,21},{19,... | collective-permute-start | bytes 393224 | tf_op jit(solution)/shard_map/ppermute | solution.py:419
  37.5 1.4 %collective-permute-start.17 = (bf16[128,512]{1,0:T(8,128)(2,1)S(1)}, bf16[128,512]{1,0:T(8,128)(2,1)S(1)}, u32[]{:S(2)}, u32[]{:S(2)}) collective-permute-start(bf16[128,512]{1,0:T(8,128)(2,1)S(1)} %shard_map.111.refs_0_), channel_id=1, source_target_pairs={{0,1},{1,0},{2,3},{3,2},{4,5},{5,4},{6,7},{7,6},{8,9},{9,8},{10,11... | collective-permute-start | bytes 393224 | tf_op jit(solution)/shard_map/ppermute | solution.py:285
  37.9 1.3 %collective-permute-start.18 = (bf16[128,512]{1,0:T(8,128)(2,1)S(1)}, bf16[128,512]{1,0:T(8,128)(2,1)S(1)}, u32[]{:S(2)}, u32[]{:S(2)}) collective-permute-start(bf16[128,512]{1,0:T(8,128)(2,1)S(1)} %collective-permute-done.15.refs_2_), channel_id=1, source_target_pairs={{0,1},{1,0},{2,3},{3,2},{4,5},{5,4},{6,7},{7,6},{8,9},{9,8},{10,11... | collective-permute-start | bytes 393224 | tf_op jit(solution)/shard_map/ppermute | solution.py:285
